TPU v7x, 32 devices: a whole 2x2x4 slice. The times are simulated.
32 devices in a mesh: dp: 8 (over z, x), tensor: 4 (over y, core).
Axes of the slice: x: 2, y: 2, z: 4, core: 2. Of those that a mesh axis runs over, the one named last changes fastest.
Arguments:
- latents: bfloat16 [1024, 16, 1024], P('tensor', 'dp'), may hold values from -6 to 6
- conditioning: bfloat16 [16, 1024], P('dp'), may hold values from -6 to 6
- mod_weight: bfloat16 [1024, 6, 1024], P('dp'), may hold values from -0.1875 to 0.1875
- mod_bias: bfloat16 [6, 1024], replicated, may hold values from -3 to 3
- qkv_weight: bfloat16 [1024, 3, 1024], P('dp', None, 'tensor'), may hold values from -0.1875 to 0.1875
- qkv_bias: bfloat16 [3, 1024], P(None, 'tensor'), may hold values from -2 to 2
- proj_weight: bfloat16 [1024, 1024], P('dp', 'tensor'), may hold values from -0.75 to 0.75
- proj_bias: bfloat16 [1024], replicated, may hold values from -2 to 2
- expand_weight: bfloat16 [1024, 4096], P('dp', 'tensor'), may hold values from -0.1875 to 0.1875
- expand_bias: bfloat16 [4096], P('tensor'), may hold values from -2 to 2
- reduce_weight: bfloat16 [1024, 4096], P('dp', 'tensor'), may hold values from -0.125 to 0.125
- reduce_bias: bfloat16 [1024], replicated, may hold values from -2 to 2
- out_grad: bfloat16 [1024, 16, 1024], P('tensor', 'dp'), may hold values from -6 to 6
Outputs:
- layer_out: bfloat16 [1024, 16, 1024], P('tensor', 'dp')
- latent_grad: float32 [1024, 16, 1024], P('tensor', 'dp')
- cond_grad: float32 [16, 1024], P('dp')
- mod_weight_grad: float32 [1024, 6, 1024], P('dp', None, 'tensor')
- mod_bias_grad: float32 [6, 1024], replicated
- qkv_weight_grad: float32 [1024, 3, 1024], P('dp', None, 'tensor')
- qkv_bias_grad: float32 [3, 1024], P(None, 'tensor')
- proj_weight_grad: float32 [1024, 1024], P('dp', 'tensor')
- proj_bias_grad: float32 [1024], replicated
- expand_weight_grad: float32 [1024, 4096], P('dp', 'tensor')
- expand_bias_grad: float32 [4096], P('tensor')
- reduce_weight_grad: float32 [1024, 4096], P('dp', 'tensor')
- reduce_bias_grad: float32 [1024], replicated
All inputs are finite; a program needn't handle non-finite values.
Results may differ from a plain program's by a relative error of at most 0.02.
The roundings to bfloat16 on the way count: a program that leaves them out, or rounds other values in their place, can miss the bound.
Values may be sent and summed in bfloat16 or wider, within the bound.
No kernel may reach another device: no remote copies, remote signals or barrier semaphores. Data moves between devices by JAX's collectives and lax.ppermute only.
A program may use at most 256 MiB of HBM per device.

v0:
```python
import jax
import jax.numpy as jnp
from jax import lax
from jax.sharding import PartitionSpec as P

HEAD_DIM = 64


def norm_rows(values):
    mean_val = jnp.mean(values, -1, keepdims=True)
    centered = values - mean_val
    variance = jnp.mean(centered * centered, -1, keepdims=True)
    return centered * lax.rsqrt(variance + 1e-06)


def gelu_tanh(values):
    return jax.nn.gelu(values, approximate=True)


def per_device(
    latents,
    conditioning,
    mod_weight,
    mod_bias,
    qkv_weight,
    qkv_bias,
    proj_weight,
    proj_bias,
    expand_weight,
    expand_bias,
    reduce_weight,
    reduce_bias,
    out_grad,
):
    f32 = jnp.float32
    bf16 = jnp.bfloat16
    n_tensor = lax.axis_size("tensor")
    n_dp = lax.axis_size("dp")
    row_count, images, model_width = latents.shape
    length = row_count * n_tensor
    local_width = qkv_weight.shape[2]
    local_heads = local_width // HEAD_DIM
    mod_rows_dev = mod_weight.shape[0]
    query_block = min(512, length)
    scale_qk = HEAD_DIM ** (-0.5)
    dp_index = lax.axis_index("dp")
    tensor_index = lax.axis_index("tensor")
    cond_float = conditioning.astype(f32)
    cond_low = jax.nn.silu(cond_float).astype(bf16)
    cond_all, qkv_full, proj_full, expand_full, reduce_full = (
        lax.all_gather(cond_low, "dp", axis=0, tiled=True),
        lax.all_gather(qkv_weight, "dp", axis=0, tiled=True),
        lax.all_gather(proj_weight, "dp", axis=0, tiled=True),
        lax.all_gather(expand_weight, "dp", axis=0, tiled=True),
        lax.all_gather(reduce_weight, "dp", axis=0, tiled=True),
    )
    cond_cols = lax.dynamic_slice_in_dim(cond_all, dp_index * mod_rows_dev, mod_rows_dev, 1)
    mod_full = lax.all_gather(mod_weight, "dp", axis=0, tiled=True)
    mod_sum = jnp.einsum("bd,dke->bke", cond_low, mod_full, preferred_element_type=f32)
    modulation = mod_sum + mod_bias.astype(f32)[None]
    x_float = latents.astype(f32)
    normed_a = norm_rows(x_float)
    shifted_a = (normed_a * (1.0 + modulation[:, 1]) + modulation[:, 0]).astype(bf16)
    gathered_a = lax.all_gather(shifted_a, "tensor", axis=0, tiled=True)
    qkv_low = (
        jnp.einsum("sbd,dke->sbke", gathered_a, qkv_full, preferred_element_type=f32)
        + qkv_bias.astype(f32)
    ).astype(bf16)
    query = qkv_low[:, :, 0].reshape(length, images, local_heads, HEAD_DIM)
    key_all = qkv_low[:, :, 1].reshape(length, images, local_heads, HEAD_DIM)
    value_all = qkv_low[:, :, 2].reshape(length, images, local_heads, HEAD_DIM)
    out_parts = []
    lse_parts = []
    for offset in range(0, length, query_block):
        query_part = query[offset : offset + query_block]
        scores = (
            jnp.einsum("qbhe,kbhe->bhqk", query_part, key_all, preferred_element_type=f32)
            * scale_qk
        )
        row_max = jnp.max(scores, -1, keepdims=True)
        exp_scores = jnp.exp(scores - row_max)
        row_total = jnp.sum(exp_scores, -1, keepdims=True)
        prob_low = (exp_scores / row_total).astype(bf16)
        out_parts.append(
            jnp.einsum("bhqk,kbhe->qbhe", prob_low, value_all, preferred_element_type=f32)
        )
        lse_parts.append(row_max + jnp.log(row_total))
    attended = jnp.concatenate(out_parts, 0).reshape(length, images, local_width).astype(bf16)
    part_rows = attended
    branch_a = lax.psum_scatter(
        jnp.einsum("sbe,oe->sbo", part_rows, proj_full, preferred_element_type=f32).astype(
            jnp.bfloat16
        ),
        "tensor",
        scatter_dimension=0,
        tiled=True,
    ).astype(jnp.float32) + proj_bias.astype(f32)
    mid_resid = x_float + modulation[:, 2] * branch_a
    normed_m = norm_rows(mid_resid)
    shifted_m = (normed_m * (1.0 + modulation[:, 4]) + modulation[:, 3]).astype(bf16)
    gathered_m = lax.all_gather(shifted_m, "tensor", axis=0, tiled=True)
    pre_act = jnp.einsum(
        "sbd,df->sbf", gathered_m, expand_full, preferred_element_type=f32
    ) + expand_bias.astype(f32)
    hidden = gelu_tanh(pre_act).astype(bf16)
    part_rows = hidden
    branch_m = lax.psum_scatter(
        jnp.einsum("sbf,of->sbo", part_rows, reduce_full, preferred_element_type=f32).astype(
            jnp.bfloat16
        ),
        "tensor",
        scatter_dimension=0,
        tiled=True,
    ).astype(jnp.float32) + reduce_bias.astype(f32)
    result = (mid_resid + modulation[:, 5] * branch_m).astype(bf16)
    grad_y = out_grad.astype(f32)
    g_gate_m = jnp.sum(grad_y * branch_m, 0)
    grad_m = (grad_y * modulation[:, 5]).astype(bf16)
    grad_m_all = lax.all_gather(grad_m, "tensor", axis=0, tiled=True)
    g_reduce_w = jnp.einsum("sbo,sbf->of", grad_m_all, hidden, preferred_element_type=f32)
    g_reduce_b = jnp.sum(grad_m_all.astype(f32), (0, 1))
    grad_hidden = jnp.einsum("sbo,of->sbf", grad_m_all, reduce_full, preferred_element_type=f32)
    gelu_out, gelu_pull = jax.vjp(gelu_tanh, pre_act)
    grad_pre = gelu_pull(grad_hidden)[0].astype(bf16)
    g_expand_b = jnp.sum(grad_pre.astype(f32), (0, 1))
    g_expand_w = jnp.einsum("sbd,sbf->df", gathered_m, grad_pre, preferred_element_type=f32)
    part_rows = grad_pre
    grad_sm = lax.psum_scatter(
        jnp.einsum("sbf,df->sbd", part_rows, expand_full, preferred_element_type=f32).astype(
            jnp.bfloat16
        ),
        "tensor",
        scatter_dimension=0,
        tiled=True,
    ).astype(jnp.float32)
    g_shift_m = jnp.sum(grad_sm, 0)
    g_scale_m = jnp.sum(grad_sm * normed_m, 0)
    norm_out_m, norm_pull_m = jax.vjp(norm_rows, mid_resid)
    grad_mid = grad_y + norm_pull_m(grad_sm * (1.0 + modulation[:, 4]))[0]
    g_gate_a = jnp.sum(grad_mid * branch_a, 0)
    grad_a = (grad_mid * modulation[:, 2]).astype(bf16)
    grad_a_all = lax.all_gather(grad_a, "tensor", axis=0, tiled=True)
    g_proj_w = jnp.einsum("sbo,sbe->oe", grad_a_all, attended, preferred_element_type=f32)
    g_proj_b = jnp.sum(grad_a_all.astype(f32), (0, 1))
    grad_att = jnp.einsum("sbo,oe->sbe", grad_a_all, proj_full, preferred_element_type=f32).astype(
        bf16
    )
    grad_att = grad_att.reshape(length, images, local_heads, HEAD_DIM)
    grad_key = jnp.zeros((length, images, local_heads, HEAD_DIM), f32)
    grad_value = jnp.zeros((length, images, local_heads, HEAD_DIM), f32)
    query_grads = []
    for block_idx, offset in enumerate(range(0, length, query_block)):
        query_part = query[offset : offset + query_block]
        grad_part = grad_att[offset : offset + query_block]
        scores = (
            jnp.einsum("qbhe,kbhe->bhqk", query_part, key_all, preferred_element_type=f32)
            * scale_qk
        )
        prob_full = jnp.exp(scores - lse_parts[block_idx])
        prob_low = prob_full.astype(bf16)
        grad_value = grad_value + jnp.einsum(
            "bhqk,qbhe->kbhe", prob_low, grad_part, preferred_element_type=f32
        )
        grad_prob = jnp.einsum("qbhe,kbhe->bhqk", grad_part, value_all, preferred_element_type=f32)
        row_dot = jnp.sum(prob_full * grad_prob, -1, keepdims=True)
        grad_score = (prob_full * (grad_prob - row_dot)).astype(bf16)
        query_grads.append(
            jnp.einsum("bhqk,kbhe->qbhe", grad_score, key_all, preferred_element_type=f32)
            * scale_qk
        )
        grad_key = (
            grad_key
            + jnp.einsum("bhqk,qbhe->kbhe", grad_score, query_part, preferred_element_type=f32)
            * scale_qk
        )
    grad_query = jnp.concatenate(query_grads, 0).reshape(length, images, local_width)
    grad_qkv = jnp.stack(
        [
            grad_query,
            grad_key.reshape(length, images, local_width),
            grad_value.reshape(length, images, local_width),
        ],
        2,
    ).astype(bf16)
    g_qkv_b = jnp.sum(grad_qkv.astype(f32), (0, 1))
    g_qkv_w = jnp.einsum("sbd,sbke->dke", gathered_a, grad_qkv, preferred_element_type=f32)
    part_rows = grad_qkv
    grad_sa = lax.psum_scatter(
        jnp.einsum("sbke,dke->sbd", part_rows, qkv_full, preferred_element_type=f32).astype(
            jnp.bfloat16
        ),
        "tensor",
        scatter_dimension=0,
        tiled=True,
    ).astype(jnp.float32)
    g_shift_a = jnp.sum(grad_sa, 0)
    g_scale_a = jnp.sum(grad_sa * normed_a, 0)
    norm_out_a, norm_pull_a = jax.vjp(norm_rows, x_float)
    grad_latent = grad_mid + norm_pull_a(grad_sa * (1.0 + modulation[:, 1]))[0]
    mod_part = jnp.stack([g_shift_a, g_scale_a, g_gate_a, g_shift_m, g_scale_m, g_gate_m], 1)
    mod_pieces = lax.all_gather(
        mod_part.astype(jnp.bfloat16), ("dp", "tensor"), axis=0, tiled=True
    ).astype(mod_part.dtype)
    grad_mod_all = jnp.sum(mod_pieces.reshape(n_dp, n_tensor, images, 6, model_width), 1)
    grad_mod_all = grad_mod_all.reshape(n_dp * images, 6, model_width)
    g_mod_b = jnp.sum(grad_mod_all, 0)
    grad_mod_low = grad_mod_all.astype(bf16)
    own_columns = lax.dynamic_slice_in_dim(grad_mod_low, tensor_index * local_width, local_width, 2)
    g_mod_w = jnp.einsum("gd,gke->dke", cond_cols, own_columns, preferred_element_type=f32)
    own_images = lax.dynamic_slice_in_dim(grad_mod_low, dp_index * images, images, 0)
    grad_act = jnp.einsum("bke,dke->bd", own_images, mod_full, preferred_element_type=f32)
    silu_out, silu_pull = jax.vjp(jax.nn.silu, cond_float)
    grad_cond = silu_pull(grad_act)[0]
    bias_total = lax.psum((g_qkv_b, g_proj_b, g_expand_b, g_reduce_b), "dp")
    weight_total = (
        lax.psum_scatter(
            g_qkv_w.astype(jnp.bfloat16), "dp", scatter_dimension=0, tiled=True
        ).astype(jnp.float32),
        lax.psum_scatter(
            g_proj_w.astype(jnp.bfloat16), "dp", scatter_dimension=0, tiled=True
        ).astype(jnp.float32),
        lax.psum_scatter(
            g_expand_w.astype(jnp.bfloat16), "dp", scatter_dimension=0, tiled=True
        ).astype(jnp.float32),
        lax.psum_scatter(
            g_reduce_w.astype(jnp.bfloat16), "dp", scatter_dimension=0, tiled=True
        ).astype(jnp.float32),
    )
    return (
        result,
        grad_latent,
        grad_cond,
        g_mod_w,
        g_mod_b,
        weight_total[0],
        bias_total[0],
        weight_total[1],
        bias_total[1],
        weight_total[2],
        bias_total[2],
        weight_total[3],
        bias_total[3],
    )


def solution(mesh):
    in_specs = (
        P("tensor", "dp", None),
        P("dp", None),
        P("dp", None, None),
        P(),
        P("dp", None, "tensor"),
        P(None, "tensor"),
        P("dp", "tensor"),
        P(),
        P("dp", "tensor"),
        P("tensor"),
        P("dp", "tensor"),
        P(),
        P("tensor", "dp", None),
    )
    out_specs = (
        P("tensor", "dp", None),
        P("tensor", "dp", None),
        P("dp", None),
        P("dp", None, "tensor"),
        P(),
        P("dp", None, "tensor"),
        P(None, "tensor"),
        P("dp", "tensor"),
        P(),
        P("dp", "tensor"),
        P("tensor"),
        P("dp", "tensor"),
        P(),
    )
    return jax.shard_map(
        per_device, mesh=mesh, in_specs=in_specs, out_specs=out_specs, check_vma=False
    )
```

profile of v0, /device:TPU:0, one launch (start us, length us, event | category | flops | bytes accessed | tf_op | source)
XLA Modules:
  0.0 1088.7 jit_solution(9454566120516406985)
XLA Ops:
  12.6 176.8 %all-gather.10.cloned.1.call-done = bf16[1024,6,1024]{2,0,1:T(8,128)(2,1)} async-done(((bf16[128,6,1024]{2,0,1:T(8,128)(2,1)}), bf16[1024,6,1024]{2,0,1:T(8,128)(2,1)}) %all-gather.10.cloned.1.call-update) | async-done | bytes 12582928 | tf_op jit(solution)/shard_map/all_gather | solution.py:58
  197.3 32.5 %all_gather.36 = bf16[1024,256]{1,0:T(8,128)(2,1)S(1)} all-gather(bf16[128,256]{1,0:T(8,128)(2,1)S(1)} %copy-done.37), channel_id=1, replica_groups=mesh['dp'=8,'tensor'=4] {'dp'}, dimensions={0}, use_global_device_ids=true | all-gather | bytes 589824 | tf_op jit(solution)/shard_map/all_gather | solution.py:53
  238.4 35.8 %all-gather.12.cloned.1.call-done = bf16[1024,2,1024]{2,0,1:T(8,128)(2,1)} async-done(((bf16[256,2,1024]{2,0,1:T(8,128)(2,1)}), bf16[1024,2,1024]{2,0,1:T(8,128)(2,1)}) %all-gather.12.cloned.1.call-update) | async-done | bytes 4194320 | tf_op jit(solution)/shard_map/all_gather | solution.py:64
  319.4 44.0 %reduce-scatter.9.cloned.1.call-done = bf16[256,2,1024]{2,0,1:T(8,128)(2,1)} async-done(((bf16[1024,2,1024]{2,0,1:T(8,128)(2,1)}), bf16[256,2,1024]{2,0,1:T(8,128)(2,1)}) %reduce-scatter.9.cloned.1.call-update) | async-done | bytes 1048592 | tf_op jit(solution)/shard_map/reduce_scatter | solution.py:90
  371.1 43.8 %all-gather.18.cloned.1.call-done = bf16[1024,1024]{1,0:T(8,128)(2,1)} async-done(((bf16[128,1024]{1,0:T(8,128)(2,1)}), bf16[1024,1024]{1,0:T(8,128)(2,1)}) %all-gather.18.cloned.1.call-update) | async-done | bytes 2097168 | tf_op jit(solution)/shard_map/all_gather | solution.py:54
  414.9 35.1 %all-gather.16.cloned.1.call-done = bf16[1024,2,1024]{2,0,1:T(8,128)(2,1)} async-done(((bf16[256,2,1024]{2,0,1:T(8,128)(2,1)}), bf16[1024,2,1024]{2,0,1:T(8,128)(2,1)}) %all-gather.16.cloned.1.call-update) | async-done | bytes 4194320 | tf_op jit(solution)/shard_map/all_gather | solution.py:101
  449.9 10.7 fusion.45
  460.6 41.0 %all-gather.20.cloned.1.call-done = bf16[1024,1024]{1,0:T(8,128)(2,1)} async-done(((bf16[128,1024]{1,0:T(8,128)(2,1)}), bf16[1024,1024]{1,0:T(8,128)(2,1)}) %all-gather.20.cloned.1.call-update) | async-done | bytes 2097168 | tf_op jit(solution)/shard_map/all_gather | solution.py:55
  501.6 35.2 %all-gather.22.cloned.1.call-done = bf16[1024,2,1024]{2,0,1:T(8,128)(2,1)} async-done(((bf16[256,2,1024]{2,0,1:T(8,128)(2,1)}), bf16[1024,2,1024]{2,0,1:T(8,128)(2,1)}) %all-gather.22.cloned.1.call-update) | async-done | bytes 4194320 | tf_op jit(solution)/shard_map/all_gather | solution.py:119
  536.8 13.8 %convert_reduce_fusion.1 = (f32[1024]{0:T(1024)}, bf16[1024,2,1024]{2,0,1:T(8,128)(2,1)S(1)}) fusion(f32[1024,2,1024]{2,0,1:T(8,128)} %fusion.45, f32[1024]{0:T(1024)S(1)} %convert_element_type.161, bf16[1024,2,1024]{2,0,1:T(8,128)(2,1)} %all-gather.22.cloned.1.call-done, bf16[1024,1024]{1,0:T(8,128)(2,1)} %all-gather.20.cloned.1.call-done), kind=kOutput, calls=%fused_computation.29 | convolution fusion | flops 4343200768 | bytes 18882560 | tf_op jit(solution)/shard_map/sbo,of->sbf/dot_general | solution.py:122
  559.0 44.6 %reduce-scatter.13.cloned.1.call-done = bf16[256,2,1024]{2,0,1:T(8,128)(2,1)} async-done(((bf16[1024,2,1024]{2,0,1:T(8,128)(2,1)}), bf16[256,2,1024]{2,0,1:T(8,128)(2,1)}) %reduce-scatter.13.cloned.1.call-update) | async-done | bytes 1048592 | tf_op jit(solution)/shard_map/reduce_scatter | solution.py:128
  609.5 9.4 bitcast_convert_fusion.2
  619.6 10.9 %bitcast_convert_fusion.1 = bf16[1024,1024]{1,0:T(8,128)(2,1)} fusion(bf16[1024,2,1024]{2,0,1:T(8,128)(2,1)} %all-gather.22.cloned.1.call-done, f32[1024,2,1024]{2,0,1:T(8,128)} %fusion.45, f32[1024]{0:T(1024)S(1)} %convert_element_type.161), kind=kOutput, calls=%fused_computation.44 | convolution fusion | flops 4316987392 | bytes 14684160 | tf_op jit(solution)/shard_map/sbo,sbf->of/dot_general | solution.py:120
  630.6 13.3 %all-gather.24.cloned.1.call-done = bf16[1024,2,1024]{2,0,1:T(8,128)(2,1)} async-done(((bf16[256,2,1024]{2,0,1:T(8,128)(2,1)}), bf16[1024,2,1024]{2,0,1:T(8,128)(2,1)}) %all-gather.24.cloned.1.call-update) | async-done | bytes 4194320 | tf_op jit(solution)/shard_map/all_gather | solution.py:142
  657.6 14.1 %multiply_reduce_fusion = (f32[2,4,512]{2,1,0:T(4,128)}, f32[2,4,512,1024]{3,2,1,0:T(8,128)}) fusion(f32[2,4,512,1024]{3,2,1,0:T(8,128)} %copy-done, f32[2,4,512]{2,1,0:T(4,128)} %bitcast.181, bf16[512,2,4,64]{0,3,2,1:T(8,128)(2,1)} %bitcast.177, bf16[1024,2,4,64]{0,3,2,1:T(8,128)(2,1)} %bitcast.164), kind=kOutput, calls=%fused_computation.1 | convolution fusion | flops 553644032 | bytes 35160064 | tf_op jit(solution)/shard_map/qbhe,kbhe->bhqk/dot_general | solution.py:164
  671.8 10.3 multiply_reduce_fusion.1
  689.7 12.6 %multiply_convert_fusion.1 = bf16[2,4,512,1024]{3,2,1,0:T(8,128)(2,1)S(1)} fusion(f32[2,4,512,1024]{3,2,1,0:T(8,128)} %get-tuple-element.119, f32[2,4,512,1024]{3,2,1,0:T(8,128)} %get-tuple-element.117, f32[2,4,512]{2,1,0:T(4,128)} %get-tuple-element.118, f32[2,4,512]{2,1,0:T(4,128)} %bitcast.185), kind=kLoop, calls=%fused_computation.3 | loop fusion | flops 20971520 | bytes 41975808 | tf_op jit(solution)/shard_map/convert_element_type | solution.py:166
  750.8 11.8 %convolution_convert_fusion.1 = bf16[1024,2,1024]{2,0,1:T(8,128)(2,1)} fusion(bf16[1024,1024]{1,0:T(8,128)(2,1)} %all-gather.20.cloned.1.call-done, f32[1024,2,1024]{2,0,1:T(8,128)} %fusion.45, f32[1024]{0:T(1024)S(1)} %copy-done.49), kind=kOutput, calls=%fused_computation.61 | convolution fusion | flops 4318035968 | bytes 14684160 | tf_op jit(solution)/shard_map/sbf,of->sbo/dot_general | solution.py:108
  772.0 30.5 %all-gather = bf16[8,2,1024]{2,1,0:T(2,128)(2,1)S(1)} all-gather(bf16[1,2,1024]{2,1,0:T(2,128)(2,1)S(1)} %fusion.92), channel_id=1, replica_groups=mesh['dp'=8,'tensor'=4] {'dp'}, dimensions={0}, use_global_device_ids=true | all-gather | bytes 36864 | tf_op jit(solution)/shard_map/all_gather | solution.py:51
  814.6 37.9 %all-reduce = (f32[3,256]{1,0:T(4,128)}, f32[1024]{0:T(1024)}, f32[1024]{0:T(1024)}, f32[1024]{0:T(1024)}) all-reduce(f32[3,256]{1,0:T(4,128)S(1)} %convert_reduce_fusion.3, f32[1024]{0:T(1024)S(1)} %convert_reduce_fusion.2, f32[1024]{0:T(1024)S(1)} %copy-done.50, ...), channel_id=1, replica_groups=mesh['dp'=8,'tensor'=4] {'dp'}, use_global_device_ids=true, to_apply=%region_28.29 | all-reduce | flops 3840 | bytes 30720 | tf_op jit(solution)/shard_map/psum | solution.py:214
  854.0 65.2 %reduce-scatter.17.cloned.1.call-done = bf16[128,3,256]{2,0,1:T(8,128)(2,1)} async-done(((bf16[1024,3,256]{2,0,1:T(8,128)(2,1)}), bf16[128,3,256]{2,0,1:T(8,128)(2,1)}) %reduce-scatter.17.cloned.1.call-update) | async-done | bytes 196624 | tf_op jit(solution)/shard_map/reduce_scatter | solution.py:216
  920.8 44.2 %reduce-scatter.11.cloned.1.call-done = bf16[256,2,1024]{2,0,1:T(8,128)(2,1)} async-done(((bf16[1024,2,1024]{2,0,1:T(8,128)(2,1)}), bf16[256,2,1024]{2,0,1:T(8,128)(2,1)}) %reduce-scatter.11.cloned.1.call-update) | async-done | bytes 1048592 | tf_op jit(solution)/shard_map/reduce_scatter | solution.py:107
  965.1 47.1 %reduce-scatter.15.cloned.1.call-done = bf16[256,2,1024]{2,0,1:T(8,128)(2,1)} async-done(((bf16[1024,2,1024]{2,0,1:T(8,128)(2,1)}), bf16[256,2,1024]{2,0,1:T(8,128)(2,1)}) %reduce-scatter.15.cloned.1.call-update) | async-done | bytes 1048592 | tf_op jit(solution)/shard_map/reduce_scatter | solution.py:188
  1024.5 43.8 %all_gather.42 = bf16[64,6,1024]{2,1,0:T(8,128)(2,1)S(1)} all-gather(bf16[2,6,1024]{2,1,0:T(8,128)(2,1)S(1)} %copy.125), channel_id=1, replica_groups=mesh['dp'=8,'tensor'=4] {'dp','tensor'}, dimensions={0}, use_global_device_ids=true | all-gather | bytes 811008 | tf_op jit(solution)/shard_map/all_gather | solution.py:201
  (254 shorter events, 209.2 us)
Async XLA Ops:
  7.2 182.2 %all-gather.10.cloned.1.call-start = ((), (), s32[]{:S(2)}) async-start(), calls=%async_computation.8 | async-start | bytes 14155776 | tf_op jit(solution)/shard_map/all_gather | solution.py:58
  7.9 230.5 %all-gather.14.cloned.1.call-start = ((), (), s32[]{:S(2)}) async-start(), calls=%async_computation.10 | async-start | bytes 1769472 | tf_op jit(solution)/shard_map/all_gather | solution.py:52
  9.7 264.5 %all-gather.12.cloned.1.call-start = ((), (), s32[]{:S(2)}) async-start(), calls=%async_computation.9 | async-start | bytes 5242880 | tf_op jit(solution)/shard_map/all_gather | solution.py:64
  197.2 166.1 %reduce-scatter.9.cloned.1.call-start = ((), (), s32[]{:S(2)}) async-start(), calls=%async_computation.11 | async-start | bytes 5242880 | tf_op jit(solution)/shard_map/reduce_scatter | solution.py:90
  318.7 96.2 %all-gather.18.cloned.1.call-start = ((), (), s32[]{:S(2)}) async-start(), calls=%async_computation.13 | async-start | bytes 2359296 | tf_op jit(solution)/shard_map/all_gather | solution.py:54
  319.3 130.7 %all-gather.16.cloned.1.call-start = ((), (), s32[]{:S(2)}) async-start(), calls=%async_computation.12 | async-start | bytes 5242880 | tf_op jit(solution)/shard_map/all_gather | solution.py:101
  367.2 239.7 %copy-start.32 = (f32[256,2]{0,1:T(2,128)}, f32[256,2]{0,1:T(2,128)S(1)}, u32[]{:S(2)}) copy-start(f32[256,2]{0,1:T(2,128)S(1)} %fusion.85) | copy-start | bytes 6148
  368.9 132.7 %all-gather.20.cloned.1.call-start = ((), (), s32[]{:S(2)}) async-start(), calls=%async_computation.14 | async-start | bytes 2359296 | tf_op jit(solution)/shard_map/all_gather | solution.py:55
  369.7 167.2 %all-gather.22.cloned.1.call-start = ((), (), s32[]{:S(2)}) async-start(), calls=%async_computation.16 | async-start | bytes 5242880 | tf_op jit(solution)/shard_map/all_gather | solution.py:119
  371.0 232.6 %reduce-scatter.13.cloned.1.call-start = ((), (), s32[]{:S(2)}) async-start(), calls=%async_computation.17 | async-start | bytes 5242880 | tf_op jit(solution)/shard_map/reduce_scatter | solution.py:128
  371.1 248.5 %copy-start.48 = (f32[1024]{0:T(1024)}, f32[1024]{0:T(1024)S(1)}, u32[]{:S(2)}) copy-start(f32[1024]{0:T(1024)S(1)} %convert_element_type.161) | copy-start | bytes 12292
  559.0 84.9 %all-gather.24.cloned.1.call-start = ((), (), s32[]{:S(2)}) async-start(), calls=%async_computation.18 | async-start | bytes 5242880 | tf_op jit(solution)/shard_map/all_gather | solution.py:142
  609.2 196.2 %reduce-scatter.21.cloned.1.call-start = ((), (), s32[]{:S(2)}) async-start(), calls=%async_computation.22 | async-start | bytes 2359296 | tf_op jit(solution)/shard_map/reduce_scatter | solution.py:222
  618.9 188.4 %reduce-scatter.23.cloned.1.call-start = ((), (), s32[]{:S(2)}) async-start(), calls=%async_computation.23 | async-start | bytes 2359296 | tf_op jit(solution)/shard_map/reduce_scatter | solution.py:225
  630.5 221.9 %reduce-scatter.19.cloned.1.call-start = ((), (), s32[]{:S(2)}) async-start(), calls=%async_computation.21 | async-start | bytes 589824 | tf_op jit(solution)/shard_map/reduce_scatter | solution.py:219
  742.6 176.6 %reduce-scatter.17.cloned.1.call-start = ((), (), s32[]{:S(2)}) async-start(), calls=%async_computation.20 | async-start | bytes 1769472 | tf_op jit(solution)/shard_map/reduce_scatter | solution.py:216
  750.5 214.6 %reduce-scatter.11.cloned.1.call-start = ((), (), s32[]{:S(2)}) async-start(), calls=%async_computation.15 | async-start | bytes 5242880 | tf_op jit(solution)/shard_map/reduce_scatter | solution.py:107
  762.6 249.6 %reduce-scatter.15.cloned.1.call-start = ((), (), s32[]{:S(2)}) async-start(), calls=%async_computation.19 | async-start | bytes 5242880 | tf_op jit(solution)/shard_map/reduce_scatter | solution.py:188
  811.6 200.5 %copy-start.29 = (f32[2,1024]{1,0:T(2,128)S(1)}, f32[2,1024]{1,0:T(2,128)}, u32[]{:S(2)}) copy-start(f32[2,1024]{1,0:T(2,128)} %copy-done.28) | copy-start | bytes 24580
  811.6 200.5 %copy-start.31 = (f32[2,1024]{1,0:T(2,128)S(1)}, f32[2,1024]{1,0:T(2,128)}, u32[]{:S(2)}) copy-start(f32[2,1024]{1,0:T(2,128)} %copy-done.30) | copy-start | bytes 24580
  811.6 200.5 %copy-start.33 = (f32[256,2]{0,1:T(2,128)S(1)}, f32[256,2]{0,1:T(2,128)}, u32[]{:S(2)}) copy-start(f32[256,2]{0,1:T(2,128)} %copy-done.32) | copy-start | bytes 6148
  811.7 200.5 %copy-start.35 = (f32[256,2]{0,1:T(2,128)S(1)}, f32[256,2]{0,1:T(2,128)}, u32[]{:S(2)}) copy-start(f32[256,2]{0,1:T(2,128)} %copy-done.34) | copy-start | bytes 6148
  811.7 200.5 %copy-start.39 = (f32[256,2]{0,1:T(2,128)S(1)}, f32[256,2]{0,1:T(2,128)}, u32[]{:S(2)}) copy-start(f32[256,2]{0,1:T(2,128)} %copy-done.38) | copy-start | bytes 6148
  811.7 200.5 %copy-start.43 = (f32[256,2]{0,1:T(2,128)S(1)}, f32[256,2]{0,1:T(2,128)}, u32[]{:S(2)}) copy-start(f32[256,2]{0,1:T(2,128)} %copy-done.42) | copy-start | bytes 6148
  (57 other events, 1754.1 us)
Sparse Core Ops, SparseCore 0:
  10.2 179.1 all-gather.9
  192.0 46.4 all-gather.13
  240.6 33.5 all-gather.11
  318.8 44.4 reduce-scatter.8
  365.5 49.2 all-gather.17
  416.9 32.9 all-gather.15
  452.3 49.2 all-gather.19
  503.8 32.9 all-gather.21
  559.1 44.5 reduce-scatter.12
  609.4 34.4 all-gather.23
  647.4 67.8 reduce-scatter.20
  718.7 66.6 reduce-scatter.22
  789.3 60.9 reduce-scatter.18
  854.6 64.4 reduce-scatter.16
  921.5 43.5 reduce-scatter.10
  967.6 44.5 reduce-scatter.14
where the time goes:
time: 1100 us; the launch traced here: 1090 us
  waiting for transfers between devices  637 us (58%)
  matrix products  191 us (17%)
  blocking collectives  145 us (13%)
  other arithmetic  76.4 us (7%)
  local copies, waits for them, and re-layouts  22.9 us (2%)
  between operations  15.3 us (1%)
    all_gather x1, waiting for transfers between devices, per_device(): mod_full = lax.all_gather(mod_weight, 'dp', axis=0, tiled=True)  177 us
    reduce_scatter x1, waiting for transfers between devices, per_device(): lax.psum_scatter(g_qkv_w.astype(jnp.bfloat16), 'dp', scatter_dimension=0,...  65.2 us
    reduce_scatter x1, waiting for transfers between devices, per_device(): lax.psum_scatter(jnp.einsum('sbke,dke->sbd', part_rows, qkv_full, preferr...  47.1 us
    reduce_scatter x1, waiting for transfers between devices, per_device(): lax.psum_scatter(jnp.einsum('sbf,df->sbd', part_rows, expand_full, prefer...  44.6 us
    reduce_scatter x1, waiting for transfers between devices, per_device(): lax.psum_scatter(jnp.einsum('sbf,of->sbo', part_rows, reduce_full, prefer...  44.2 us
    reduce_scatter x1, waiting for transfers between devices, per_device(): lax.psum_scatter(jnp.einsum('sbe,oe->sbo', part_rows, proj_full, preferre...  44 us
    all_gather x1, blocking collectives, per_device(): lax.all_gather(mod_part.astype(jnp.bfloat16), ('dp', 'tensor'), axis=0, t...  43.8 us
    all_gather x1, waiting for transfers between devices, per_device(): lax.all_gather(expand_weight, 'dp', axis=0, tiled=True)  43.8 us
  transfers between devices with their start and end apart: 16, of which 13 were waited for; matrix products, arithmetic and copies ran while one was open for 17% of the time, Pallas kernels for 0%

commit v1 on v0

v1 whole, which is shorter than its diff:
```python
import functools

import jax
import jax.numpy as jnp
from jax import lax
from jax.experimental import pallas as pl
from jax.experimental.pallas import tpu as pltpu
from jax.sharding import PartitionSpec as P

HEAD_DIM = 64
F32 = jnp.float32
BF16 = jnp.bfloat16
LOG2E = 1.4426950408889634
GELU_C = 0.7978845608028654
GELU_A = 0.044715
NN = (((1,), (0,)), ((), ()))
NT = (((1,), (1,)), ((), ()))
VMEM_BYTES = 56 * 1024 * 1024


def dot(left, right, dims=NN):
    return lax.dot_general(left, right, dims, preferred_element_type=F32)


def params(*kinds):
    return pltpu.CompilerParams(dimension_semantics=kinds, vmem_limit_bytes=VMEM_BYTES)


def attend_kernel(chunk, q_ref, k_ref, v_ref, out_ref, lse_ref):
    length, width = q_ref.shape
    factor = HEAD_DIM ** (-0.5) * LOG2E
    values_t = v_ref[...].astype(F32).T.astype(BF16)
    keys = [k_ref[:, lo : lo + HEAD_DIM] for lo in range(0, width, HEAD_DIM)]

    def body(step, carry):
        rows = pl.ds(pl.multiple_of(step * chunk, chunk), chunk)
        outs = []
        for head, key in enumerate(keys):
            lo = head * HEAD_DIM
            scores = dot(key, q_ref[rows, lo : lo + HEAD_DIM], NT)
            top = jnp.max(scores, 0, keepdims=True)
            weights = jnp.exp2((scores - top) * factor)
            total = jnp.sum(weights, 0, keepdims=True)
            out_t = dot(values_t[lo : lo + HEAD_DIM], weights.astype(BF16))
            outs.append(out_t / total)
            lse_ref[0, head : head + 1, rows] = top * factor + jnp.log(total) * LOG2E
        out_ref[rows, :] = jnp.concatenate(outs, 0).T.astype(BF16)
        return carry

    lax.fori_loop(0, length // chunk, body, 0)


def attend(qkv):
    length, three = qkv.shape
    width = three // 3
    pairs = width // 128
    chunk = min(256, length)
    flops = 4 * length * length * width
    spec = lambda part: pl.BlockSpec((length, 128), lambda i: (0, part * pairs + i))
    return pl.pallas_call(
        functools.partial(attend_kernel, chunk),
        grid=(pairs,),
        in_specs=[spec(0), spec(1), spec(2)],
        out_specs=[
            pl.BlockSpec((length, 128), lambda i: (0, i)),
            pl.BlockSpec((1, 8, length), lambda i: (i, 0, 0)),
        ],
        out_shape=[
            jax.ShapeDtypeStruct((length, width), BF16),
            jax.ShapeDtypeStruct((pairs, 8, length), F32),
        ],
        compiler_params=params("arbitrary"),
        cost_estimate=pl.CostEstimate(
            flops=4 * flops, bytes_accessed=8 * length * width, transcendentals=length * length
        ),
        name="attend",
    )(qkv, qkv, qkv)


def attend_back_kernel(chunk, q_ref, k_ref, v_ref, g_ref, lse_ref, out_ref, dk_ref, dv_ref):
    length, width = q_ref.shape
    total_width = out_ref.shape[1] // 3
    scale = HEAD_DIM ** (-0.5)
    factor = scale * LOG2E
    pair = pl.program_id(0)
    keys_t = k_ref[...].astype(F32).T.astype(BF16)
    heads = range(0, width, HEAD_DIM)
    keys = [k_ref[:, lo : lo + HEAD_DIM] for lo in heads]
    values = [v_ref[:, lo : lo + HEAD_DIM] for lo in heads]
    dk_ref[...] = jnp.zeros_like(dk_ref)
    dv_ref[...] = jnp.zeros_like(dv_ref)

    def columns(part):
        return pl.ds(pl.multiple_of(part * total_width + pair * width, width), width)

    def body(step, carry):
        rows = pl.ds(pl.multiple_of(step * chunk, chunk), chunk)
        outs = []
        for head, (key, value) in enumerate(zip(keys, values)):
            lo = head * HEAD_DIM
            query = q_ref[rows, lo : lo + HEAD_DIM]
            grad = g_ref[rows, lo : lo + HEAD_DIM]
            probs = jnp.exp2(dot(key, query, NT) * factor - lse_ref[0, head : head + 1, rows])
            dv_ref[head] += dot(probs.astype(BF16), grad)
            weighted = probs * dot(value, grad, NT)
            row_dot = jnp.sum(weighted, 0, keepdims=True)
            g_scores = (weighted - probs * row_dot).astype(BF16)
            dk_ref[head] += dot(g_scores, query)
            outs.append(dot(keys_t[lo : lo + HEAD_DIM], g_scores) * scale)
        out_ref[rows, columns(0)] = jnp.concatenate(outs, 0).T.astype(BF16)
        return carry

    lax.fori_loop(0, length // chunk, body, 0)
    n_heads = len(keys)
    out_ref[:, columns(1)] = (
        jnp.concatenate([dk_ref[h] for h in range(n_heads)], 1) * scale
    ).astype(BF16)
    out_ref[:, columns(2)] = jnp.concatenate([dv_ref[h] for h in range(n_heads)], 1).astype(BF16)


def attend_back(qkv, grad_att, lse):
    length, three = qkv.shape
    width = three // 3
    pairs = width // 128
    chunk = min(256, length)
    flops = 10 * length * length * width
    spec = lambda part: pl.BlockSpec((length, 128), lambda i: (0, part * pairs + i))
    return pl.pallas_call(
        functools.partial(attend_back_kernel, chunk),
        grid=(pairs,),
        in_specs=[
            spec(0),
            spec(1),
            spec(2),
            pl.BlockSpec((length, 128), lambda i: (0, i)),
            pl.BlockSpec((1, 8, length), lambda i: (i, 0, 0)),
        ],
        out_specs=pl.BlockSpec((length, three), lambda i: (0, 0)),
        out_shape=jax.ShapeDtypeStruct((length, three), BF16),
        scratch_shapes=[
            pltpu.VMEM((128 // HEAD_DIM, length, HEAD_DIM), F32),
            pltpu.VMEM((128 // HEAD_DIM, length, HEAD_DIM), F32),
        ],
        compiler_params=params("arbitrary"),
        cost_estimate=pl.CostEstimate(
            flops=4 * flops, bytes_accessed=16 * length * width, transcendentals=length * length
        ),
        name="attend_back",
    )(qkv, qkv, qkv, grad_att, lse)


def mlp_kernel(
    x_ref, g_ref, up_ref, down_ref, bias_ref, hid_ref, gpre_ref, out_ref, gx_ref, gbias_ref
):
    pre = dot(x_ref[...], up_ref[...]) + bias_ref[...].astype(F32)
    square = pre * pre
    th = jnp.tanh(GELU_C * pre * (1.0 + GELU_A * square))
    half = 0.5 * (1.0 + th)
    hidden = (pre * half).astype(BF16)
    slope = half + (0.5 * GELU_C) * pre * (1.0 - th * th) * (1.0 + 3.0 * GELU_A * square)
    g_pre = (dot(g_ref[...], down_ref[...]) * slope).astype(BF16)
    hid_ref[...] = hidden
    gpre_ref[...] = g_pre
    gx_ref[...] = dot(g_pre, up_ref[...], NT).astype(BF16)
    out_ref[...] = dot(hidden, down_ref[...], NT).astype(BF16)

    @pl.when(pl.program_id(0) == 0)
    def _():
        gbias_ref[...] = jnp.zeros_like(gbias_ref)

    gbias_ref[...] += jnp.sum(g_pre.astype(F32), 0, keepdims=True)


def mlp(x_full, g_full, up, down, bias):
    tokens, width = x_full.shape
    hidden = up.shape[1]
    tile = min(256, tokens)
    rows = lambda cols: pl.BlockSpec((tile, cols), lambda i: (i, 0))
    whole = lambda r, c: pl.BlockSpec((r, c), lambda i: (0, 0))
    return pl.pallas_call(
        mlp_kernel,
        grid=(tokens // tile,),
        in_specs=[
            rows(width),
            rows(width),
            whole(width, hidden),
            whole(width, hidden),
            whole(1, hidden),
        ],
        out_specs=[rows(hidden), rows(hidden), rows(width), rows(width), whole(1, hidden)],
        out_shape=[
            jax.ShapeDtypeStruct((tokens, hidden), BF16),
            jax.ShapeDtypeStruct((tokens, hidden), BF16),
            jax.ShapeDtypeStruct((tokens, width), BF16),
            jax.ShapeDtypeStruct((tokens, width), BF16),
            jax.ShapeDtypeStruct((1, hidden), F32),
        ],
        compiler_params=params("arbitrary"),
        cost_estimate=pl.CostEstimate(
            flops=8 * tokens * width * hidden,
            bytes_accessed=12 * tokens * width + 4 * width * hidden,
            transcendentals=tokens * hidden,
        ),
        name="feed_forward",
    )(x_full, g_full, up, down, bias)


def norm_parts(values):
    centered = values - jnp.mean(values, -1, keepdims=True)
    scale = lax.rsqrt(jnp.mean(centered * centered, -1, keepdims=True) + 1e-06)
    return centered * scale, scale


def norm_back(normed, scale, grad):
    mean_g = jnp.mean(grad, -1, keepdims=True)
    mean_gn = jnp.mean(grad * normed, -1, keepdims=True)
    return scale * (grad - mean_g - normed * mean_gn)


def swap(value, bit):
    n = lax.axis_size("tensor")
    return lax.ppermute(value, "tensor", [(i, i ^ bit) for i in range(n)])


def spread(value):
    pair = jnp.concatenate([value, swap(value, 2)], 0)
    return jnp.concatenate([pair, swap(pair, 1)], 0)


def collect(value):
    half = value.shape[0] // 2
    pair = value[:half].astype(F32) + swap(value[half:], 1).astype(F32)
    own = half // 2
    return pair[:own] + swap(pair[own:].astype(BF16), 2).astype(F32)


def per_device(
    latents,
    conditioning,
    mod_weight,
    mod_bias,
    qkv_weight,
    qkv_bias,
    proj_weight,
    proj_bias,
    expand_weight,
    expand_bias,
    reduce_weight,
    reduce_bias,
    out_grad,
):
    n_tensor = lax.axis_size("tensor")
    n_dp = lax.axis_size("dp")
    row_count, images, model_width = latents.shape
    local_width = qkv_weight.shape[2]
    hidden_width = expand_weight.shape[1]
    mod_rows = mod_weight.shape[0]

    qkv_full = lax.all_gather(
        qkv_weight.reshape(mod_rows, 3 * local_width), "dp", axis=0, tiled=True
    )
    rest = jnp.concatenate([expand_weight, reduce_weight, proj_weight], 1)
    rest, qkv_full = lax.optimization_barrier((rest, qkv_full))
    rest_full = lax.all_gather(rest, "dp", axis=0, tiled=True)
    expand_full = rest_full[:, :hidden_width]
    reduce_full = rest_full[:, hidden_width : 2 * hidden_width]
    proj_full = rest_full[:, 2 * hidden_width :]

    cond_float = conditioning.astype(F32)
    cond_low = jax.nn.silu(cond_float).astype(BF16)
    cond_cols = lax.all_to_all(
        cond_low.reshape(images, n_dp, mod_rows).transpose(1, 0, 2), "dp", 0, 0, tiled=True
    ).reshape(n_dp * images, mod_rows)
    mod_part = jnp.einsum("gd,dke->gke", cond_cols, mod_weight, preferred_element_type=F32)
    mod_sum = jnp.sum(
        lax.all_to_all(
            mod_part.reshape(n_dp, images, 6, model_width), "dp", 0, 0, tiled=True
        ).reshape(n_dp, images, 6, model_width),
        0,
    )
    modulation = mod_sum + mod_bias.astype(F32)[None]

    x = [latents[:, i].astype(F32) for i in range(images)]
    grad_y = [out_grad[:, i].astype(F32) for i in range(images)]
    mod = [[modulation[i, k] for k in range(6)] for i in range(images)]
    both = range(images)

    norm_a = [norm_parts(x[i]) for i in both]
    shifted_a = [(norm_a[i][0] * (1.0 + mod[i][1]) + mod[i][0]).astype(BF16) for i in both]
    full_a = [spread(v) for v in shifted_a]
    grad_m = [(grad_y[i] * mod[i][5]).astype(BF16) for i in both]
    full_gm = [spread(v) for v in grad_m]

    bias_qkv = qkv_bias.astype(F32).reshape(1, 3 * local_width)
    qkv = [(dot(v, qkv_full) + bias_qkv).astype(BF16) for v in full_a]
    attended = [attend(v) for v in qkv]
    branch_a = [
        collect(dot(out, proj_full, NT).astype(BF16)) + proj_bias.astype(F32)
        for out, _ in attended
    ]
    mid = [x[i] + mod[i][2] * branch_a[i] for i in both]
    norm_m = [norm_parts(mid[i]) for i in both]
    shifted_m = [(norm_m[i][0] * (1.0 + mod[i][4]) + mod[i][3]).astype(BF16) for i in both]
    full_m = [spread(v) for v in shifted_m]

    ff = [
        mlp(full_m[i], full_gm[i], expand_full, reduce_full, expand_bias.reshape(1, hidden_width))
        for i in both
    ]
    grad_sm = [collect(ff[i][3]) for i in both]
    branch_m = [collect(ff[i][2]) + reduce_bias.astype(F32) for i in both]
    result = jnp.stack([(mid[i] + mod[i][5] * branch_m[i]).astype(BF16) for i in both], 1)

    tn = (((0,), (0,)), ((), ()))

    def weight_grad(lefts, rights):
        total = dot(lefts[0], rights[0], tn)
        for left, right in zip(lefts[1:], rights[1:]):
            total = total + dot(left, right, tn)
        return total.astype(BF16)

    def scatter_rows(value):
        return lax.psum_scatter(value, "dp", scatter_dimension=0, tiled=True).astype(F32)

    g_reduce_w = scatter_rows(weight_grad(full_gm, [f[0] for f in ff]))
    g_expand_w = scatter_rows(weight_grad(full_m, [f[1] for f in ff]))

    grad_mid = [
        grad_y[i] + norm_back(*norm_m[i], grad_sm[i] * (1.0 + mod[i][4])) for i in both
    ]
    grad_a = [(grad_mid[i] * mod[i][2]).astype(BF16) for i in both]
    full_ga = [spread(v) for v in grad_a]
    grad_att = [dot(v, proj_full).astype(BF16) for v in full_ga]
    g_proj_w = scatter_rows(weight_grad(full_ga, [out for out, _ in attended]))
    grad_qkv = [attend_back(qkv[i], grad_att[i], attended[i][1]) for i in both]
    grad_sa = [collect(dot(v, qkv_full, NT).astype(BF16)) for v in grad_qkv]
    g_qkv_w = scatter_rows(weight_grad(full_a, grad_qkv)).reshape(mod_rows, 3, local_width)
    grad_latent = jnp.stack(
        [
            grad_mid[i] + norm_back(*norm_a[i], grad_sa[i] * (1.0 + mod[i][1]))
            for i in both
        ],
        1,
    )

    mod_parts = jnp.stack(
        [
            jnp.stack(
                [
                    jnp.sum(grad_sa[i], 0),
                    jnp.sum(grad_sa[i] * norm_a[i][0], 0),
                    jnp.sum(grad_mid[i] * branch_a[i], 0),
                    jnp.sum(grad_sm[i], 0),
                    jnp.sum(grad_sm[i] * norm_m[i][0], 0),
                    jnp.sum(grad_y[i] * branch_m[i], 0),
                ],
                0,
            )
            for i in both
        ],
        0,
    )
    mod_cols = model_width // n_tensor
    by_cols = mod_parts.reshape(images, 6, n_tensor, mod_cols).transpose(2, 0, 1, 3)
    own_cols = jnp.sum(
        lax.all_to_all(by_cols, "tensor", 0, 0, tiled=True).reshape(by_cols.shape), 0
    )
    all_cols = lax.all_to_all(
        jnp.broadcast_to(own_cols[None], (n_dp,) + own_cols.shape), "dp", 0, 0, tiled=True
    ).reshape(n_dp * images, 6, mod_cols)
    g_mod_w = jnp.einsum(
        "gd,gke->dke", cond_cols, all_cols.astype(BF16), preferred_element_type=F32
    )
    g_mod_all = lax.all_gather(all_cols, "tensor", axis=2, tiled=True)
    g_mod_b = jnp.sum(g_mod_all, 0)
    act_rows = jnp.einsum(
        "gke,dke->gd", g_mod_all.astype(BF16), mod_weight, preferred_element_type=F32
    )
    grad_act = (
        lax.all_to_all(act_rows.reshape(n_dp, images, mod_rows), "dp", 0, 0, tiled=True)
        .reshape(n_dp, images, mod_rows)
        .transpose(1, 0, 2)
        .reshape(images, n_dp * mod_rows)
    )
    silu_out, silu_pull = jax.vjp(jax.nn.silu, cond_float)
    grad_cond = silu_pull(grad_act)[0]

    shared = jnp.concatenate(
        [
            sum(jnp.sum(v.astype(F32), 0) for v in grad_a),
            sum(jnp.sum(v.astype(F32), 0) for v in grad_m),
        ]
    )
    for bit in (1, 2):
        shared = shared + swap(shared, bit)
    biases = jnp.concatenate(
        [
            sum(jnp.sum(v.astype(F32), 0) for v in grad_qkv),
            sum(f[4][0] for f in ff),
            shared,
        ]
    )
    bit = 1
    while bit < n_dp:
        biases = biases + lax.ppermute(biases, "dp", [(i, i ^ bit) for i in range(n_dp)])
        bit *= 2
    cuts = [0, 3 * local_width]
    cuts.append(cuts[-1] + hidden_width)
    cuts.append(cuts[-1] + model_width)
    cuts.append(cuts[-1] + model_width)
    g_qkv_b, g_expand_b, g_proj_b, g_reduce_b = (
        biases[lo:hi] for lo, hi in zip(cuts, cuts[1:])
    )
    return (
        result,
        grad_latent,
        grad_cond,
        g_mod_w,
        g_mod_b,
        g_qkv_w,
        g_qkv_b.reshape(3, local_width),
        g_proj_w,
        g_proj_b,
        g_expand_w,
        g_expand_b,
        g_reduce_w,
        g_reduce_b,
    )


def solution(mesh):
    in_specs = (
        P("tensor", "dp", None),
        P("dp", None),
        P("dp", None, None),
        P(),
        P("dp", None, "tensor"),
        P(None, "tensor"),
        P("dp", "tensor"),
        P(),
        P("dp", "tensor"),
        P("tensor"),
        P("dp", "tensor"),
        P(),
        P("tensor", "dp", None),
    )
    out_specs = (
        P("tensor", "dp", None),
        P("tensor", "dp", None),
        P("dp", None),
        P("dp", None, "tensor"),
        P(),
        P("dp", None, "tensor"),
        P(None, "tensor"),
        P("dp", "tensor"),
        P(),
        P("dp", "tensor"),
        P("tensor"),
        P("dp", "tensor"),
        P(),
    )
    return jax.shard_map(
        per_device, mesh=mesh, in_specs=in_specs, out_specs=out_specs, check_vma=False
    )
```

time: 1100 us -> 592 us (0.54)
  waiting for transfers between devices: 637 us -> 263 us
  blocking collectives: 145 us -> 6.15 us
  matrix products: 191 us -> 56.1 us
  Pallas kernels: 0 us -> 102 us
  starting transfers between devices: 1.08 us -> 48.5 us
  other arithmetic: 76.4 us -> 60.2 us
  local copies, waits for them, and re-layouts: 22.9 us -> 35 us
    all_gather x8 -> x2, waiting for transfers between devices: 390 us -> 47.5 us  [the longest x1 47.5 us: per_device(): lax.all_gather(qkv_weight.reshape(mod_rows, 3 * local_width), 'dp', axis=...]
    reduce_scatter x8 -> x4, waiting for transfers between devices: 245 us -> 54.8 us  [scatter_rows(): lax.psum_scatter(value, 'dp', scatter_dimension=0, tiled=True).astype(F32)]
    dot_general x27 -> x19, matrix products: 191 us -> 56.1 us  [the longest x16 53.5 us: dot(): return lax.dot_general(left, right, dims, preferred_element_type=F32)]
    ppermute x0 -> x37, waiting for transfers between devices: none -> 124 us  [the longest x34 124 us: swap(): return lax.ppermute(value, 'tensor', [(i, i ^ bit) for i in range(n)])]
    pallas_call x0 -> x6, Pallas kernels: none -> 102 us  [the longest x2 42 us: attend_back(): pl.pallas_call(functools.partial(attend_back_kernel, chunk), grid=(pairs,...]
    all_gather x3 -> x1, blocking collectives: 107 us -> 6.15 us  [per_device(): g_mod_all = lax.all_gather(all_cols, 'tensor', axis=2, tiled=True)]
    psum x1 -> x0, blocking collectives: 37.9 us -> none  [per_device(): bias_total = lax.psum((g_qkv_b, g_proj_b, g_expand_b, g_reduce_b), 'dp')]
    all_to_all x0 -> x5, waiting for transfers between devices: none -> 35.9 us  [the longest x1 20.7 us: per_device(): lax.all_to_all(mod_part.reshape(n_dp, images, 6, model_width), 'dp', 0, 0...]
  transfers between devices with their start and end apart: 16 -> 48, of which waited for: 13 -> 22; matrix products, arithmetic and copies ran while one was open for 17% -> 23% of each run, Pallas kernels for 0% -> 15%
where the time goes in v1:
time: 592 us; the launch traced here: 586 us
  waiting for transfers between devices  263 us (44%)
  Pallas kernels  102 us (17%)
  other arithmetic  60.2 us (10%)
  matrix products  56.1 us (9%)
  starting transfers between devices  48.5 us (8%)
  local copies, waits for them, and re-layouts  35 us (6%)
  between operations  15.9 us (3%)
  blocking collectives  6.15 us (1%)
    ppermute x34, waiting for transfers between devices, swap(): return lax.ppermute(value, 'tensor', [(i, i ^ bit) for i in range(n)])  124 us
    reduce_scatter x4, waiting for transfers between devices, scatter_rows(): lax.psum_scatter(value, 'dp', scatter_dimension=0, tiled=True).astype(F32)  54.8 us
    dot_general x16, matrix products, dot(): return lax.dot_general(left, right, dims, preferred_element_type=F32)  53.5 us
    all_gather x1, waiting for transfers between devices, per_device(): lax.all_gather(qkv_weight.reshape(mod_rows, 3 * local_width), 'dp', axis=...  47.5 us
    pallas_call x2, Pallas kernels, attend_back(): pl.pallas_call(functools.partial(attend_back_kernel, chunk), grid=(pairs,...  42 us
    pallas_call x2, Pallas kernels, attend(): pl.pallas_call(functools.partial(attend_kernel, chunk), grid=(pairs,), in...  30.7 us
    pallas_call x2, Pallas kernels, mlp(): pl.pallas_call(mlp_kernel, grid=(tokens // tile,), in_specs=[rows(width),...  29.1 us
    ppermute x34, starting transfers between devices, swap(): return lax.ppermute(value, 'tensor', [(i, i ^ bit) for i in range(n)])  26.9 us
  transfers between devices with their start and end apart: 48, of which 22 were waited for; matrix products, arithmetic and copies ran while one was open for 23% of the time, Pallas kernels for 15%

profile of v1, /device:TPU:0, one launch (start us, length us, event | category | flops | bytes accessed | tf_op | source)
XLA Modules:
  0.0 586.2 jit_solution(15082777551664441816)
XLA Ops:
  11.2 47.5 %all-gather.3.cloned.1.call-done = bf16[1024,768]{0,1:T(8,128)(2,1)} async-done(((bf16[128,768]{0,1:T(8,128)(2,1)}), bf16[1024,768]{0,1:T(8,128)(2,1)}) %all-gather.3.cloned.1.call-update) | async-done | bytes 1572880 | tf_op jit(solution)/shard_map/all_gather | solution.py:259
  75.7 20.7 %all-to-all-done.1 = f32[8,2,6,1024]{3,1,2,0:T(2,128)S(1)} async-done(((f32[8,2,6,1024]{3,1,2,0:T(2,128)}), f32[8,2,6,1024]{3,1,2,0:T(2,128)S(1)}, u32[]{:S(2)}, u32[]{:S(2)}) %all-to-all-start.1) | async-done | bytes 393248 | tf_op jit(solution)/shard_map/all_to_all | solution.py:276
  99.6 8.6 %collective-permute-done = bf16[256,1024]{1,0:T(8,128)(2,1)S(1)} collective-permute-done((bf16[256,1024]{1,0:T(8,128)(2,1)S(1)}, bf16[256,1024]{1,0:T(8,128)(2,1)S(1)}, u32[]{:S(2)}, u32[]{:S(2)}) %collective-permute-start) | collective-permute-done | bytes 524320 | tf_op jit(solution)/shard_map/ppermute | solution.py:222
  111.4 12.6 %collective-permute-done.10 = bf16[256,1024]{1,0:T(8,128)(2,1)S(1)} collective-permute-done((bf16[256,1024]{1,0:T(8,128)(2,1)S(1)}, bf16[256,1024]{1,0:T(8,128)(2,1)S(1)}, u32[]{:S(2)}, u32[]{:S(2)}) %collective-permute-start.10) | collective-permute-done | bytes 524320 | tf_op jit(solution)/shard_map/ppermute | solution.py:222
  130.0 15.5 %attend.2 = (bf16[1024,256]{1,0:T(8,128)(2,1)}, f32[2,8,1024]{2,1,0:T(8,128)}) custom-call(bf16[1024,768]{1,0:T(8,128)(2,1)} %add_convert_fusion.4.q_ref.k_ref.v_ref, bf16[1024,768]{1,0:T(8,128)(2,1)} %add_convert_fusion.4.q_ref.k_ref.v_ref, bf16[1024,768]{1,0:T(8,128)(2,1)} %add_convert_fusion.4.q_ref.k_ref.v_ref), custom_call_target="tpu_custom_call" | custom-call | flops 4294967296 | bytes 2097152 | tf_op jit(solution)/shard_map/attend/pallas_call | solution.py:60
  149.8 15.2 %attend.3 = (bf16[1024,256]{1,0:T(8,128)(2,1)}, f32[2,8,1024]{2,1,0:T(8,128)}) custom-call(bf16[1024,768]{1,0:T(8,128)(2,1)} %add_convert_fusion.3.q_ref.k_ref.v_ref, bf16[1024,768]{1,0:T(8,128)(2,1)} %add_convert_fusion.3.q_ref.k_ref.v_ref, bf16[1024,768]{1,0:T(8,128)(2,1)} %add_convert_fusion.3.q_ref.k_ref.v_ref), custom_call_target="tpu_custom_call" | custom-call | flops 4294967296 | bytes 2097152 | tf_op jit(solution)/shard_map/attend/pallas_call | solution.py:60
  176.5 9.2 %collective-permute-done.16 = bf16[256,1024]{1,0:T(8,128)(2,1)S(1)} collective-permute-done((bf16[256,1024]{1,0:T(8,128)(2,1)S(1)}, bf16[256,1024]{1,0:T(8,128)(2,1)S(1)}, u32[]{:S(2)}, u32[]{:S(2)}) %collective-permute-start.16) | collective-permute-done | bytes 524320 | tf_op jit(solution)/shard_map/ppermute | solution.py:222
  185.9 11.1 %collective-permute-done.6 = bf16[256,1024]{1,0:T(8,128)(2,1)S(1)} collective-permute-done((bf16[256,1024]{1,0:T(8,128)(2,1)S(1)}, bf16[256,1024]{1,0:T(8,128)(2,1)S(1)}, u32[]{:S(2)}, u32[]{:S(2)}) %collective-permute-start.6) | collective-permute-done | bytes 524320 | tf_op jit(solution)/shard_map/ppermute | solution.py:222
  197.1 11.1 %collective-permute-done.13 = bf16[256,1024]{1,0:T(8,128)(2,1)S(1)} collective-permute-done((bf16[256,1024]{1,0:T(8,128)(2,1)S(1)}, bf16[256,1024]{1,0:T(8,128)(2,1)S(1)}, u32[]{:S(2)}, u32[]{:S(2)}) %collective-permute-start.13) | collective-permute-done | bytes 524320 | tf_op jit(solution)/shard_map/ppermute | solution.py:222
  208.2 10.7 %collective-permute-done.3 = bf16[256,1024]{1,0:T(8,128)(2,1)S(1)} collective-permute-done((bf16[256,1024]{1,0:T(8,128)(2,1)S(1)}, bf16[256,1024]{1,0:T(8,128)(2,1)S(1)}, u32[]{:S(2)}, u32[]{:S(2)}) %collective-permute-start.3) | collective-permute-done | bytes 524320 | tf_op jit(solution)/shard_map/ppermute | solution.py:222
  222.3 11.3 %collective-permute-done.4 = bf16[256,1024]{1,0:T(8,128)(2,1)S(1)} collective-permute-done((bf16[256,1024]{1,0:T(8,128)(2,1)S(1)}, bf16[256,1024]{1,0:T(8,128)(2,1)S(1)}, u32[]{:S(2)}, u32[]{:S(2)}) %collective-permute-start.4) | collective-permute-done | bytes 524320 | tf_op jit(solution)/shard_map/ppermute | solution.py:222
  239.8 8.6 %collective-permute-done.14 = bf16[256,1024]{1,0:T(8,128)(2,1)S(1)} collective-permute-done((bf16[256,1024]{1,0:T(8,128)(2,1)S(1)}, bf16[256,1024]{1,0:T(8,128)(2,1)S(1)}, u32[]{:S(2)}, u32[]{:S(2)}) %collective-permute-start.14) | collective-permute-done | bytes 524320 | tf_op jit(solution)/shard_map/ppermute | solution.py:222
  253.8 14.8 %feed_forward.2 = (bf16[1024,1024]{1,0:T(8,128)(2,1)}, bf16[1024,1024]{1,0:T(8,128)(2,1)}, bf16[1024,1024]{1,0:T(8,128)(2,1)}, bf16[1024,1024]{1,0:T(8,128)(2,1)}, f32[1,1024]{1,0:T(1,128)}) custom-call(bf16[1024,1024]{1,0:T(8,128)(2,1)} %pad_maximum_fusion.1.x_ref, bf16[1024,1024]{1,0:T(8,128)(2,1)} %pad_maximum_fusion.2.g_ref, ...), custom_call_target="tpu_custom_call" | custom-call | flops 8589934592 | bytes 16777216 | tf_op jit(solution)/shard_map/feed_forward/pallas_call | solution.py:180
  274.8 14.3 %feed_forward.3 = (bf16[1024,1024]{1,0:T(8,128)(2,1)}, bf16[1024,1024]{1,0:T(8,128)(2,1)}, bf16[1024,1024]{1,0:T(8,128)(2,1)}, bf16[1024,1024]{1,0:T(8,128)(2,1)}, f32[1,1024]{1,0:T(1,128)}) custom-call(bf16[1024,1024]{1,0:T(8,128)(2,1)} %pad_maximum_fusion.4.x_ref, bf16[1024,1024]{1,0:T(8,128)(2,1)} %pad_maximum_fusion.5.g_ref, ...), custom_call_target="tpu_custom_call" | custom-call | flops 8589934592 | bytes 16777216 | tf_op jit(solution)/shard_map/feed_forward/pallas_call | solution.py:180
  317.8 5.1 collective-permute-done.27
  326.8 7.2 %collective-permute-done.19 = bf16[256,1024]{1,0:T(8,128)(2,1)S(1)} collective-permute-done((bf16[256,1024]{1,0:T(8,128)(2,1)S(1)}, bf16[256,1024]{1,0:T(8,128)(2,1)S(1)}, u32[]{:S(2)}, u32[]{:S(2)}) %collective-permute-start.19) | collective-permute-done | bytes 524320 | tf_op jit(solution)/shard_map/ppermute | solution.py:222
  334.1 11.2 %collective-permute-done.21 = bf16[256,1024]{1,0:T(8,128)(2,1)S(1)} collective-permute-done((bf16[256,1024]{1,0:T(8,128)(2,1)S(1)}, bf16[256,1024]{1,0:T(8,128)(2,1)S(1)}, u32[]{:S(2)}, u32[]{:S(2)}) %collective-permute-start.21) | collective-permute-done | bytes 524320 | tf_op jit(solution)/shard_map/ppermute | solution.py:222
  345.3 11.2 %collective-permute-done.9 = bf16[256,1024]{1,0:T(8,128)(2,1)S(1)} collective-permute-done((bf16[256,1024]{1,0:T(8,128)(2,1)S(1)}, bf16[256,1024]{1,0:T(8,128)(2,1)S(1)}, u32[]{:S(2)}, u32[]{:S(2)}) %collective-permute-start.9) | collective-permute-done | bytes 524320 | tf_op jit(solution)/shard_map/ppermute | solution.py:222
  362.5 5.3 collective-permute-done.28
  383.9 21.1 %attend_back.3 = bf16[1024,768]{1,0:T(8,128)(2,1)} custom-call(bf16[1024,768]{1,0:T(8,128)(2,1)} %add_convert_fusion.3.q_ref.k_ref.v_ref, bf16[1024,768]{1,0:T(8,128)(2,1)} %add_convert_fusion.3.q_ref.k_ref.v_ref, bf16[1024,768]{1,0:T(8,128)(2,1)} %add_convert_fusion.3.q_ref.k_ref.v_ref, bf16[1024,256]{1,0:T(8,128)(2,1)} %convolution_convert_fusion.4.g_ref, ...), custom_call_target="tpu_custom_call" | custom-call | flops 10737418240 | bytes 4194304 | tf_op jit(solution)/shard_map/attend_back/pallas_call | solution.py:128
  414.1 20.9 %attend_back.2 = bf16[1024,768]{1,0:T(8,128)(2,1)} custom-call(bf16[1024,768]{1,0:T(8,128)(2,1)} %add_convert_fusion.4.q_ref.k_ref.v_ref, bf16[1024,768]{1,0:T(8,128)(2,1)} %add_convert_fusion.4.q_ref.k_ref.v_ref, bf16[1024,768]{1,0:T(8,128)(2,1)} %add_convert_fusion.4.q_ref.k_ref.v_ref, bf16[1024,256]{1,0:T(8,128)(2,1)} %convolution_convert_fusion.5.g_ref, ...), custom_call_target="tpu_custom_call" | custom-call | flops 10737418240 | bytes 4194304 | tf_op jit(solution)/shard_map/attend_back/pallas_call | solution.py:128
  473.9 34.2 %reduce-scatter.7.cloned.1.call-done = bf16[128,256]{1,0:T(8,128)(2,1)} async-done(((bf16[1024,256]{1,0:T(8,128)(2,1)}), bf16[128,256]{1,0:T(8,128)(2,1)}) %reduce-scatter.7.cloned.1.call-update) | async-done | bytes 65552 | tf_op jit(solution)/shard_map/reduce_scatter | solution.py:323
  538.3 6.1 %all_gather.11 = f32[16,6,1024]{2,0,1:T(8,128)S(1)} all-gather(f32[16,6,256]{2,0,1:T(8,128)S(1)} %reshape.226), channel_id=1, replica_groups=mesh['dp'=8,'tensor'=4] {'tensor'}, dimensions={2}, use_global_device_ids=true | all-gather | bytes 491520 | tf_op jit(solution)/shard_map/all_gather | solution.py:374
  556.3 20.6 %reduce-scatter.5.cloned.1.call-done = bf16[128,768]{1,0:T(8,128)(2,1)} async-done(((bf16[1024,768]{1,0:T(8,128)(2,1)}), bf16[128,768]{1,0:T(8,128)(2,1)}) %reduce-scatter.5.cloned.1.call-update) | async-done | bytes 196624 | tf_op jit(solution)/shard_map/reduce_scatter | solution.py:323
  (414 shorter events, 216.0 us)
Async XLA Ops:
  7.2 51.5 %all-gather.3.cloned.1.call-start = ((), (), s32[]{:S(2)}) async-start(), calls=%async_computation.9 | async-start | bytes 1769472 | tf_op jit(solution)/shard_map/all_gather | solution.py:259
  9.2 155.8 %all-gather.5.cloned.1.call-start = ((), (), s32[]{:S(2)}) async-start(), calls=%async_computation.10 | async-start | bytes 5308416 | tf_op jit(solution)/shard_map/all_gather | solution.py:264
  70.4 26.1 %all-to-all-start.1 = ((f32[8,2,6,1024]{3,1,2,0:T(2,128)}), f32[8,2,6,1024]{3,1,2,0:T(2,128)S(1)}, u32[]{:S(2)}, u32[]{:S(2)}) async-start(f32[8,2,6,1024]{3,1,2,0:T(2,128)} %copy.80), calls=%async_computation.1 | async-start | bytes 786432 | tf_op jit(solution)/shard_map/all_to_all | solution.py:276
  73.8 391.7 %reduce-scatter.9.cloned.1.call-start = ((), (), s32[]{:S(2)}) async-start(), calls=%async_computation.13 | async-start | bytes 2359296 | tf_op jit(solution)/shard_map/reduce_scatter | solution.py:323
  125.2 20.3 %collective-permute-start.11 = (bf16[512,1024]{1,0:T(8,128)(2,1)}, bf16[512,1024]{1,0:T(8,128)(2,1)}, u32[]{:S(2)}, u32[]{:S(2)}) collective-permute-start(bf16[512,1024]{1,0:T(8,128)(2,1)} %pad_maximum_fusion.12), channel_id=1, source_target_pairs={{0,1},{1,0},{2,3},{3,2},{4,5},{5,4},{6,7},{7,6},{8,9},{9,8},{10,11... | collective-permute-start | bytes 3145736 | tf_op jit(solution)/shard_map/ppermute | solution.py:222
  173.0 24.0 %collective-permute-start.6 = (bf16[256,1024]{1,0:T(8,128)(2,1)S(1)}, bf16[256,1024]{1,0:T(8,128)(2,1)S(1)}, u32[]{:S(2)}, u32[]{:S(2)}) collective-permute-start(bf16[256,1024]{1,0:T(8,128)(2,1)S(1)} %get-tuple-element.139), channel_id=1, source_target_pairs={{0,2},{1,3},{2,0},{3,1},{4,6},{5,7},{6,4},{7,5},{8,10},{9,11},{10,... | collective-permute-start | bytes 1572872 | tf_op jit(solution)/shard_map/ppermute | solution.py:222
  173.8 34.3 %collective-permute-start.13 = (bf16[256,1024]{1,0:T(8,128)(2,1)S(1)}, bf16[256,1024]{1,0:T(8,128)(2,1)S(1)}, u32[]{:S(2)}, u32[]{:S(2)}) collective-permute-start(bf16[256,1024]{1,0:T(8,128)(2,1)S(1)} %slice.391), channel_id=1, source_target_pairs={{0,2},{1,3},{2,0},{3,1},{4,6},{5,7},{6,4},{7,5},{8,10},{9,11},{10,... | collective-permute-start | bytes 1572872 | tf_op jit(solution)/shard_map/ppermute | solution.py:222
  176.1 42.7 %collective-permute-start.3 = (bf16[256,1024]{1,0:T(8,128)(2,1)S(1)}, bf16[256,1024]{1,0:T(8,128)(2,1)S(1)}, u32[]{:S(2)}, u32[]{:S(2)}) collective-permute-start(bf16[256,1024]{1,0:T(8,128)(2,1)S(1)} %slice.393), channel_id=1, source_target_pairs={{0,2},{1,3},{2,0},{3,1},{4,6},{5,7},{6,4},{7,5},{8,10},{9,11},{10,... | collective-permute-start | bytes 1572872 | tf_op jit(solution)/shard_map/ppermute | solution.py:222
  185.8 52.3 %collective-permute-start.17 = (bf16[512,1024]{1,0:T(8,128)(2,1)S(1)}, bf16[512,1024]{1,0:T(8,128)(2,1)S(1)}, u32[]{:S(2)}, u32[]{:S(2)}) collective-permute-start(bf16[512,1024]{1,0:T(8,128)(2,1)S(1)} %pad_maximum_fusion.14), channel_id=1, source_target_pairs={{0,1},{1,0},{2,3},{3,2},{4,5},{5,4},{6,7},{7,6},{8,9},{9,8},{10,11... | collective-permute-start | bytes 3145736 | tf_op jit(solution)/shard_map/ppermute | solution.py:222
  197.0 39.4 %collective-permute-start.7 = (bf16[512,1024]{1,0:T(8,128)(2,1)S(1)}, bf16[512,1024]{1,0:T(8,128)(2,1)S(1)}, u32[]{:S(2)}, u32[]{:S(2)}) collective-permute-start(bf16[512,1024]{1,0:T(8,128)(2,1)S(1)} %pad_maximum_fusion.11), channel_id=1, source_target_pairs={{0,1},{1,0},{2,3},{3,2},{4,5},{5,4},{6,7},{7,6},{8,9},{9,8},{10,11... | collective-permute-start | bytes 3145736 | tf_op jit(solution)/shard_map/ppermute | solution.py:222
  249.5 22.6 %collective-permute-start.15 = (bf16[512,1024]{1,0:T(8,128)(2,1)}, bf16[512,1024]{1,0:T(8,128)(2,1)}, u32[]{:S(2)}, u32[]{:S(2)}) collective-permute-start(bf16[512,1024]{1,0:T(8,128)(2,1)} %pad_maximum_fusion.13), channel_id=1, source_target_pairs={{0,1},{1,0},{2,3},{3,2},{4,5},{5,4},{6,7},{7,6},{8,9},{9,8},{10,11... | collective-permute-start | bytes 3145736 | tf_op jit(solution)/shard_map/ppermute | solution.py:222
  293.6 21.8 %collective-permute-start.8 = (bf16[512,1024]{1,0:T(8,128)(2,1)}, bf16[512,1024]{1,0:T(8,128)(2,1)}, u32[]{:S(2)}, u32[]{:S(2)}) collective-permute-start(bf16[512,1024]{1,0:T(8,128)(2,1)} %slice.199), channel_id=1, source_target_pairs={{0,1},{1,0},{2,3},{3,2},{4,5},{5,4},{6,7},{7,6},{8,9},{9,8},{10,11... | collective-permute-start | bytes 3145736 | tf_op jit(solution)/shard_map/ppermute | solution.py:222
  301.2 166.1 %reduce-scatter.11.cloned.1.call-start = ((), (), s32[]{:S(2)}) async-start(), calls=%async_computation.14 | async-start | bytes 2359296 | tf_op jit(solution)/shard_map/reduce_scatter | solution.py:323
  311.6 22.5 %collective-permute-start.19 = (bf16[256,1024]{1,0:T(8,128)(2,1)S(1)}, bf16[256,1024]{1,0:T(8,128)(2,1)S(1)}, u32[]{:S(2)}, u32[]{:S(2)}) collective-permute-start(bf16[256,1024]{1,0:T(8,128)(2,1)S(1)} %slice.390), channel_id=1, source_target_pairs={{0,2},{1,3},{2,0},{3,1},{4,6},{5,7},{6,4},{7,5},{8,10},{9,11},{10,... | collective-permute-start | bytes 1572872 | tf_op jit(solution)/shard_map/ppermute | solution.py:222
  313.9 31.4 %collective-permute-start.21 = (bf16[256,1024]{1,0:T(8,128)(2,1)S(1)}, bf16[256,1024]{1,0:T(8,128)(2,1)S(1)}, u32[]{:S(2)}, u32[]{:S(2)}) collective-permute-start(bf16[256,1024]{1,0:T(8,128)(2,1)S(1)} %slice.389), channel_id=1, source_target_pairs={{0,2},{1,3},{2,0},{3,1},{4,6},{5,7},{6,4},{7,5},{8,10},{9,11},{10,... | collective-permute-start | bytes 1572872 | tf_op jit(solution)/shard_map/ppermute | solution.py:222
  317.1 39.4 %collective-permute-start.9 = (bf16[256,1024]{1,0:T(8,128)(2,1)S(1)}, bf16[256,1024]{1,0:T(8,128)(2,1)S(1)}, u32[]{:S(2)}, u32[]{:S(2)}) collective-permute-start(bf16[256,1024]{1,0:T(8,128)(2,1)S(1)} %slice.392), channel_id=1, source_target_pairs={{0,2},{1,3},{2,0},{3,1},{4,6},{5,7},{6,4},{7,5},{8,10},{9,11},{10,... | collective-permute-start | bytes 1572872 | tf_op jit(solution)/shard_map/ppermute | solution.py:222
  325.1 42.7 %collective-permute-start.28 = (bf16[256,1024]{1,0:T(8,128)(2,1)S(1)}, bf16[256,1024]{1,0:T(8,128)(2,1)S(1)}, u32[]{:S(2)}, u32[]{:S(2)}) collective-permute-start(bf16[256,1024]{1,0:T(8,128)(2,1)S(1)} %get-tuple-element.131), channel_id=1, source_target_pairs={{0,2},{1,3},{2,0},{3,1},{4,6},{5,7},{6,4},{7,5},{8,10},{9,11},{10,... | collective-permute-start | bytes 1572872 | tf_op jit(solution)/shard_map/ppermute | solution.py:222
  372.9 135.2 %reduce-scatter.7.cloned.1.call-start = ((), (), s32[]{:S(2)}) async-start(), calls=%async_computation.12 | async-start | bytes 589824 | tf_op jit(solution)/shard_map/reduce_scatter | solution.py:323
  381.0 30.0 %collective-permute-start.23 = (bf16[512,1024]{1,0:T(8,128)(2,1)}, bf16[512,1024]{1,0:T(8,128)(2,1)}, u32[]{:S(2)}, u32[]{:S(2)}) collective-permute-start(bf16[512,1024]{1,0:T(8,128)(2,1)} %pad_maximum_fusion.16), channel_id=1, source_target_pairs={{0,1},{1,0},{2,3},{3,2},{4,5},{5,4},{6,7},{7,6},{8,9},{9,8},{10,11... | collective-permute-start | bytes 3145736 | tf_op jit(solution)/shard_map/ppermute | solution.py:222
  409.2 50.1 %collective-permute-start.30 = (bf16[512,1024]{1,0:T(8,128)(2,1)}, bf16[512,1024]{1,0:T(8,128)(2,1)}, u32[]{:S(2)}, u32[]{:S(2)}) collective-permute-start(bf16[512,1024]{1,0:T(8,128)(2,1)} %slice.275), channel_id=1, source_target_pairs={{0,1},{1,0},{2,3},{3,2},{4,5},{5,4},{6,7},{7,6},{8,9},{9,8},{10,11... | collective-permute-start | bytes 3145736 | tf_op jit(solution)/shard_map/ppermute | solution.py:222
  443.0 26.1 %collective-permute-start.24 = (bf16[512,1024]{1,0:T(8,128)(2,1)}, bf16[512,1024]{1,0:T(8,128)(2,1)}, u32[]{:S(2)}, u32[]{:S(2)}) collective-permute-start(bf16[512,1024]{1,0:T(8,128)(2,1)} %slice.269), channel_id=1, source_target_pairs={{0,1},{1,0},{2,3},{3,2},{4,5},{5,4},{6,7},{7,6},{8,9},{9,8},{10,11... | collective-permute-start | bytes 3145736 | tf_op jit(solution)/shard_map/ppermute | solution.py:222
  448.4 128.5 %reduce-scatter.5.cloned.1.call-start = ((), (), s32[]{:S(2)}) async-start(), calls=%async_computation.11 | async-start | bytes 1769472 | tf_op jit(solution)/shard_map/reduce_scatter | solution.py:323
  463.4 46.2 %collective-permute-start.31 = (bf16[256,1024]{1,0:T(8,128)(2,1)}, bf16[256,1024]{1,0:T(8,128)(2,1)}, u32[]{:S(2)}, u32[]{:S(2)}) collective-permute-start(bf16[256,1024]{1,0:T(8,128)(2,1)} %slice.386), channel_id=1, source_target_pairs={{0,2},{1,3},{2,0},{3,1},{4,6},{5,7},{6,4},{7,5},{8,10},{9,11},{10,... | collective-permute-start | bytes 1572872 | tf_op jit(solution)/shard_map/ppermute | solution.py:222
  473.4 38.5 %collective-permute-start.25 = (bf16[256,1024]{1,0:T(8,128)(2,1)}, bf16[256,1024]{1,0:T(8,128)(2,1)S(1)}, u32[]{:S(2)}, u32[]{:S(2)}) collective-permute-start(bf16[256,1024]{1,0:T(8,128)(2,1)} %slice.388), channel_id=1, source_target_pairs={{0,2},{1,3},{2,0},{3,1},{4,6},{5,7},{6,4},{7,5},{8,10},{9,11},{10,... | collective-permute-start | bytes 1572872 | tf_op jit(solution)/shard_map/ppermute | solution.py:222
  (114 other events, 1767.0 us)
Sparse Core Ops, SparseCore 0:
  10.7 47.9 all-gather.2
  61.5 86.4 all-gather.4
  301.3 66.9 reduce-scatter.8
  373.0 66.9 reduce-scatter.10
  448.5 59.5 reduce-scatter.6
  511.8 65.0 reduce-scatter.4

commit v2 on v1

v2 whole, which is shorter than its diff:
```python
import functools

import jax
import jax.numpy as jnp
from jax import lax
from jax.experimental import pallas as pl
from jax.experimental.pallas import tpu as pltpu
from jax.sharding import PartitionSpec as P

HEAD_DIM = 64
F32 = jnp.float32
BF16 = jnp.bfloat16
LOG2E = 1.4426950408889634
GELU_C = 0.7978845608028654
GELU_A = 0.044715
NN = (((1,), (0,)), ((), ()))
NT = (((1,), (1,)), ((), ()))
TN = (((0,), (0,)), ((), ()))
SMALL_COST = pl.CostEstimate(flops=1000, bytes_accessed=1000, transcendentals=0)
VMEM_BYTES = 56 * 1024 * 1024


def dot(left, right, dims=NN):
    return lax.dot_general(left, right, dims, preferred_element_type=F32)


def params(*kinds):
    return pltpu.CompilerParams(dimension_semantics=kinds, vmem_limit_bytes=VMEM_BYTES)


def attend_kernel(chunk, q_ref, k_ref, v_ref, out_ref, lse_ref):
    length, width = q_ref.shape
    factor = HEAD_DIM ** (-0.5) * LOG2E
    values_t = v_ref[...].astype(F32).T.astype(BF16)
    keys = [k_ref[:, lo : lo + HEAD_DIM] for lo in range(0, width, HEAD_DIM)]

    def body(step, carry):
        rows = pl.ds(pl.multiple_of(step * chunk, chunk), chunk)
        outs = []
        for head, key in enumerate(keys):
            lo = head * HEAD_DIM
            scores = dot(key, q_ref[rows, lo : lo + HEAD_DIM], NT)
            top = jnp.max(scores, 0, keepdims=True)
            weights = jnp.exp2((scores - top) * factor)
            total = jnp.sum(weights, 0, keepdims=True)
            out_t = dot(values_t[lo : lo + HEAD_DIM], weights.astype(BF16))
            outs.append(out_t / total)
            lse_ref[0, head : head + 1, rows] = top * factor + jnp.log(total) * LOG2E
        out_ref[rows, :] = jnp.concatenate(outs, 0).T.astype(BF16)
        return carry

    lax.fori_loop(0, length // chunk, body, 0)


def attend(qkv):
    length, three = qkv.shape
    width = three // 3
    pairs = width // 128
    chunk = min(256, length)
    spec = lambda part: pl.BlockSpec((length, 128), lambda i: (0, part * pairs + i))
    return pl.pallas_call(
        functools.partial(attend_kernel, chunk),
        grid=(pairs,),
        in_specs=[spec(0), spec(1), spec(2)],
        out_specs=[
            pl.BlockSpec((length, 128), lambda i: (0, i)),
            pl.BlockSpec((1, 8, length), lambda i: (i, 0, 0)),
        ],
        out_shape=[
            jax.ShapeDtypeStruct((length, width), BF16),
            jax.ShapeDtypeStruct((pairs, 8, length), F32),
        ],
        compiler_params=params("arbitrary"),
        cost_estimate=SMALL_COST,
        name="attend",
    )(qkv, qkv, qkv)


def attend_back_kernel(chunk, q_ref, k_ref, v_ref, g_ref, lse_ref, out_ref, dk_ref, dv_ref):
    length, width = q_ref.shape
    total_width = out_ref.shape[1] // 3
    scale = HEAD_DIM ** (-0.5)
    factor = scale * LOG2E
    pair = pl.program_id(0)
    keys_t = k_ref[...].astype(F32).T.astype(BF16)
    heads = range(0, width, HEAD_DIM)
    keys = [k_ref[:, lo : lo + HEAD_DIM] for lo in heads]
    values = [v_ref[:, lo : lo + HEAD_DIM] for lo in heads]
    dk_ref[...] = jnp.zeros_like(dk_ref)
    dv_ref[...] = jnp.zeros_like(dv_ref)

    def columns(part):
        return pl.ds(pl.multiple_of(part * total_width + pair * width, width), width)

    def body(step, carry):
        rows = pl.ds(pl.multiple_of(step * chunk, chunk), chunk)
        outs = []
        for head, (key, value) in enumerate(zip(keys, values)):
            lo = head * HEAD_DIM
            query = q_ref[rows, lo : lo + HEAD_DIM]
            grad = g_ref[rows, lo : lo + HEAD_DIM]
            probs = jnp.exp2(dot(key, query, NT) * factor - lse_ref[0, head : head + 1, rows])
            dv_ref[head] += dot(probs.astype(BF16), grad)
            weighted = probs * dot(value, grad, NT)
            row_dot = jnp.sum(weighted, 0, keepdims=True)
            g_scores = (weighted - probs * row_dot).astype(BF16)
            dk_ref[head] += dot(g_scores, query)
            outs.append(dot(keys_t[lo : lo + HEAD_DIM], g_scores) * scale)
        out_ref[rows, columns(0)] = jnp.concatenate(outs, 0).T.astype(BF16)
        return carry

    lax.fori_loop(0, length // chunk, body, 0)
    n_heads = len(keys)
    out_ref[:, columns(1)] = (
        jnp.concatenate([dk_ref[h] for h in range(n_heads)], 1) * scale
    ).astype(BF16)
    out_ref[:, columns(2)] = jnp.concatenate([dv_ref[h] for h in range(n_heads)], 1).astype(BF16)


def attend_back(qkv, grad_att, lse):
    length, three = qkv.shape
    width = three // 3
    pairs = width // 128
    chunk = min(256, length)
    spec = lambda part: pl.BlockSpec((length, 128), lambda i: (0, part * pairs + i))
    return pl.pallas_call(
        functools.partial(attend_back_kernel, chunk),
        grid=(pairs,),
        in_specs=[
            spec(0),
            spec(1),
            spec(2),
            pl.BlockSpec((length, 128), lambda i: (0, i)),
            pl.BlockSpec((1, 8, length), lambda i: (i, 0, 0)),
        ],
        out_specs=pl.BlockSpec((length, three), lambda i: (0, 0)),
        out_shape=jax.ShapeDtypeStruct((length, three), BF16),
        scratch_shapes=[
            pltpu.VMEM((128 // HEAD_DIM, length, HEAD_DIM), F32),
            pltpu.VMEM((128 // HEAD_DIM, length, HEAD_DIM), F32),
        ],
        compiler_params=params("arbitrary"),
        cost_estimate=SMALL_COST,
        name="attend_back",
    )(qkv, qkv, qkv, grad_att, lse)


def norm_parts(values):
    centered = values - jnp.mean(values, -1, keepdims=True)
    scale = lax.rsqrt(jnp.mean(centered * centered, -1, keepdims=True) + 1e-06)
    return centered * scale, scale


def norm_back(normed, scale, grad):
    mean_g = jnp.mean(grad, -1, keepdims=True)
    mean_gn = jnp.mean(grad * normed, -1, keepdims=True)
    return scale * (grad - mean_g - normed * mean_gn)


def row(ref, index):
    return ref[index : index + 1, :]


def add_sums(ref, values):
    @pl.when(pl.program_id(0) == 0)
    def _():
        ref[...] = jnp.zeros_like(ref)

    for index, value in enumerate(values):
        ref[index : index + 1, :] += jnp.sum(value, 0, keepdims=True)


def total_of(near_ref, core_ref, chip_ref):
    near = near_ref[...].astype(F32) + core_ref[...].astype(F32)
    return near + chip_ref[...].astype(F32)


def middle_kernel(near, core, chip, x_ref, mod_ref, bias_ref, branch_ref, mid_ref, out_ref):
    branch = total_of(near, core, chip) + bias_ref[...].astype(F32)
    mid = x_ref[...].astype(F32) + row(mod_ref, 2) * branch
    normed, _ = norm_parts(mid)
    branch_ref[...] = branch
    mid_ref[...] = mid
    out_ref[...] = (normed * (1.0 + row(mod_ref, 4)) + row(mod_ref, 3)).astype(BF16)


def middle_back_kernel(
    near, core, chip, mid_ref, g_ref, branch_ref, mod_ref, gmid_ref, ga_ref, sums_ref
):
    g_sm = total_of(near, core, chip)
    normed, scale = norm_parts(mid_ref[...])
    g_mid = g_ref[...].astype(F32) + norm_back(normed, scale, g_sm * (1.0 + row(mod_ref, 4)))
    g_a = (g_mid * row(mod_ref, 2)).astype(BF16)
    gmid_ref[...] = g_mid
    ga_ref[...] = g_a
    add_sums(sums_ref, [g_sm, g_sm * normed, g_mid * branch_ref[...], g_a.astype(F32)])


def last_kernel(near, core, chip, x_ref, gmid_ref, mod_ref, out_ref, sums_ref):
    g_sa = total_of(near, core, chip)
    normed, scale = norm_parts(x_ref[...].astype(F32))
    out_ref[...] = gmid_ref[...] + norm_back(normed, scale, g_sa * (1.0 + row(mod_ref, 1)))
    add_sums(sums_ref, [g_sa, g_sa * normed])


def result_kernel(near, core, chip, mid_ref, g_ref, mod_ref, bias_ref, out_ref, sums_ref):
    branch = total_of(near, core, chip) + bias_ref[...].astype(F32)
    grad = g_ref[...].astype(F32)
    out_ref[...] = (mid_ref[...] + row(mod_ref, 5) * branch).astype(BF16)
    g_m = (grad * row(mod_ref, 5)).astype(BF16).astype(F32)
    add_sums(sums_ref, [grad * branch, g_m])


def by_rows(kernel, name, tall, wide, outs, sums):
    count, width = tall[-1].shape
    tile = min(128, count)
    tiled = pl.BlockSpec((tile, width), lambda i: (i, 0))
    out_specs = [tiled] * len(outs)
    out_shape = [jax.ShapeDtypeStruct((count, width), t) for t in outs]
    if sums:
        out_specs.append(pl.BlockSpec((8, width), lambda i: (0, 0)))
        out_shape.append(jax.ShapeDtypeStruct((8, width), F32))
    return pl.pallas_call(
        kernel,
        grid=(count // tile,),
        in_specs=[tiled] * len(tall) + [pl.BlockSpec(w.shape, lambda i: (0, 0)) for w in wide],
        out_specs=out_specs,
        out_shape=out_shape,
        compiler_params=params("arbitrary"),
        cost_estimate=SMALL_COST,
        name=name,
    )(*tall, *wide)


def two_parts(tile, width):
    return [
        pl.BlockSpec((tile, width), lambda i: (jnp.minimum(i, 1), 0)),
        pl.BlockSpec((tile, width), lambda i: (jnp.maximum(i - 2, 0), 0)),
    ]


def pick(first_ref, second_ref):
    return jnp.where(pl.program_id(0) < 2, first_ref[...], second_ref[...])


def put(first_ref, second_ref, value):
    @pl.when(pl.program_id(0) < 2)
    def _():
        first_ref[...] = value

    @pl.when(pl.program_id(0) >= 2)
    def _():
        second_ref[...] = value


def norm_project_kernel(xa_ref, xb_ref, mod_ref, w_ref, bias_ref, shifted_ref, out_ref):
    normed, _ = norm_parts(pick(xa_ref, xb_ref).astype(F32))
    shifted = (normed * (1.0 + row(mod_ref, 1)) + row(mod_ref, 0)).astype(BF16)
    shifted_ref[...] = shifted
    out_ref[...] = (dot(shifted, w_ref[...]) + bias_ref[...].astype(F32)).astype(BF16)


def norm_project(pieces, mod, weight, bias):
    count, width = pieces[0].shape
    tokens, tile = 2 * count, count // 2
    outs = bias.shape[1]
    whole = lambda r, c: pl.BlockSpec((r, c), lambda i: (0, 0))
    return pl.pallas_call(
        norm_project_kernel,
        grid=(4,),
        in_specs=two_parts(tile, width) + [whole(*mod.shape), whole(width, outs), whole(1, outs)],
        out_specs=[pl.BlockSpec((tile, c), lambda i: (i, 0)) for c in (width, outs)],
        out_shape=[jax.ShapeDtypeStruct((tokens, c), BF16) for c in (width, outs)],
        compiler_params=params("arbitrary"),
        cost_estimate=SMALL_COST,
        name="norm_project",
    )(*pieces, mod, weight, bias)


def row_sums_kernel(pa_ref, pb_ref, xa_ref, xb_ref, sums_ref):
    part = pick(pa_ref, pb_ref).astype(F32)
    normed, _ = norm_parts(pick(xa_ref, xb_ref).astype(F32))
    add_sums(sums_ref, [part, part * normed])


def row_sums(parts, rows):
    count, width = parts[0].shape
    tile = count // 2
    return pl.pallas_call(
        row_sums_kernel,
        grid=(4,),
        in_specs=two_parts(tile, width) + two_parts(tile, width),
        out_specs=pl.BlockSpec((8, width), lambda i: (0, 0)),
        out_shape=jax.ShapeDtypeStruct((8, width), F32),
        compiler_params=params("arbitrary"),
        cost_estimate=SMALL_COST,
        name="row_sums",
    )(*parts, *rows)


def project(x, weight):
    half = x.shape[0] // 2
    far = dot(x[half:], weight, NT).astype(BF16)
    return dot(x[:half], weight, NT).astype(BF16), far


def weight_grad_kernel(n_jobs, *refs):
    out_ref = refs[-1]
    for job in range(n_jobs):
        left_a, left_b, right_a, right_b = refs[4 * job : 4 * job + 4]

        @pl.when(pl.program_id(0) == job)
        def _():
            total = dot(left_a[...], right_a[...], TN) + dot(left_b[...], right_b[...], TN)
            out_ref[...] = total.astype(BF16)


def weight_grad(*jobs):
    tokens, rows = jobs[0][0][0].shape
    width = jobs[0][1][0].shape[1]
    tile = min(256, rows)
    steps = rows // tile

    def left_spec(job):
        def index(j, i):
            return 0, jnp.where(j == job, i, jnp.where(j < job, 0, steps - 1))

        return pl.BlockSpec((tokens, tile), index)

    in_specs, operands = [], []
    for job, (lefts, rights) in enumerate(jobs):
        in_specs += [left_spec(job)] * 2
        in_specs += [pl.BlockSpec((tokens, width), lambda j, i: (0, 0))] * 2
        operands += list(lefts) + list(rights)
    return pl.pallas_call(
        functools.partial(weight_grad_kernel, len(jobs)),
        grid=(len(jobs), steps),
        in_specs=in_specs,
        out_specs=pl.BlockSpec((tile, width), lambda j, i: (i, j)),
        out_shape=jax.ShapeDtypeStruct((rows, len(jobs) * width), BF16),
        compiler_params=params("arbitrary", "arbitrary"),
        cost_estimate=SMALL_COST,
        name="weight_grad",
    )(*operands)


def mlp_kernel(
    xa_ref, xb_ref, ga_ref, gb_ref, mod_ref, up_ref, down_ref, bias_ref,
    x_out, g_out, hid_ref, gpre_ref, near_ref, far_ref, gnear_ref, gfar_ref, gbias_ref,
):
    x = pick(xa_ref, xb_ref)
    grad = (pick(ga_ref, gb_ref).astype(F32) * row(mod_ref, 5)).astype(BF16)
    x_out[...] = x
    g_out[...] = grad
    pre = dot(x, up_ref[...]) + bias_ref[...].astype(F32)
    square = pre * pre
    th = jnp.tanh(GELU_C * pre * (1.0 + GELU_A * square))
    half = 0.5 * (1.0 + th)
    hidden = (pre * half).astype(BF16)
    slope = half + (0.5 * GELU_C) * pre * (1.0 - th * th) * (1.0 + 3.0 * GELU_A * square)
    g_pre = (dot(grad, down_ref[...]) * slope).astype(BF16)
    hid_ref[...] = hidden
    gpre_ref[...] = g_pre
    put(gnear_ref, gfar_ref, dot(g_pre, up_ref[...], NT).astype(BF16))
    put(near_ref, far_ref, dot(hidden, down_ref[...], NT).astype(BF16))
    add_sums(gbias_ref, [g_pre.astype(F32)])


def mlp(x_pieces, g_pieces, mod, weights, bias):
    count, width = x_pieces[0].shape
    tokens, tile = 2 * count, count // 2
    hidden = bias.shape[1]
    rows = lambda cols: pl.BlockSpec((tile, cols), lambda i: (i, 0))
    whole = lambda r, c: pl.BlockSpec((r, c), lambda i: (0, 0))
    return pl.pallas_call(
        mlp_kernel,
        grid=(4,),
        in_specs=two_parts(tile, width)
        + two_parts(tile, width)
        + [
            whole(*mod.shape),
            pl.BlockSpec((width, hidden), lambda i: (0, 0)),
            pl.BlockSpec((width, hidden), lambda i: (0, 1)),
            whole(1, hidden),
        ],
        out_specs=[rows(width), rows(width), rows(hidden), rows(hidden)]
        + two_parts(tile, width)
        + two_parts(tile, width)
        + [whole(8, hidden)],
        out_shape=[
            jax.ShapeDtypeStruct((tokens, width), BF16),
            jax.ShapeDtypeStruct((tokens, width), BF16),
            jax.ShapeDtypeStruct((tokens, hidden), BF16),
            jax.ShapeDtypeStruct((tokens, hidden), BF16),
        ]
        + [jax.ShapeDtypeStruct((count, width), BF16)] * 4
        + [jax.ShapeDtypeStruct((8, hidden), F32)],
        compiler_params=params("arbitrary"),
        cost_estimate=SMALL_COST,
        name="feed_forward",
    )(*x_pieces, *g_pieces, mod, weights, weights, bias)


def swap(value, bit):
    n = lax.axis_size("tensor")
    return lax.ppermute(value, "tensor", [(i, i ^ bit) for i in range(n)])


def joined(*values):
    return lax.optimization_barrier(values)


def after(value, token):
    return lax.optimization_barrier((value, token))[0]


def with_core(near, core):
    count = near.shape[0] // 2
    return (near[count:].astype(F32) + core[count:].astype(F32)).astype(BF16)


def exchange(value):
    return lax.all_to_all(value, "dp", 0, 0, tiled=True).reshape(value.shape)


def per_device(
    latents,
    conditioning,
    mod_weight,
    mod_bias,
    qkv_weight,
    qkv_bias,
    proj_weight,
    proj_bias,
    expand_weight,
    expand_bias,
    reduce_weight,
    reduce_bias,
    out_grad,
):
    n_tensor = lax.axis_size("tensor")
    n_dp = lax.axis_size("dp")
    row_count, images, model_width = latents.shape
    local_width = qkv_weight.shape[2]
    hidden_width = expand_weight.shape[1]
    mod_rows = mod_weight.shape[0]
    both = range(images)

    attn_full = lax.all_gather(
        jnp.concatenate([qkv_weight.reshape(mod_rows, 3 * local_width), proj_weight], 1),
        "dp",
        axis=0,
        tiled=True,
    )
    qkv_full, proj_full = attn_full[:, : 3 * local_width], attn_full[:, 3 * local_width :]
    x = [latents[:, i] for i in both]
    grad_y = [out_grad[:, i] for i in both]
    recv_x0 = swap(x[0], 2)

    cond_float = conditioning.astype(F32)
    cond_low = jax.nn.silu(cond_float).astype(BF16)
    cond_cols = exchange(
        cond_low.reshape(images, n_dp, mod_rows).transpose(1, 0, 2)
    ).reshape(n_dp * images, mod_rows)
    mod_part = jnp.einsum("gd,dke->gke", cond_cols, mod_weight, preferred_element_type=F32)
    mod_part, recv_x0 = joined(mod_part, recv_x0)
    recv_x1 = swap(after(x[1], recv_x0), 2)
    mod_recv = exchange(mod_part.reshape(n_dp, images, 6, model_width))
    pair_x0 = jnp.concatenate([x[0], recv_x0])
    core_x0 = swap(pair_x0, 1)
    mod_recv, core_x0, recv_x1 = joined(mod_recv, core_x0, recv_x1)
    recv_g = swap(after(out_grad, recv_x1), 2)
    pair_x = [pair_x0, jnp.concatenate([x[1], recv_x1])]
    core_x1 = swap(pair_x[1], 1)
    modulation = jnp.sum(mod_recv, 0) + mod_bias.astype(F32)[None]
    mod = [modulation[i] for i in both]

    ff_full = lax.all_gather(
        after(jnp.concatenate([expand_weight, reduce_weight], 1), modulation),
        "dp",
        axis=0,
        tiled=True,
    )

    bias_qkv = qkv_bias.reshape(1, 3 * local_width)
    bias_row = proj_bias.reshape(1, model_width)
    bias_out = reduce_bias.reshape(1, model_width)
    bias_hidden = expand_bias.reshape(1, hidden_width)

    def middle(i, pieces):
        return by_rows(
            middle_kernel,
            "middle",
            list(pieces) + [x[i]],
            [mod[i], bias_row],
            [F32, F32, BF16],
            False,
        )

    sh0, qkv0 = norm_project((pair_x[0], core_x0), mod[0], attn_full, bias_qkv)
    att0, lse0 = attend(qkv0)
    att0, recv_g, core_x1 = joined(att0, recv_g, core_x1)
    near0, far0 = project(att0, proj_full)
    core0 = swap(far0, 1)
    sh1, qkv1 = norm_project((after(pair_x[1], near0), core_x1), mod[1], attn_full, bias_qkv)
    qkv1, core0 = joined(qkv1, core0)
    chip0 = with_core(near0, core0)
    recv0 = swap(chip0, 2)
    pair_g = [jnp.concatenate([grad_y[i], recv_g[:, i]]) for i in both]
    core_g = [swap(v, 1) for v in pair_g]
    att1, lse1 = attend(after(qkv1, (chip0, pair_g)))
    att1, recv0, core_g = joined(att1, recv0, core_g)
    branch0, mid0, low0 = middle(0, (near0, core0, recv0))
    recv_m0 = swap(low0, 2)
    near1, far1 = project(after(att1, low0), proj_full)
    core1 = swap(far1, 1)
    recv1 = swap(with_core(near1, core1), 2)
    recv1, recv_m0 = joined(recv1, recv_m0)
    pair_m0 = jnp.concatenate([low0, recv_m0])
    core_m0 = swap(pair_m0, 1)
    branch1, mid1, low1 = middle(1, (near1, core1, recv1))
    low1, core_m0 = joined(low1, core_m0)
    recv_m1 = swap(low1, 2)
    shifted_a, attended, lse = [sh0, sh1], [att0, att1], [lse0, lse1]
    branch_a, mid = [branch0, branch1], [mid0, mid1]

    def feed(i, pieces):
        return mlp(pieces, (pair_g[i], core_g[i]), mod[i], ff_full, bias_hidden)

    ff0 = feed(0, (after(pair_m0, low1), core_m0))
    ff0, recv_m1 = joined(ff0, recv_m1)
    core0 = swap(ff0[7], 1)
    pair_m1 = jnp.concatenate([low1, recv_m1])
    core_m1 = swap(pair_m1, 1)
    chip0 = with_core(ff0[6], core0)
    recv0 = swap(chip0, 2)
    ff1 = feed(1, after((pair_m1, core_m1), chip0))
    ff1, recv0 = joined(ff1, recv0)
    ff = [ff0, ff1]

    def middle_back(i, pieces):
        return by_rows(
            middle_back_kernel,
            "middle_back",
            list(pieces) + [mid[i], grad_y[i], branch_a[i]],
            [mod[i]],
            [F32, BF16],
            True,
        )

    core1 = swap(ff1[7], 1)
    gmid0, ga0, sums_m0 = middle_back(0, (ff0[6], core0, recv0))
    ga0, core1 = joined(ga0, core1)
    recv_ga0 = swap(ga0, 2)
    chip1 = with_core(ff1[6], core1)
    recv1 = swap(chip1, 2)
    core_b = [swap(after(f[5], ga0), 1) for f in ff]
    x_parts, g_parts = after(([f[0] for f in ff], [f[1] for f in ff]), (ga0, chip1))
    g_ff = weight_grad((x_parts, [f[3] for f in ff]), (g_parts, [f[2] for f in ff]))
    g_ff, recv_ga0, recv1, core_b = joined(g_ff, recv_ga0, recv1, core_b)
    g_ff_w = lax.psum_scatter(g_ff, "dp", scatter_dimension=0, tiled=True).astype(F32)
    g_expand_w, g_reduce_w = g_ff_w[:, :hidden_width], g_ff_w[:, hidden_width:]
    pair_ga0 = jnp.concatenate([ga0, recv_ga0])
    core_ga0 = swap(pair_ga0, 1)
    gmid1, ga1, sums_m1 = middle_back(1, (ff1[6], core1, recv1))
    ga1, core_ga0 = joined(ga1, core_ga0)
    recv_ga1 = swap(ga1, 2)
    full_ga0 = jnp.concatenate([after(pair_ga0, ga1), core_ga0])
    grad_mid, grad_a, sums_m = [gmid0, gmid1], [ga0, ga1], [sums_m0, sums_m1]

    def finish(i, pieces):
        return by_rows(
            result_kernel,
            "result",
            list(pieces) + [mid[i], grad_y[i]],
            [mod[i], bias_out],
            [BF16],
            True,
        )

    chip_b = [with_core(ff[i][4], core_b[i]) for i in both]
    recv_b0 = swap(after(chip_b[0], ga1), 2)
    gatt0 = dot(full_ga0, proj_full).astype(BF16)
    gqkv0 = attend_back(qkv0, after(gatt0, chip_b), lse0)
    gqkv0, recv_ga1, recv_b0 = joined(gqkv0, recv_ga1, recv_b0)
    pair_ga1 = jnp.concatenate([ga1, recv_ga1])
    core_ga1 = swap(pair_ga1, 1)
    near0, far0 = project(gqkv0, qkv_full)
    near0, far0, core_ga1 = joined(near0, far0, core_ga1)
    core0 = swap(far0, 1)
    full_ga = [full_ga0, jnp.concatenate([pair_ga1, core_ga1])]
    g_proj = weight_grad((after(full_ga, far0), attended))
    res0, sums_r0 = finish(0, (ff0[4], core_b[0], after(recv_b0, far0)))
    g_proj, res0, core0 = joined(g_proj, res0, core0)
    chip0 = with_core(near0, core0)
    recv0 = swap(chip0, 2)
    recv_b1 = swap(after(chip_b[1], chip0), 2)
    gatt1 = dot(after(full_ga[1], chip0), proj_full).astype(BF16)
    pieces_p = exchange(g_proj.reshape(n_dp, -1, local_width))
    gqkv1 = attend_back(qkv1, after(gatt1, chip0), lse1)
    gqkv1, recv0, recv_b1, pieces_p = joined(gqkv1, recv0, recv_b1, pieces_p)
    g_proj_w = jnp.sum(pieces_p.astype(F32), 0)
    grad_qkv = [gqkv0, gqkv1]
    g_qkv = weight_grad((shifted_a, grad_qkv))
    g_qkv_w = lax.psum_scatter(g_qkv, "dp", scatter_dimension=0, tiled=True)
    near1, far1 = project(after(gqkv1, g_qkv), qkv_full)
    core1 = swap(far1, 1)
    sums_p1 = row_sums(after((near1, far1), g_ff_w), (pair_x[1], core_x1))
    sums_p1, core1 = joined(sums_p1, core1)

    def last(i, pieces):
        return by_rows(
            last_kernel, "last", list(pieces) + [x[i], grad_mid[i]], [mod[i]], [F32], True
        )

    lat0, sums_a0 = last(0, (near0, core0, after(recv0, sums_p1)))
    res1, sums_r1 = finish(1, (ff1[4], core_b[1], after(recv_b1, sums_p1)))
    sums_a, sums_r = [sums_a0, sums_p1], [sums_r0, sums_r1]

    shared = jnp.concatenate(
        [jnp.concatenate([sums_a[i][:2], sums_m[i][2:3], sums_m[i][:2], sums_r[i][:1]]) for i in both]
        + [sum(s[3:4] for s in sums_m), sum(s[1:2] for s in sums_r)]
    )
    shared = shared + swap(shared, 1)
    chip1 = with_core(near1, core1)
    recv1 = swap(after(chip1, shared), 2)
    shared = shared + swap(shared, 2)
    local = jnp.concatenate(
        [
            sum(jnp.sum(v.astype(F32), 0) for v in grad_qkv),
            sum(f[8][0] for f in ff),
        ]
    )
    n_mod = images * 6 * model_width
    shared = shared.reshape(-1)
    local = jnp.concatenate([shared[n_mod:], local])
    high = local.astype(BF16)
    mine = jnp.concatenate(
        [shared[:n_mod].astype(BF16), high, (local - high.astype(F32)).astype(BF16)]
    )
    everyone = exchange(jnp.broadcast_to(mine[None], (n_dp,) + mine.shape)).astype(F32)
    lat1 = last(1, (near1, core1, recv1))[0]
    grad_latent, result = [lat0, lat1], [res0, res1]
    g_mod_all = everyone[:, :n_mod].reshape(n_dp * images, 6, model_width)
    biases = jnp.sum(everyone[:, n_mod:].reshape(n_dp, 2, -1), (0, 1))
    sizes = [model_width, model_width, 3 * local_width, hidden_width]
    cuts = [sum(sizes[:n]) for n in range(len(sizes) + 1)]
    g_proj_b, g_reduce_b, g_qkv_b, g_expand_b = (
        biases[lo:hi] for lo, hi in zip(cuts, cuts[1:])
    )

    g_mod_b = jnp.sum(g_mod_all, 0)
    g_mod_low = g_mod_all.astype(BF16)
    mod_cols = model_width // n_tensor
    own_cols = lax.dynamic_slice_in_dim(
        g_mod_low, lax.axis_index("tensor") * mod_cols, mod_cols, 2
    )
    g_mod_w = jnp.einsum("gd,gke->dke", cond_cols, own_cols, preferred_element_type=F32)
    act_rows = jnp.einsum("gke,dke->gd", g_mod_low, mod_weight, preferred_element_type=F32)
    grad_act = (
        exchange(act_rows.reshape(n_dp, images, mod_rows))
        .transpose(1, 0, 2)
        .reshape(images, n_dp * mod_rows)
    )
    silu_out, silu_pull = jax.vjp(jax.nn.silu, cond_float)
    grad_cond = silu_pull(grad_act)[0]
    g_qkv_w = after(g_qkv_w, (grad_cond, grad_latent, g_mod_w)).astype(F32)
    g_qkv_w = g_qkv_w.reshape(mod_rows, 3, local_width)
    return (
        jnp.stack(result, 1),
        jnp.stack(grad_latent, 1),
        grad_cond,
        g_mod_w,
        g_mod_b,
        g_qkv_w,
        g_qkv_b.reshape(3, local_width),
        g_proj_w,
        g_proj_b,
        g_expand_w,
        g_expand_b,
        g_reduce_w,
        g_reduce_b,
    )


def solution(mesh):
    in_specs = (
        P("tensor", "dp", None),
        P("dp", None),
        P("dp", None, None),
        P(),
        P("dp", None, "tensor"),
        P(None, "tensor"),
        P("dp", "tensor"),
        P(),
        P("dp", "tensor"),
        P("tensor"),
        P("dp", "tensor"),
        P(),
        P("tensor", "dp", None),
    )
    out_specs = (
        P("tensor", "dp", None),
        P("tensor", "dp", None),
        P("dp", None),
        P("dp", None, "tensor"),
        P(),
        P("dp", None, "tensor"),
        P(None, "tensor"),
        P("dp", "tensor"),
        P(),
        P("dp", "tensor"),
        P("tensor"),
        P("dp", "tensor"),
        P(),
    )
    return jax.shard_map(
        per_device, mesh=mesh, in_specs=in_specs, out_specs=out_specs, check_vma=False
    )
```

time: 592 us -> 404 us (0.68)
  waiting for transfers between devices: 263 us -> 60.8 us
  Pallas kernels: 102 us -> 180 us
  matrix products: 56.1 us -> 20.6 us
  other arithmetic: 60.2 us -> 28.2 us
  blocking collectives: 6.15 us -> 12.1 us
    ppermute x34 -> x33, waiting for transfers between devices: 124 us -> 43.3 us  [swap(): return lax.ppermute(value, 'tensor', [(i, i ^ bit) for i in range(n)])]
    pallas_call x2 -> x16, Pallas kernels: 29.1 us -> 107 us  [the longest x2 34 us: mlp(): pl.pallas_call(mlp_kernel, grid=(4,), in_specs=two_parts(tile, width) + t...]
    reduce_scatter x4 -> x2, waiting for transfers between devices: 54.8 us -> 6.81 us  [the longest x1 6.79 us: per_device(): g_qkv_w = lax.psum_scatter(g_qkv, 'dp', scatter_dimension=0, tiled=True)]
    all_gather x2, waiting for transfers between devices: 47.5 us -> 3.61 us  [the longest x1 3.61 us: per_device(): lax.all_gather(jnp.concatenate([qkv_weight.reshape(mod_rows, 3 * local_wi...]
    dot_general x16 -> x10, matrix products: 53.5 us -> 18.6 us  [dot(): return lax.dot_general(left, right, dims, preferred_element_type=F32)]
    all_to_all x5 -> x4, waiting for transfers between devices: 35.9 us -> 7.07 us  [exchange(): return lax.all_to_all(value, 'dp', 0, 0, tiled=True).reshape(value.shape)]
    reduce_sum x14 -> x4, other arithmetic: 14.4 us -> 1.57 us  [the longest x1 0.75 us: per_device(): modulation = jnp.sum(mod_recv, 0) + mod_bias.astype(F32)[None]]
    slice x19 -> x10, local copies, waits for them, and re-layouts: 17.8 us -> 5.65 us  [the longest x1 2.29 us: per_device(): x = [latents[:, i] for i in both]]
  transfers between devices with their start and end apart: 48 -> 41, of which waited for: 22 -> 13; matrix products, arithmetic and copies ran while one was open for 23% -> 18% of each run, Pallas kernels for 15% -> 45%
where the time goes in v2:
time: 404 us; the launch traced here: 398 us
  Pallas kernels  180 us (45%)
  waiting for transfers between devices  60.8 us (15%)
  starting transfers between devices  44.3 us (11%)
  local copies, waits for them, and re-layouts  37.3 us (9%)
  other arithmetic  28.2 us (7%)
  matrix products  20.6 us (5%)
  between operations  15.1 us (4%)
  blocking collectives  12.1 us (3%)
    ppermute x33, waiting for transfers between devices, swap(): return lax.ppermute(value, 'tensor', [(i, i ^ bit) for i in range(n)])  43.3 us
    pallas_call x2, Pallas kernels, attend_back(): pl.pallas_call(functools.partial(attend_back_kernel, chunk), grid=(pairs,...  42.2 us
    pallas_call x2, Pallas kernels, mlp(): pl.pallas_call(mlp_kernel, grid=(4,), in_specs=two_parts(tile, width) + t...  34 us
    pallas_call x2, Pallas kernels, attend(): pl.pallas_call(functools.partial(attend_kernel, chunk), grid=(pairs,), in...  30.5 us
    pallas_call x3, Pallas kernels, weight_grad(): pl.pallas_call(functools.partial(weight_grad_kernel, len(jobs)), grid=(le...  28.7 us
    pallas_call x8, Pallas kernels, by_rows(): pl.pallas_call(kernel, grid=(count // tile,), in_specs=[tiled] * len(tall...  26.6 us
    ppermute x33, starting transfers between devices, swap(): return lax.ppermute(value, 'tensor', [(i, i ^ bit) for i in range(n)])  22.3 us
    all_to_all x4, starting transfers between devices, exchange(): return lax.all_to_all(value, 'dp', 0, 0, tiled=True).reshape(value.shape)  21.6 us
  transfers between devices with their start and end apart: 41, of which 13 were waited for; matrix products, arithmetic and copies ran while one was open for 18% of the time, Pallas kernels for 45%

profile of v2, /device:TPU:0, one launch (start us, length us, event | category | flops | bytes accessed | tf_op | source)
XLA Modules:
  0.0 398.4 jit_solution(4824446108262269151)
XLA Ops:
  15.8 12.1 %all_to_all.26 = bf16[8,2,128]{2,1,0:T(2,128)(2,1)S(1)} all-to-all(bf16[8,2,128]{2,1,0:T(2,128)(2,1)S(1)} %fusion.33), channel_id=1, replica_groups=mesh['dp'=8,'tensor'=4] {'dp'}, dimensions={0} | all-to-all | bytes 8192 | tf_op jit(solution)/shard_map/all_to_all | solution.py:423
  30.2 5.5 %all-to-all-start.1 = ((f32[8,2,6,1024]{3,1,2,0:T(2,128)}), f32[8,2,6,1024]{3,1,2,0:T(2,128)S(1)}, u32[]{:S(2)}, u32[]{:S(2)}) async-start(f32[8,2,6,1024]{3,1,2,0:T(2,128)} %copy.70), calls=%async_computation.1 | async-start | bytes 786432 | tf_op jit(solution)/shard_map/all_to_all | solution.py:423
  40.9 9.3 %collective-permute-done.2 = bf16[256,1024]{1,0:T(8,128)(2,1)} collective-permute-done((bf16[256,1024]{1,0:T(8,128)(2,1)S(1)}, bf16[256,1024]{1,0:T(8,128)(2,1)}, u32[]{:S(2)}, u32[]{:S(2)}) %collective-permute-start.2) | collective-permute-done | bytes 524320 | tf_op jit(solution)/shard_map/ppermute | solution.py:406
  65.5 6.3 %norm_project.2 = (bf16[1024,1024]{1,0:T(8,128)(2,1)}, bf16[1024,768]{1,0:T(8,128)(2,1)}) custom-call(bf16[512,1024]{1,0:T(8,128)(2,1)} %pad_maximum_fusion.1.xa_ref, bf16[512,1024]{1,0:T(8,128)(2,1)} %collective-permute-done.1.xb_ref, f32[6,1024]{1,0:T(8,128)} %get-tuple-element.350.mod_ref, bf16[1024,1024]{1,0:T(8,128)(2,1)} %all-gather.3.cloned.1.call-done.w_ref, ...), custom_call_target="tpu_custom_call" | custom-call | flops 1000 | bytes 1000 | tf_op jit(solution)/shard_map/norm_project/pallas_call | solution.py:268
  71.8 15.3 %attend.2 = (bf16[1024,256]{1,0:T(8,128)(2,1)}, f32[2,8,1024]{2,1,0:T(8,128)}) custom-call(bf16[1024,768]{1,0:T(8,128)(2,1)} %get-tuple-element.156.q_ref.k_ref.v_ref, bf16[1024,768]{1,0:T(8,128)(2,1)} %get-tuple-element.156.q_ref.k_ref.v_ref, bf16[1024,768]{1,0:T(8,128)(2,1)} %get-tuple-element.156.q_ref.k_ref.v_ref), custom_call_target="tpu_custom_call" | custom-call | flops 1000 | bytes 1000 | tf_op jit(solution)/shard_map/attend/pallas_call | solution.py:61
  94.5 6.7 %norm_project.3 = (bf16[1024,1024]{1,0:T(8,128)(2,1)}, bf16[1024,768]{1,0:T(8,128)(2,1)}) custom-call(bf16[512,1024]{1,0:T(8,128)(2,1)} %pad_maximum_fusion.2.xa_ref, bf16[512,1024]{1,0:T(8,128)(2,1)} %collective-permute-done.4.xb_ref, f32[6,1024]{1,0:T(8,128)} %get-tuple-element.349.mod_ref, bf16[1024,1024]{1,0:T(8,128)(2,1)} %all-gather.3.cloned.1.call-done.w_ref, ...), custom_call_target="tpu_custom_call" | custom-call | flops 1000 | bytes 1000 | tf_op jit(solution)/shard_map/norm_project/pallas_call | solution.py:268
  104.7 15.1 %attend.3 = (bf16[1024,256]{1,0:T(8,128)(2,1)}, f32[2,8,1024]{2,1,0:T(8,128)}) custom-call(bf16[1024,768]{1,0:T(8,128)(2,1)} %get-tuple-element.167.q_ref.k_ref.v_ref, bf16[1024,768]{1,0:T(8,128)(2,1)} %get-tuple-element.167.q_ref.k_ref.v_ref, bf16[1024,768]{1,0:T(8,128)(2,1)} %get-tuple-element.167.q_ref.k_ref.v_ref), custom_call_target="tpu_custom_call" | custom-call | flops 1000 | bytes 1000 | tf_op jit(solution)/shard_map/attend/pallas_call | solution.py:61
  127.7 11.7 %collective-permute-done.11 = bf16[256,1024]{1,0:T(8,128)(2,1)S(1)} collective-permute-done((bf16[256,1024]{1,0:T(8,128)(2,1)}, bf16[256,1024]{1,0:T(8,128)(2,1)S(1)}, u32[]{:S(2)}, u32[]{:S(2)}) %collective-permute-start.11) | collective-permute-done | bytes 524320 | tf_op jit(solution)/shard_map/ppermute | solution.py:406
  139.4 10.7 %collective-permute-done.10.chip = bf16[256,1024]{1,0:T(8,128)(2,1)S(1)} collective-permute-done((bf16[256,1024]{1,0:T(8,128)(2,1)S(1)}, bf16[256,1024]{1,0:T(8,128)(2,1)S(1)}, u32[]{:S(2)}, u32[]{:S(2)}) %collective-permute-start.10) | collective-permute-done | bytes 524320 | tf_op jit(solution)/shard_map/ppermute | solution.py:406
  155.8 17.2 %feed_forward.2 = (bf16[1024,1024]{1,0:T(8,128)(2,1)}, bf16[1024,1024]{1,0:T(8,128)(2,1)}, bf16[1024,1024]{1,0:T(8,128)(2,1)}, bf16[1024,1024]{1,0:T(8,128)(2,1)...) custom-call(bf16[512,1024]{1,0:T(8,128)(2,1)} %copy-done.25, ...), custom_call_target="tpu_custom_call" | custom-call | flops 1000 | bytes 1000 | tf_op jit(solution)/shard_map/feed_forward/pallas_call | solution.py:375
  178.8 16.8 %feed_forward.3 = (bf16[1024,1024]{1,0:T(8,128)(2,1)}, bf16[1024,1024]{1,0:T(8,128)(2,1)}, bf16[1024,1024]{1,0:T(8,128)(2,1)}, bf16[1024,1024]{1,0:T(8,128)(2,1)...) custom-call(bf16[512,1024]{1,0:T(8,128)(2,1)} %copy-done.26, ...), custom_call_target="tpu_custom_call" | custom-call | flops 1000 | bytes 1000 | tf_op jit(solution)/shard_map/feed_forward/pallas_call | solution.py:375
  196.5 4.0 middle_back.2
  204.1 16.0 %weight_grad.3 = bf16[1024,2048]{1,0:T(8,128)(2,1)} custom-call(bf16[1024,1024]{1,0:T(8,128)(2,1)} %get-tuple-element.217.refs_0_, bf16[1024,1024]{1,0:T(8,128)(2,1)} %get-tuple-element.218.refs_1_, bf16[1024,1024]{1,0:T(8,128)(2,1)} %get-tuple-element.219.refs_2_, bf16[1024,1024]{1,0:T(8,128)(2,1)} %get-tuple-element.220.refs_3_, ...), custom_call_target="tpu_custom_call" | custom-call | flops 1000 | bytes 1000 | tf_op jit(solution)/shard_map/weight_grad/pallas_call | solution.py:335
  220.1 7.4 %collective-permute-done.18 = bf16[256,1024]{1,0:T(8,128)(2,1)} collective-permute-done((bf16[256,1024]{1,0:T(8,128)(2,1)}, bf16[256,1024]{1,0:T(8,128)(2,1)}, u32[]{:S(2)}, u32[]{:S(2)}) %collective-permute-start.18) | collective-permute-done | bytes 524320 | tf_op jit(solution)/shard_map/ppermute | solution.py:406
  228.8 4.1 %middle_back.3 = (f32[256,1024]{1,0:T(8,128)}, bf16[256,1024]{1,0:T(8,128)(2,1)}, f32[8,1024]{1,0:T(8,128)}) custom-call(bf16[512,1024]{1,0:T(8,128)(2,1)} %get-tuple-element.215.near, bf16[512,1024]{1,0:T(8,128)(2,1)} %copy-done.22, bf16[256,1024]{1,0:T(8,128)(2,1)} %copy-done.41, f32[256,1024]{1,0:T(8,128)} %get-tuple-element.231.mid_ref, ...), custom_call_target="tpu_custom_call" | custom-call | flops 1000 | bytes 1000 | tf_op jit(solution)/shard_map/middle_back/pallas_call | solution.py:223
  239.8 21.2 %attend_back.2.refs_2_ = bf16[1024,768]{1,0:T(8,128)(2,1)} custom-call(bf16[1024,768]{1,0:T(8,128)(2,1)} %get-tuple-element.156.q_ref.k_ref.v_ref, bf16[1024,768]{1,0:T(8,128)(2,1)} %get-tuple-element.156.q_ref.k_ref.v_ref, bf16[1024,768]{1,0:T(8,128)(2,1)} %get-tuple-element.156.q_ref.k_ref.v_ref, bf16[1024,256]{1,0:T(8,128)(2,1)} %convolution_convert_fusion.9.g_ref, ...), custom_call_target="tpu_custom_call" | custom-call | flops 1000 | bytes 1000 | tf_op jit(solution)/shard_map/attend_back/pallas_call | solution.py:126
  271.0 5.1 %weight_grad.4 = bf16[1024,256]{1,0:T(8,128)(2,1)} custom-call(bf16[1024,1024]{1,0:T(8,128)(2,1)} %copy-done.15, bf16[1024,1024]{1,0:T(8,128)(2,1)} %copy-done.20, bf16[1024,256]{1,0:T(8,128)(2,1)} %get-tuple-element.160.refs_2_, bf16[1024,256]{1,0:T(8,128)(2,1)} %get-tuple-element.172.refs_3_), custom_call_target="tpu_custom_call" | custom-call | flops 1000 | bytes 1000 | tf_op jit(solution)/shard_map/weight_grad/pallas_call | solution.py:335
  276.1 4.0 all-to-all-start.2
  287.4 21.0 %attend_back.3.refs_3_ = bf16[1024,768]{1,0:T(8,128)(2,1)} custom-call(bf16[1024,768]{1,0:T(8,128)(2,1)} %get-tuple-element.167.q_ref.k_ref.v_ref, bf16[1024,768]{1,0:T(8,128)(2,1)} %get-tuple-element.167.q_ref.k_ref.v_ref, bf16[1024,768]{1,0:T(8,128)(2,1)} %get-tuple-element.167.q_ref.k_ref.v_ref, bf16[1024,256]{1,0:T(8,128)(2,1)} %convolution_convert_fusion.8.g_ref, ...), custom_call_target="tpu_custom_call" | custom-call | flops 1000 | bytes 1000 | tf_op jit(solution)/shard_map/attend_back/pallas_call | solution.py:126
  309.6 7.6 %weight_grad.5 = bf16[1024,768]{1,0:T(8,128)(2,1)} custom-call(bf16[1024,1024]{1,0:T(8,128)(2,1)} %get-tuple-element.263.refs_0_, bf16[1024,1024]{1,0:T(8,128)(2,1)} %get-tuple-element.264.refs_1_, bf16[1024,768]{1,0:T(8,128)(2,1)} %attend_back.2.refs_2_, bf16[1024,768]{1,0:T(8,128)(2,1)} %attend_back.3.refs_3_), custom_call_target="tpu_custom_call" | custom-call | flops 1000 | bytes 1000 | tf_op jit(solution)/shard_map/weight_grad/pallas_call | solution.py:335
  325.7 5.0 %row_sums.1 = f32[8,1024]{1,0:T(8,128)} custom-call(bf16[512,1024]{1,0:T(8,128)(2,1)} %convolution_convert_fusion.1.pa_ref.near, bf16[512,1024]{1,0:T(8,128)(2,1)} %convolution_convert_fusion.pb_ref, bf16[512,1024]{1,0:T(8,128)(2,1)} %pad_maximum_fusion.2.xa_ref, bf16[512,1024]{1,0:T(8,128)(2,1)} %collective-permute-done.4.xb_ref), custom_call_target="tpu_custom_call" | custom-call | flops 1000 | bytes 1000 | tf_op jit(solution)/shard_map/row_sums/pallas_call | solution.py:289
  349.0 6.2 %all-to-all-start.3 = ((bf16[8,2,9984]{2,1,0:T(2,128)(2,1)}), bf16[8,2,9984]{2,1,0:T(2,128)(2,1)S(1)}, u32[]{:S(2)}, u32[]{:S(2)}) async-start(bf16[8,2,9984]{2,1,0:T(2,128)(2,1)} %reshape.111), calls=%async_computation.4 | async-start | bytes 638976 | tf_op jit(solution)/shard_map/all_to_all | solution.py:423
  369.7 6.0 %all-to-all-start.4 = ((f32[8,2,128]{2,1,0:T(2,128)}), f32[8,2,128]{2,1,0:T(2,128)S(1)}, u32[]{:S(2)}, u32[]{:S(2)}) async-start(f32[8,2,128]{2,1,0:T(2,128)} %copy.81), calls=%async_computation.5 | async-start | bytes 16384 | tf_op jit(solution)/shard_map/all_to_all | solution.py:423
  382.8 6.8 %reduce-scatter.5.cloned.1.call-done = bf16[128,768]{1,0:T(8,128)(2,1)} async-done(((bf16[1024,768]{1,0:T(8,128)(2,1)}), bf16[128,768]{1,0:T(8,128)(2,1)}) %reduce-scatter.5.cloned.1.call-update) | async-done | bytes 196624 | tf_op jit(solution)/shard_map/reduce_scatter | solution.py:605
  (305 shorter events, 142.3 us)
Async XLA Ops:
  7.2 58.3 %all-gather.3.cloned.1.call-start = ((), (), s32[]{:S(2)}) async-start(), calls=%async_computation.7 | async-start | bytes 2359296 | tf_op jit(solution)/shard_map/all_gather | solution.py:449
  29.2 24.7 %collective-permute-start.1 = (bf16[512,1024]{1,0:T(8,128)(2,1)}, bf16[512,1024]{1,0:T(8,128)(2,1)}, u32[]{:S(2)}, u32[]{:S(2)}) collective-permute-start(bf16[512,1024]{1,0:T(8,128)(2,1)} %pad_maximum_fusion.1.xa_ref), channel_id=1, source_target_pairs={{0,1},{1,0},{2,3},{3,2},{4,5},{5,4},{6,7},{7,6},{8,9},{9,8},{10,11... | collective-permute-start | bytes 3145736 | tf_op jit(solution)/shard_map/ppermute | solution.py:406
  30.2 23.7 %all-to-all-start.1 = ((f32[8,2,6,1024]{3,1,2,0:T(2,128)}), f32[8,2,6,1024]{3,1,2,0:T(2,128)S(1)}, u32[]{:S(2)}, u32[]{:S(2)}) async-start(f32[8,2,6,1024]{3,1,2,0:T(2,128)} %copy.70), calls=%async_computation.1 | async-start | bytes 786432 | tf_op jit(solution)/shard_map/all_to_all | solution.py:423
  35.8 120.0 %all-gather.5.cloned.1.call-start = ((), (), s32[]{:S(2)}) async-start(), calls=%async_computation.8 | async-start | bytes 4718592 | tf_op jit(solution)/shard_map/all_gather | solution.py:478
  55.6 270.1 %reduce-scatter.3.cloned.1.call-start = ((), (), s32[]{:S(2)}) async-start(), calls=%async_computation.9 | async-start | bytes 4718592 | tf_op jit(solution)/shard_map/reduce_scatter | solution.py:561
  57.9 29.2 %collective-permute-start.4 = (bf16[512,1024]{1,0:T(8,128)(2,1)}, bf16[512,1024]{1,0:T(8,128)(2,1)}, u32[]{:S(2)}, u32[]{:S(2)}) collective-permute-start(bf16[512,1024]{1,0:T(8,128)(2,1)} %pad_maximum_fusion.2.xa_ref), channel_id=1, source_target_pairs={{0,1},{1,0},{2,3},{3,2},{4,5},{5,4},{6,7},{7,6},{8,9},{9,8},{10,11... | collective-permute-start | bytes 3145736 | tf_op jit(solution)/shard_map/ppermute | solution.py:406
  59.2 28.0 %collective-permute-start.3 = (bf16[256,2,1024]{2,0,1:T(8,128)(2,1)}, bf16[256,2,1024]{2,0,1:T(8,128)(2,1)}, u32[]{:S(2)}, u32[]{:S(2)}) collective-permute-start(bf16[256,2,1024]{2,0,1:T(8,128)(2,1)} %copy.76), channel_id=1, source_target_pairs={{0,2},{1,3},{2,0},{3,1},{4,6},{5,7},{6,4},{7,5},{8,10},{9,11},{10,... | collective-permute-start | bytes 3145736 | tf_op jit(solution)/shard_map/ppermute | solution.py:406
  93.0 26.8 %collective-permute-start.7 = (bf16[512,1024]{1,0:T(8,128)(2,1)S(1)}, bf16[512,1024]{1,0:T(8,128)(2,1)}, u32[]{:S(2)}, u32[]{:S(2)}) collective-permute-start(bf16[512,1024]{1,0:T(8,128)(2,1)S(1)} %pad_maximum_fusion.3.ga_ref), channel_id=1, source_target_pairs={{0,1},{1,0},{2,3},{3,2},{4,5},{5,4},{6,7},{7,6},{8,9},{9,8},{10,11... | collective-permute-start | bytes 3145736 | tf_op jit(solution)/shard_map/ppermute | solution.py:406
  93.6 26.2 %collective-permute-start.8 = (bf16[512,1024]{1,0:T(8,128)(2,1)S(1)}, bf16[512,1024]{1,0:T(8,128)(2,1)}, u32[]{:S(2)}, u32[]{:S(2)}) collective-permute-start(bf16[512,1024]{1,0:T(8,128)(2,1)S(1)} %pad_maximum_fusion.4.ga_ref), channel_id=1, source_target_pairs={{0,1},{1,0},{2,3},{3,2},{4,5},{5,4},{6,7},{7,6},{8,9},{9,8},{10,11... | collective-permute-start | bytes 3145736 | tf_op jit(solution)/shard_map/ppermute | solution.py:406
  102.4 17.4 %collective-permute-start.6 = (bf16[256,1024]{1,0:T(8,128)(2,1)S(1)}, bf16[256,1024]{1,0:T(8,128)(2,1)S(1)}, u32[]{:S(2)}, u32[]{:S(2)}) collective-permute-start(bf16[256,1024]{1,0:T(8,128)(2,1)S(1)} %add_convert_fusion.7), channel_id=1, source_target_pairs={{0,2},{1,3},{2,0},{3,1},{4,6},{5,7},{6,4},{7,5},{8,10},{9,11},{10,... | collective-permute-start | bytes 1572872 | tf_op jit(solution)/shard_map/ppermute | solution.py:406
  127.2 22.9 %collective-permute-start.10 = (bf16[256,1024]{1,0:T(8,128)(2,1)S(1)}, bf16[256,1024]{1,0:T(8,128)(2,1)S(1)}, u32[]{:S(2)}, u32[]{:S(2)}) collective-permute-start(bf16[256,1024]{1,0:T(8,128)(2,1)S(1)} %add_convert_fusion.6), channel_id=1, source_target_pairs={{0,2},{1,3},{2,0},{3,1},{4,6},{5,7},{6,4},{7,5},{8,10},{9,11},{10,... | collective-permute-start | bytes 1572872 | tf_op jit(solution)/shard_map/ppermute | solution.py:406
  154.8 18.2 %collective-permute-start.13 = (bf16[256,1024]{1,0:T(8,128)(2,1)}, bf16[256,1024]{1,0:T(8,128)(2,1)}, u32[]{:S(2)}, u32[]{:S(2)}) collective-permute-start(bf16[256,1024]{1,0:T(8,128)(2,1)} %get-tuple-element.176), channel_id=1, source_target_pairs={{0,2},{1,3},{2,0},{3,1},{4,6},{5,7},{6,4},{7,5},{8,10},{9,11},{10,... | collective-permute-start | bytes 1572872 | tf_op jit(solution)/shard_map/ppermute | solution.py:406
  176.1 19.5 %collective-permute-start.16 = (bf16[256,1024]{1,0:T(8,128)(2,1)S(1)}, bf16[256,1024]{1,0:T(8,128)(2,1)S(1)}, u32[]{:S(2)}, u32[]{:S(2)}) collective-permute-start(bf16[256,1024]{1,0:T(8,128)(2,1)S(1)} %add_convert_fusion.5), channel_id=1, source_target_pairs={{0,2},{1,3},{2,0},{3,1},{4,6},{5,7},{6,4},{7,5},{8,10},{9,11},{10,... | collective-permute-start | bytes 1572872 | tf_op jit(solution)/shard_map/ppermute | solution.py:406
  200.5 27.0 %collective-permute-start.21 = (bf16[512,1024]{1,0:T(8,128)(2,1)}, bf16[512,1024]{1,0:T(8,128)(2,1)}, u32[]{:S(2)}, u32[]{:S(2)}) collective-permute-start(bf16[512,1024]{1,0:T(8,128)(2,1)} %get-tuple-element.228), channel_id=1, source_target_pairs={{0,1},{1,0},{2,3},{3,2},{4,5},{5,4},{6,7},{7,6},{8,9},{9,8},{10,11... | collective-permute-start | bytes 3145736 | tf_op jit(solution)/shard_map/ppermute | solution.py:406
  200.5 27.0 %collective-permute-start.20 = (bf16[512,1024]{1,0:T(8,128)(2,1)}, bf16[512,1024]{1,0:T(8,128)(2,1)}, u32[]{:S(2)}, u32[]{:S(2)}) collective-permute-start(bf16[512,1024]{1,0:T(8,128)(2,1)} %get-tuple-element.226), channel_id=1, source_target_pairs={{0,1},{1,0},{2,3},{3,2},{4,5},{5,4},{6,7},{7,6},{8,9},{9,8},{10,11... | collective-permute-start | bytes 3145736 | tf_op jit(solution)/shard_map/ppermute | solution.py:406
  202.0 18.0 %collective-permute-start.19 = (bf16[256,1024]{1,0:T(8,128)(2,1)}, bf16[256,1024]{1,0:T(8,128)(2,1)S(1)}, u32[]{:S(2)}, u32[]{:S(2)}) collective-permute-start(bf16[256,1024]{1,0:T(8,128)(2,1)} %add_convert_fusion.4), channel_id=1, source_target_pairs={{0,2},{1,3},{2,0},{3,1},{4,6},{5,7},{6,4},{7,5},{8,10},{9,11},{10,... | collective-permute-start | bytes 1572872 | tf_op jit(solution)/shard_map/ppermute | solution.py:406
  203.1 24.4 %collective-permute-start.18 = (bf16[256,1024]{1,0:T(8,128)(2,1)}, bf16[256,1024]{1,0:T(8,128)(2,1)}, u32[]{:S(2)}, u32[]{:S(2)}) collective-permute-start(bf16[256,1024]{1,0:T(8,128)(2,1)} %get-tuple-element.210), channel_id=1, source_target_pairs={{0,2},{1,3},{2,0},{3,1},{4,6},{5,7},{6,4},{7,5},{8,10},{9,11},{10,... | collective-permute-start | bytes 1572872 | tf_op jit(solution)/shard_map/ppermute | solution.py:406
  235.8 25.5 %collective-permute-start.23 = (bf16[256,1024]{1,0:T(8,128)(2,1)S(1)}, bf16[256,1024]{1,0:T(8,128)(2,1)S(1)}, u32[]{:S(2)}, u32[]{:S(2)}) collective-permute-start(bf16[256,1024]{1,0:T(8,128)(2,1)S(1)} %copy-done.34), channel_id=1, source_target_pairs={{0,2},{1,3},{2,0},{3,1},{4,6},{5,7},{6,4},{7,5},{8,10},{9,11},{10,... | collective-permute-start | bytes 1572872 | tf_op jit(solution)/shard_map/ppermute | solution.py:406
  236.7 24.6 %collective-permute-start.24 = (bf16[256,1024]{1,0:T(8,128)(2,1)}, bf16[256,1024]{1,0:T(8,128)(2,1)S(1)}, u32[]{:S(2)}, u32[]{:S(2)}) collective-permute-start(bf16[256,1024]{1,0:T(8,128)(2,1)} %get-tuple-element.243), channel_id=1, source_target_pairs={{0,2},{1,3},{2,0},{3,1},{4,6},{5,7},{6,4},{7,5},{8,10},{9,11},{10,... | collective-permute-start | bytes 1572872 | tf_op jit(solution)/shard_map/ppermute | solution.py:406
  276.1 32.3 %all-to-all-start.2 = ((bf16[8,128,256]{2,1,0:T(8,128)(2,1)}), bf16[8,128,256]{2,1,0:T(8,128)(2,1)S(1)}, u32[]{:S(2)}, u32[]{:S(2)}) async-start(bf16[8,128,256]{2,1,0:T(8,128)(2,1)} %bitcast.89), calls=%async_computation.2 | async-start | bytes 1048576 | tf_op jit(solution)/shard_map/all_to_all | solution.py:423
  280.1 109.5 %reduce-scatter.5.cloned.1.call-start = ((), (), s32[]{:S(2)}) async-start(), calls=%async_computation.10 | async-start | bytes 1769472 | tf_op jit(solution)/shard_map/reduce_scatter | solution.py:605
  282.2 26.2 %collective-permute-start.28 = (bf16[256,1024]{1,0:T(8,128)(2,1)}, bf16[256,1024]{1,0:T(8,128)(2,1)S(1)}, u32[]{:S(2)}, u32[]{:S(2)}) collective-permute-start(bf16[256,1024]{1,0:T(8,128)(2,1)} %get-tuple-element.259), channel_id=1, source_target_pairs={{0,2},{1,3},{2,0},{3,1},{4,6},{5,7},{6,4},{7,5},{8,10},{9,11},{10,... | collective-permute-start | bytes 1572872 | tf_op jit(solution)/shard_map/ppermute | solution.py:406
  283.1 25.3 %collective-permute-start.27 = (bf16[256,1024]{1,0:T(8,128)(2,1)}, bf16[256,1024]{1,0:T(8,128)(2,1)S(1)}, u32[]{:S(2)}, u32[]{:S(2)}) collective-permute-start(bf16[256,1024]{1,0:T(8,128)(2,1)} %add_convert_fusion.1), channel_id=1, source_target_pairs={{0,2},{1,3},{2,0},{3,1},{4,6},{5,7},{6,4},{7,5},{8,10},{9,11},{10,... | collective-permute-start | bytes 1572872 | tf_op jit(solution)/shard_map/ppermute | solution.py:406
  349.0 18.5 %all-to-all-start.3 = ((bf16[8,2,9984]{2,1,0:T(2,128)(2,1)}), bf16[8,2,9984]{2,1,0:T(2,128)(2,1)S(1)}, u32[]{:S(2)}, u32[]{:S(2)}) async-start(bf16[8,2,9984]{2,1,0:T(2,128)(2,1)} %reshape.111), calls=%async_computation.4 | async-start | bytes 638976 | tf_op jit(solution)/shard_map/all_to_all | solution.py:423
  (75 other events, 542.7 us)
Sparse Core Ops, SparseCore 0:
  10.7 54.7 all-gather.2
  67.6 72.4 all-gather.4
  227.7 92.3 reduce-scatter.2
  323.7 65.8 reduce-scatter.4

commit v3 on v2

--- a/solution.py
+++ b/solution.py
@@ -17,6 +17,7 @@
 NT = (((1,), (1,)), ((), ()))
 TN = (((0,), (0,)), ((), ()))
 SMALL_COST = pl.CostEstimate(flops=1000, bytes_accessed=1000, transcendentals=0)
+HALF_STEPS = 2
 VMEM_BYTES = 56 * 1024 * 1024
 
 
@@ -49,14 +50,14 @@
         out_ref[rows, :] = jnp.concatenate(outs, 0).T.astype(BF16)
         return carry
 
-    lax.fori_loop(0, length // chunk, body, 0)
+    lax.fori_loop(0, length // chunk, body, 0, unroll=True)
 
 
 def attend(qkv):
     length, three = qkv.shape
     width = three // 3
     pairs = width // 128
-    chunk = min(256, length)
+    chunk = min(1024, length)
     spec = lambda part: pl.BlockSpec((length, 128), lambda i: (0, part * pairs + i))
     return pl.pallas_call(
         functools.partial(attend_kernel, chunk),
@@ -109,7 +110,7 @@
         out_ref[rows, columns(0)] = jnp.concatenate(outs, 0).T.astype(BF16)
         return carry
 
-    lax.fori_loop(0, length // chunk, body, 0)
+    lax.fori_loop(0, length // chunk, body, 0, unroll=True)
     n_heads = len(keys)
     out_ref[:, columns(1)] = (
         jnp.concatenate([dk_ref[h] for h in range(n_heads)], 1) * scale
@@ -121,7 +122,7 @@
     length, three = qkv.shape
     width = three // 3
     pairs = width // 128
-    chunk = min(256, length)
+    chunk = min(1024, length)
     spec = lambda part: pl.BlockSpec((length, 128), lambda i: (0, part * pairs + i))
     return pl.pallas_call(
         functools.partial(attend_back_kernel, chunk),
@@ -203,12 +204,9 @@
     add_sums(sums_ref, [g_sa, g_sa * normed])
 
 
-def result_kernel(near, core, chip, mid_ref, g_ref, mod_ref, bias_ref, out_ref, sums_ref):
+def result_kernel(near, core, chip, mid_ref, mod_ref, bias_ref, out_ref):
     branch = total_of(near, core, chip) + bias_ref[...].astype(F32)
-    grad = g_ref[...].astype(F32)
     out_ref[...] = (mid_ref[...] + row(mod_ref, 5) * branch).astype(BF16)
-    g_m = (grad * row(mod_ref, 5)).astype(BF16).astype(F32)
-    add_sums(sums_ref, [grad * branch, g_m])
 
 
 def by_rows(kernel, name, tall, wide, outs, sums):
@@ -234,21 +232,21 @@
 
 def two_parts(tile, width):
     return [
-        pl.BlockSpec((tile, width), lambda i: (jnp.minimum(i, 1), 0)),
-        pl.BlockSpec((tile, width), lambda i: (jnp.maximum(i - 2, 0), 0)),
+        pl.BlockSpec((tile, width), lambda i: (jnp.minimum(i, HALF_STEPS - 1), 0)),
+        pl.BlockSpec((tile, width), lambda i: (jnp.maximum(i - HALF_STEPS, 0), 0)),
     ]
 
 
 def pick(first_ref, second_ref):
-    return jnp.where(pl.program_id(0) < 2, first_ref[...], second_ref[...])
+    return jnp.where(pl.program_id(0) < HALF_STEPS, first_ref[...], second_ref[...])
 
 
 def put(first_ref, second_ref, value):
-    @pl.when(pl.program_id(0) < 2)
+    @pl.when(pl.program_id(0) < HALF_STEPS)
     def _():
         first_ref[...] = value
 
-    @pl.when(pl.program_id(0) >= 2)
+    @pl.when(pl.program_id(0) >= HALF_STEPS)
     def _():
         second_ref[...] = value
 
@@ -262,12 +260,12 @@
 
 def norm_project(pieces, mod, weight, bias):
     count, width = pieces[0].shape
-    tokens, tile = 2 * count, count // 2
+    tokens, tile = 2 * count, count // HALF_STEPS
     outs = bias.shape[1]
     whole = lambda r, c: pl.BlockSpec((r, c), lambda i: (0, 0))
     return pl.pallas_call(
         norm_project_kernel,
-        grid=(4,),
+        grid=(2 * HALF_STEPS,),
         in_specs=two_parts(tile, width) + [whole(*mod.shape), whole(width, outs), whole(1, outs)],
         out_specs=[pl.BlockSpec((tile, c), lambda i: (i, 0)) for c in (width, outs)],
         out_shape=[jax.ShapeDtypeStruct((tokens, c), BF16) for c in (width, outs)],
@@ -285,10 +283,10 @@
 
 def row_sums(parts, rows):
     count, width = parts[0].shape
-    tile = count // 2
+    tile = count // HALF_STEPS
     return pl.pallas_call(
         row_sums_kernel,
-        grid=(4,),
+        grid=(2 * HALF_STEPS,),
         in_specs=two_parts(tile, width) + two_parts(tile, width),
         out_specs=pl.BlockSpec((8, width), lambda i: (0, 0)),
         out_shape=jax.ShapeDtypeStruct((8, width), F32),
@@ -318,7 +316,7 @@
 def weight_grad(*jobs):
     tokens, rows = jobs[0][0][0].shape
     width = jobs[0][1][0].shape[1]
-    tile = min(256, rows)
+    tile = min(512, rows)
     steps = rows // tile
 
     def left_spec(job):
@@ -346,7 +344,7 @@
 
 def mlp_kernel(
     xa_ref, xb_ref, ga_ref, gb_ref, mod_ref, up_ref, down_ref, bias_ref,
-    x_out, g_out, hid_ref, gpre_ref, near_ref, far_ref, gnear_ref, gfar_ref, gbias_ref,
+    x_out, g_out, hid_ref, gpre_ref, near_ref, far_ref, gnear_ref, gfar_ref, gbias_ref, gate_ref,
 ):
     x = pick(xa_ref, xb_ref)
     grad = (pick(ga_ref, gb_ref).astype(F32) * row(mod_ref, 5)).astype(BF16)
@@ -354,27 +352,29 @@
     g_out[...] = grad
     pre = dot(x, up_ref[...]) + bias_ref[...].astype(F32)
     square = pre * pre
-    th = jnp.tanh(GELU_C * pre * (1.0 + GELU_A * square))
-    half = 0.5 * (1.0 + th)
+    th = jnp.tanh(pre * (GELU_C + (GELU_C * GELU_A) * square))
+    half = 0.5 + 0.5 * th
     hidden = (pre * half).astype(BF16)
-    slope = half + (0.5 * GELU_C) * pre * (1.0 - th * th) * (1.0 + 3.0 * GELU_A * square)
+    slope = half + pre * (1.0 - th * th) * (0.5 * GELU_C + (1.5 * GELU_A * GELU_C) * square)
     g_pre = (dot(grad, down_ref[...]) * slope).astype(BF16)
     hid_ref[...] = hidden
     gpre_ref[...] = g_pre
     put(gnear_ref, gfar_ref, dot(g_pre, up_ref[...], NT).astype(BF16))
-    put(near_ref, far_ref, dot(hidden, down_ref[...], NT).astype(BF16))
+    branch = dot(hidden, down_ref[...], NT)
+    put(near_ref, far_ref, branch.astype(BF16))
     add_sums(gbias_ref, [g_pre.astype(F32)])
+    add_sums(gate_ref, [branch * pick(ga_ref, gb_ref).astype(F32)])
 
 
 def mlp(x_pieces, g_pieces, mod, weights, bias):
     count, width = x_pieces[0].shape
-    tokens, tile = 2 * count, count // 2
+    tokens, tile = 2 * count, count // HALF_STEPS
     hidden = bias.shape[1]
     rows = lambda cols: pl.BlockSpec((tile, cols), lambda i: (i, 0))
     whole = lambda r, c: pl.BlockSpec((r, c), lambda i: (0, 0))
     return pl.pallas_call(
         mlp_kernel,
-        grid=(4,),
+        grid=(2 * HALF_STEPS,),
         in_specs=two_parts(tile, width)
         + two_parts(tile, width)
         + [
@@ -386,7 +386,7 @@
         out_specs=[rows(width), rows(width), rows(hidden), rows(hidden)]
         + two_parts(tile, width)
         + two_parts(tile, width)
-        + [whole(8, hidden)],
+        + [whole(8, hidden), whole(8, width)],
         out_shape=[
             jax.ShapeDtypeStruct((tokens, width), BF16),
             jax.ShapeDtypeStruct((tokens, width), BF16),
@@ -394,13 +394,39 @@
             jax.ShapeDtypeStruct((tokens, hidden), BF16),
         ]
         + [jax.ShapeDtypeStruct((count, width), BF16)] * 4
-        + [jax.ShapeDtypeStruct((8, hidden), F32)],
+        + [jax.ShapeDtypeStruct((8, hidden), F32), jax.ShapeDtypeStruct((8, width), F32)],
         compiler_params=params("arbitrary"),
         cost_estimate=SMALL_COST,
         name="feed_forward",
     )(*x_pieces, *g_pieces, mod, weights, weights, bias)
 
 
+def attn_grad_kernel(xa, xb, qa, qb, ga, gb, va, vb, out_ref):
+    wide = qa.shape[1]
+    first = dot(xa[...], qa[...], TN) + dot(xb[...], qb[...], TN)
+    out_ref[:, :wide] = first.astype(BF16)
+    second = dot(ga[...], va[...], TN) + dot(gb[...], vb[...], TN)
+    out_ref[:, wide:] = second.astype(BF16)
+
+
+def attn_grad(*operands):
+    tokens, rows = operands[0].shape
+    wide, narrow = operands[2].shape[1], operands[6].shape[1]
+    tile = min(256, rows)
+    left = pl.BlockSpec((tokens, tile), lambda i: (0, i))
+    right = lambda width: pl.BlockSpec((tokens, width), lambda i: (0, 0))
+    return pl.pallas_call(
+        attn_grad_kernel,
+        grid=(rows // tile,),
+        in_specs=[left, left, right(wide), right(wide), left, left, right(narrow), right(narrow)],
+        out_specs=pl.BlockSpec((tile, wide + narrow), lambda i: (i, 0)),
+        out_shape=jax.ShapeDtypeStruct((rows, wide + narrow), BF16),
+        compiler_params=params("arbitrary"),
+        cost_estimate=SMALL_COST,
+        name="attn_grad",
+    )(*operands)
+
+
 def swap(value, bit):
     n = lax.axis_size("tensor")
     return lax.ppermute(value, "tensor", [(i, i ^ bit) for i in range(n)])
@@ -417,6 +443,20 @@
 def with_core(near, core):
     count = near.shape[0] // 2
     return (near[count:].astype(F32) + core[count:].astype(F32)).astype(BF16)
+
+
+def halve(value, bit):
+    n = lax.axis_size("dp")
+    count, rows, width = value.shape
+    mine = (lax.axis_index("dp") // bit) % 2
+    value = value.reshape(count // 2, 2, rows, width)
+    keep = lax.dynamic_index_in_dim(value, mine, 1, keepdims=False)
+    send = lax.dynamic_index_in_dim(value, 1 - mine, 1, keepdims=False)
+    return keep, lax.ppermute(send, "dp", [(i, i ^ bit) for i in range(n)])
+
+
+def summed(keep, received):
+    return keep.astype(F32) + received.astype(F32)
 
 
 def exchange(value):
@@ -537,6 +577,13 @@
     ff1 = feed(1, after((pair_m1, core_m1), chip0))
     ff1, recv0 = joined(ff1, recv0)
     ff = [ff0, ff1]
+    own_g = [v.astype(F32) for v in grad_y]
+    gate_m = [
+        ff[i][9][:1] + bias_out.astype(F32) * jnp.sum(own_g[i], 0, keepdims=True) for i in both
+    ]
+    g_reduce_own = sum(
+        jnp.sum((own_g[i] * mod[i][5:6]).astype(BF16).astype(F32), 0, keepdims=True) for i in both
+    )
 
     def middle_back(i, pieces):
         return by_rows(
@@ -558,8 +605,7 @@
     x_parts, g_parts = after(([f[0] for f in ff], [f[1] for f in ff]), (ga0, chip1))
     g_ff = weight_grad((x_parts, [f[3] for f in ff]), (g_parts, [f[2] for f in ff]))
     g_ff, recv_ga0, recv1, core_b = joined(g_ff, recv_ga0, recv1, core_b)
-    g_ff_w = lax.psum_scatter(g_ff, "dp", scatter_dimension=0, tiled=True).astype(F32)
-    g_expand_w, g_reduce_w = g_ff_w[:, :hidden_width], g_ff_w[:, hidden_width:]
+    g_ff_w = lax.psum_scatter(g_ff, "dp", scatter_dimension=0, tiled=True)
     pair_ga0 = jnp.concatenate([ga0, recv_ga0])
     core_ga0 = swap(pair_ga0, 1)
     gmid1, ga1, sums_m1 = middle_back(1, (ff1[6], core1, recv1))
@@ -572,40 +618,33 @@
         return by_rows(
             result_kernel,
             "result",
-            list(pieces) + [mid[i], grad_y[i]],
+            list(pieces) + [mid[i]],
             [mod[i], bias_out],
             [BF16],
-            True,
-        )
-
-    chip_b = [with_core(ff[i][4], core_b[i]) for i in both]
-    recv_b0 = swap(after(chip_b[0], ga1), 2)
+            False,
+        )[0]
+
     gatt0 = dot(full_ga0, proj_full).astype(BF16)
-    gqkv0 = attend_back(qkv0, after(gatt0, chip_b), lse0)
-    gqkv0, recv_ga1, recv_b0 = joined(gqkv0, recv_ga1, recv_b0)
+    gqkv0 = attend_back(qkv0, gatt0, lse0)
+    gqkv0, recv_ga1 = joined(gqkv0, recv_ga1)
     pair_ga1 = jnp.concatenate([ga1, recv_ga1])
     core_ga1 = swap(pair_ga1, 1)
     near0, far0 = project(gqkv0, qkv_full)
     near0, far0, core_ga1 = joined(near0, far0, core_ga1)
     core0 = swap(far0, 1)
     full_ga = [full_ga0, jnp.concatenate([pair_ga1, core_ga1])]
-    g_proj = weight_grad((after(full_ga, far0), attended))
-    res0, sums_r0 = finish(0, (ff0[4], core_b[0], after(recv_b0, far0)))
-    g_proj, res0, core0 = joined(g_proj, res0, core0)
+    gatt1 = dot(after(full_ga[1], far0), proj_full).astype(BF16)
+    gatt1, core0 = joined(gatt1, core0)
     chip0 = with_core(near0, core0)
     recv0 = swap(chip0, 2)
-    recv_b1 = swap(after(chip_b[1], chip0), 2)
-    gatt1 = dot(after(full_ga[1], chip0), proj_full).astype(BF16)
-    pieces_p = exchange(g_proj.reshape(n_dp, -1, local_width))
     gqkv1 = attend_back(qkv1, after(gatt1, chip0), lse1)
-    gqkv1, recv0, recv_b1, pieces_p = joined(gqkv1, recv0, recv_b1, pieces_p)
-    g_proj_w = jnp.sum(pieces_p.astype(F32), 0)
+    gqkv1, recv0 = joined(gqkv1, recv0)
     grad_qkv = [gqkv0, gqkv1]
-    g_qkv = weight_grad((shifted_a, grad_qkv))
-    g_qkv_w = lax.psum_scatter(g_qkv, "dp", scatter_dimension=0, tiled=True)
-    near1, far1 = project(after(gqkv1, g_qkv), qkv_full)
+    g_attn = attn_grad(*shifted_a, *grad_qkv, *full_ga, *attended)
+    keep, received = halve(g_attn.reshape(n_dp, mod_rows, -1), 1)
+    near1, far1 = project(after(gqkv1, keep), qkv_full)
     core1 = swap(far1, 1)
-    sums_p1 = row_sums(after((near1, far1), g_ff_w), (pair_x[1], core_x1))
+    sums_p1 = row_sums((near1, far1), (pair_x[1], core_x1))
     sums_p1, core1 = joined(sums_p1, core1)
 
     def last(i, pieces):
@@ -614,16 +653,18 @@
         )
 
     lat0, sums_a0 = last(0, (near0, core0, after(recv0, sums_p1)))
-    res1, sums_r1 = finish(1, (ff1[4], core_b[1], after(recv_b1, sums_p1)))
-    sums_a, sums_r = [sums_a0, sums_p1], [sums_r0, sums_r1]
+    sums_a = [sums_a0, sums_p1]
 
     shared = jnp.concatenate(
-        [jnp.concatenate([sums_a[i][:2], sums_m[i][2:3], sums_m[i][:2], sums_r[i][:1]]) for i in both]
-        + [sum(s[3:4] for s in sums_m), sum(s[1:2] for s in sums_r)]
-    )
-    shared = shared + swap(shared, 1)
+        [jnp.concatenate([sums_a[i][:2], sums_m[i][2:3], sums_m[i][:2], gate_m[i]]) for i in both]
+        + [sum(s[3:4] for s in sums_m), g_reduce_own]
+    )
+    shared, received = joined(shared, received)
+    keep, received = halve(summed(keep, received).astype(BF16), 2)
+    shared = shared + swap(after(shared, keep), 1)
     chip1 = with_core(near1, core1)
     recv1 = swap(after(chip1, shared), 2)
+    recv_b = [swap(after(with_core(ff[i][4], core_b[i]), chip1), 2) for i in both]
     shared = shared + swap(shared, 2)
     local = jnp.concatenate(
         [
@@ -638,9 +679,12 @@
     mine = jnp.concatenate(
         [shared[:n_mod].astype(BF16), high, (local - high.astype(F32)).astype(BF16)]
     )
-    everyone = exchange(jnp.broadcast_to(mine[None], (n_dp,) + mine.shape)).astype(F32)
+    everyone = exchange(jnp.broadcast_to(mine[None], (n_dp,) + mine.shape))
+    everyone, received, g_ff_w = joined(everyone, received, g_ff_w)
+    everyone = everyone.astype(F32)
+    keep, received = halve(summed(keep, received).astype(BF16), 4)
     lat1 = last(1, (near1, core1, recv1))[0]
-    grad_latent, result = [lat0, lat1], [res0, res1]
+    grad_latent = [lat0, lat1]
     g_mod_all = everyone[:, :n_mod].reshape(n_dp * images, 6, model_width)
     biases = jnp.sum(everyone[:, n_mod:].reshape(n_dp, 2, -1), (0, 1))
     sizes = [model_width, model_width, 3 * local_width, hidden_width]
@@ -657,6 +701,8 @@
     )
     g_mod_w = jnp.einsum("gd,gke->dke", cond_cols, own_cols, preferred_element_type=F32)
     act_rows = jnp.einsum("gke,dke->gd", g_mod_low, mod_weight, preferred_element_type=F32)
+    act_rows, keep = joined(act_rows, keep)
+    result = [finish(i, (ff[i][4], core_b[i], after(recv_b[i], act_rows))) for i in both]
     grad_act = (
         exchange(act_rows.reshape(n_dp, images, mod_rows))
         .transpose(1, 0, 2)
@@ -664,8 +710,17 @@
     )
     silu_out, silu_pull = jax.vjp(jax.nn.silu, cond_float)
     grad_cond = silu_pull(grad_act)[0]
-    g_qkv_w = after(g_qkv_w, (grad_cond, grad_latent, g_mod_w)).astype(F32)
-    g_qkv_w = g_qkv_w.reshape(mod_rows, 3, local_width)
+    received, g_ff_w = after((received, g_ff_w), (grad_cond, result, grad_latent))
+    g_attn_w = summed(keep, received)
+    bit = 8
+    while bit < n_dp:
+        g_attn_w = summed(*halve(g_attn_w.astype(BF16), bit))
+        bit *= 2
+    g_attn_w = g_attn_w[0]
+    g_expand_w = g_ff_w[:, :hidden_width].astype(F32)
+    g_reduce_w = g_ff_w[:, hidden_width:].astype(F32)
+    g_qkv_w = g_attn_w[:, : 3 * local_width].reshape(mod_rows, 3, local_width)
+    g_proj_w = g_attn_w[:, 3 * local_width :]
     return (
         jnp.stack(result, 1),
         jnp.stack(grad_latent, 1),

time: 404 us -> 404 us (level)
  Pallas kernels: 180 us -> 152 us
  waiting for transfers between devices: 60.8 us -> 72.3 us
  local copies, waits for them, and re-layouts: 37.3 us -> 46.4 us
  other arithmetic: 28.2 us -> 35.6 us
  starting transfers between devices: 44.3 us -> 51.5 us
  matrix products: 20.6 us -> 14.5 us
    ppermute x0 -> x3, waiting for transfers between devices: none -> 16.1 us  [halve(): return (keep, lax.ppermute(send, 'dp', [(i, i ^ bit) for i in range(n)]))]
    pallas_call x2, Pallas kernels: 30.5 us -> 16.4 us  [attend(): pl.pallas_call(functools.partial(attend_kernel, chunk), grid=(pairs,), in...]
    pallas_call x3 -> x1, Pallas kernels: 28.7 us -> 16.1 us  [weight_grad(): pl.pallas_call(functools.partial(weight_grad_kernel, len(jobs)), grid=(le...]
    pallas_call x2, Pallas kernels: 42.2 us -> 30.4 us  [attend_back(): pl.pallas_call(functools.partial(attend_back_kernel, chunk), grid=(pairs,...]
    pallas_call x5 -> x6, Pallas kernels: 52 us -> 62.9 us  [the longest x2 35 us: mlp(): pl.pallas_call(mlp_kernel, grid=(2 * HALF_STEPS,), in_specs=two_parts(til...]
    ppermute x33, waiting for transfers between devices: 43.3 us -> 52.4 us  [swap(): return lax.ppermute(value, 'tensor', [(i, i ^ bit) for i in range(n)])]
    ppermute x0 -> x3, starting transfers between devices: none -> 8.31 us  [halve(): return (keep, lax.ppermute(send, 'dp', [(i, i ^ bit) for i in range(n)]))]
    reduce_scatter x2 -> x1, waiting for transfers between devices: 6.81 us -> 0.02 us  [per_device(): g_ff_w = lax.psum_scatter(g_ff, 'dp', scatter_dimension=0, tiled=True)]
  transfers between devices with their start and end apart: 41 -> 42, of which waited for: 13 -> 15; matrix products, arithmetic and copies ran while one was open for 18% -> 20% of each run, Pallas kernels for 45% -> 38%
where the time goes in v3:
time: 404 us; the launch traced here: 399 us
  Pallas kernels  152 us (38%)
  waiting for transfers between devices  72.3 us (18%)
  starting transfers between devices  51.5 us (13%)
  local copies, waits for them, and re-layouts  46.4 us (11%)
  other arithmetic  35.6 us (9%)
  between operations  15.1 us (4%)
  matrix products  14.5 us (4%)
  blocking collectives  12.1 us (3%)
    ppermute x33, waiting for transfers between devices, swap(): return lax.ppermute(value, 'tensor', [(i, i ^ bit) for i in range(n)])  52.4 us
    pallas_call x2, Pallas kernels, mlp(): pl.pallas_call(mlp_kernel, grid=(2 * HALF_STEPS,), in_specs=two_parts(til...  35 us
    pallas_call x2, Pallas kernels, attend_back(): pl.pallas_call(functools.partial(attend_back_kernel, chunk), grid=(pairs,...  30.4 us
    pallas_call x8, Pallas kernels, by_rows(): pl.pallas_call(kernel, grid=(count // tile,), in_specs=[tiled] * len(tall...  26.2 us
    ppermute x33, starting transfers between devices, swap(): return lax.ppermute(value, 'tensor', [(i, i ^ bit) for i in range(n)])  23.9 us
    unnamed x138, local copies, waits for them, and re-layouts  21 us
    all_to_all x3, starting transfers between devices, exchange(): return lax.all_to_all(value, 'dp', 0, 0, tiled=True).reshape(value.shape)  19 us
    pallas_call x2, Pallas kernels, attend(): pl.pallas_call(functools.partial(attend_kernel, chunk), grid=(pairs,), in...  16.4 us
  transfers between devices with their start and end apart: 42, of which 15 were waited for; matrix products, arithmetic and copies ran while one was open for 20% of the time, Pallas kernels for 38%

profile of v3, /device:TPU:0, one launch (start us, length us, event | category | flops | bytes accessed | tf_op | source)
XLA Modules:
  0.0 399.5 jit_solution(8105028754349030874)
XLA Ops:
  15.8 12.1 %all_to_all.24 = bf16[8,2,128]{2,1,0:T(2,128)(2,1)S(1)} all-to-all(bf16[8,2,128]{2,1,0:T(2,128)(2,1)S(1)} %fusion.29), channel_id=1, replica_groups=mesh['dp'=8,'tensor'=4] {'dp'}, dimensions={0} | all-to-all | bytes 8192 | tf_op jit(solution)/shard_map/all_to_all | solution.py:463
  30.3 5.6 %all-to-all-start.1 = ((f32[8,2,6,1024]{3,1,2,0:T(2,128)}), f32[8,2,6,1024]{3,1,2,0:T(2,128)S(1)}, u32[]{:S(2)}, u32[]{:S(2)}) async-start(f32[8,2,6,1024]{3,1,2,0:T(2,128)} %copy.83), calls=%async_computation.1 | async-start | bytes 786432 | tf_op jit(solution)/shard_map/all_to_all | solution.py:463
  42.2 9.4 %collective-permute-done.2 = bf16[256,1024]{1,0:T(8,128)(2,1)} collective-permute-done((bf16[256,1024]{1,0:T(8,128)(2,1)S(1)}, bf16[256,1024]{1,0:T(8,128)(2,1)}, u32[]{:S(2)}, u32[]{:S(2)}) %collective-permute-start.2) | collective-permute-done | bytes 524320 | tf_op jit(solution)/shard_map/ppermute | solution.py:432
  65.7 6.3 %norm_project.2 = (bf16[1024,1024]{1,0:T(8,128)(2,1)}, bf16[1024,768]{1,0:T(8,128)(2,1)}) custom-call(bf16[512,1024]{1,0:T(8,128)(2,1)} %pad_maximum_fusion.1.xa_ref, bf16[512,1024]{1,0:T(8,128)(2,1)} %collective-permute-done.1.xb_ref, f32[6,1024]{1,0:T(8,128)} %get-tuple-element.377.mod_ref, bf16[1024,1024]{1,0:T(8,128)(2,1)} %all-gather.3.cloned.1.call-done.w_ref, ...), custom_call_target="tpu_custom_call" | custom-call | flops 1000 | bytes 1000 | tf_op jit(solution)/shard_map/norm_project/pallas_call | solution.py:266
  72.0 8.3 %attend.2 = (bf16[1024,256]{1,0:T(8,128)(2,1)}, f32[2,8,1024]{2,1,0:T(8,128)}) custom-call(bf16[1024,768]{1,0:T(8,128)(2,1)} %get-tuple-element.156.q_ref.k_ref.v_ref, bf16[1024,768]{1,0:T(8,128)(2,1)} %get-tuple-element.156.q_ref.k_ref.v_ref, bf16[1024,768]{1,0:T(8,128)(2,1)} %get-tuple-element.156.q_ref.k_ref.v_ref), custom_call_target="tpu_custom_call" | custom-call | flops 1000 | bytes 1000 | tf_op jit(solution)/shard_map/attend/pallas_call | solution.py:62
  87.9 6.7 %norm_project.3 = (bf16[1024,1024]{1,0:T(8,128)(2,1)}, bf16[1024,768]{1,0:T(8,128)(2,1)}) custom-call(bf16[512,1024]{1,0:T(8,128)(2,1)} %pad_maximum_fusion.2.xa_ref, bf16[512,1024]{1,0:T(8,128)(2,1)} %collective-permute-done.4.xb_ref, f32[6,1024]{1,0:T(8,128)} %get-tuple-element.376.mod_ref, bf16[1024,1024]{1,0:T(8,128)(2,1)} %all-gather.3.cloned.1.call-done.w_ref, ...), custom_call_target="tpu_custom_call" | custom-call | flops 1000 | bytes 1000 | tf_op jit(solution)/shard_map/norm_project/pallas_call | solution.py:266
  97.9 8.1 %attend.3 = (bf16[1024,256]{1,0:T(8,128)(2,1)}, f32[2,8,1024]{2,1,0:T(8,128)}) custom-call(bf16[1024,768]{1,0:T(8,128)(2,1)} %get-tuple-element.167.q_ref.k_ref.v_ref, bf16[1024,768]{1,0:T(8,128)(2,1)} %get-tuple-element.167.q_ref.k_ref.v_ref, bf16[1024,768]{1,0:T(8,128)(2,1)} %get-tuple-element.167.q_ref.k_ref.v_ref), custom_call_target="tpu_custom_call" | custom-call | flops 1000 | bytes 1000 | tf_op jit(solution)/shard_map/attend/pallas_call | solution.py:62
  106.0 4.3 %collective-permute-done.6.chip = bf16[256,1024]{1,0:T(8,128)(2,1)S(1)} collective-permute-done((bf16[256,1024]{1,0:T(8,128)(2,1)}, bf16[256,1024]{1,0:T(8,128)(2,1)S(1)}, u32[]{:S(2)}, u32[]{:S(2)}) %collective-permute-start.6) | collective-permute-done | bytes 524320 | tf_op jit(solution)/shard_map/ppermute | solution.py:432
  119.2 10.5 %collective-permute-done.11 = bf16[256,1024]{1,0:T(8,128)(2,1)S(1)} collective-permute-done((bf16[256,1024]{1,0:T(8,128)(2,1)}, bf16[256,1024]{1,0:T(8,128)(2,1)S(1)}, u32[]{:S(2)}, u32[]{:S(2)}) %collective-permute-start.11) | collective-permute-done | bytes 524320 | tf_op jit(solution)/shard_map/ppermute | solution.py:432
  129.7 10.8 %collective-permute-done.10.chip = bf16[256,1024]{1,0:T(8,128)(2,1)S(1)} collective-permute-done((bf16[256,1024]{1,0:T(8,128)(2,1)S(1)}, bf16[256,1024]{1,0:T(8,128)(2,1)S(1)}, u32[]{:S(2)}, u32[]{:S(2)}) %collective-permute-start.10) | collective-permute-done | bytes 524320 | tf_op jit(solution)/shard_map/ppermute | solution.py:432
  147.3 17.6 %feed_forward.2 = (bf16[1024,1024]{1,0:T(8,128)(2,1)}, bf16[1024,1024]{1,0:T(8,128)(2,1)}, bf16[1024,1024]{1,0:T(8,128)(2,1)}, bf16[1024,1024]{1,0:T(8,128)(2,1)...) custom-call(bf16[512,1024]{1,0:T(8,128)(2,1)} %copy-done.29, ...), custom_call_target="tpu_custom_call" | custom-call | flops 1000 | bytes 1000 | tf_op jit(solution)/shard_map/feed_forward/pallas_call | solution.py:375
  170.1 17.4 %feed_forward.3 = (bf16[1024,1024]{1,0:T(8,128)(2,1)}, bf16[1024,1024]{1,0:T(8,128)(2,1)}, bf16[1024,1024]{1,0:T(8,128)(2,1)}, bf16[1024,1024]{1,0:T(8,128)(2,1)...) custom-call(bf16[512,1024]{1,0:T(8,128)(2,1)} %copy-done.30, ...), custom_call_target="tpu_custom_call" | custom-call | flops 1000 | bytes 1000 | tf_op jit(solution)/shard_map/feed_forward/pallas_call | solution.py:375
  188.4 4.0 %middle_back.2 = (f32[256,1024]{1,0:T(8,128)}, bf16[256,1024]{1,0:T(8,128)(2,1)}, f32[8,1024]{1,0:T(8,128)}) custom-call(bf16[512,1024]{1,0:T(8,128)(2,1)} %get-tuple-element.194.near, bf16[512,1024]{1,0:T(8,128)(2,1)} %copy-done.28, bf16[256,1024]{1,0:T(8,128)(2,1)} %copy-done.47, f32[256,1024]{1,0:T(8,128)} %get-tuple-element.213.mid_ref, ...), custom_call_target="tpu_custom_call" | custom-call | flops 1000 | bytes 1000 | tf_op jit(solution)/shard_map/middle_back/pallas_call | solution.py:221
  196.0 16.1 %weight_grad.1 = bf16[1024,2048]{1,0:T(8,128)(2,1)} custom-call(bf16[1024,1024]{1,0:T(8,128)(2,1)} %get-tuple-element.220.refs_0_, bf16[1024,1024]{1,0:T(8,128)(2,1)} %get-tuple-element.221.refs_1_, bf16[1024,1024]{1,0:T(8,128)(2,1)} %get-tuple-element.222.refs_2_, bf16[1024,1024]{1,0:T(8,128)(2,1)} %get-tuple-element.223.refs_3_, ...), custom_call_target="tpu_custom_call" | custom-call | flops 1000 | bytes 1000 | tf_op jit(solution)/shard_map/weight_grad/pallas_call | solution.py:333
  214.0 5.5 %collective-permute-done.18 = bf16[256,1024]{1,0:T(8,128)(2,1)} collective-permute-done((bf16[256,1024]{1,0:T(8,128)(2,1)}, bf16[256,1024]{1,0:T(8,128)(2,1)}, u32[]{:S(2)}, u32[]{:S(2)}) %collective-permute-start.18) | collective-permute-done | bytes 524320 | tf_op jit(solution)/shard_map/ppermute | solution.py:432
  221.9 3.9 middle_back.3
  230.9 15.2 %attend_back.2.qa = bf16[1024,768]{1,0:T(8,128)(2,1)} custom-call(bf16[1024,768]{1,0:T(8,128)(2,1)} %get-tuple-element.156.q_ref.k_ref.v_ref, bf16[1024,768]{1,0:T(8,128)(2,1)} %get-tuple-element.156.q_ref.k_ref.v_ref, bf16[1024,768]{1,0:T(8,128)(2,1)} %get-tuple-element.156.q_ref.k_ref.v_ref, bf16[1024,256]{1,0:T(8,128)(2,1)} %convolution_convert_fusion.9.g_ref, ...), custom_call_target="tpu_custom_call" | custom-call | flops 1000 | bytes 1000 | tf_op jit(solution)/shard_map/attend_back/pallas_call | solution.py:127
  256.0 15.1 %attend_back.3.qb = bf16[1024,768]{1,0:T(8,128)(2,1)} custom-call(bf16[1024,768]{1,0:T(8,128)(2,1)} %get-tuple-element.167.q_ref.k_ref.v_ref, bf16[1024,768]{1,0:T(8,128)(2,1)} %get-tuple-element.167.q_ref.k_ref.v_ref, bf16[1024,768]{1,0:T(8,128)(2,1)} %get-tuple-element.167.q_ref.k_ref.v_ref, bf16[1024,256]{1,0:T(8,128)(2,1)} %convolution_convert_fusion.8.g_ref, ...), custom_call_target="tpu_custom_call" | custom-call | flops 1000 | bytes 1000 | tf_op jit(solution)/shard_map/attend_back/pallas_call | solution.py:127
  271.1 9.9 %attn_grad.1 = bf16[1024,1024]{1,0:T(8,128)(2,1)} custom-call(bf16[1024,1024]{1,0:T(8,128)(2,1)} %get-tuple-element.253.xa, bf16[1024,1024]{1,0:T(8,128)(2,1)} %get-tuple-element.254.xb, bf16[1024,768]{1,0:T(8,128)(2,1)} %attend_back.2.qa, bf16[1024,768]{1,0:T(8,128)(2,1)} %attend_back.3.qb, bf16[1024,1024]{1,0:T(8,128)(2,1)} %copy-done.14, ...), custom_call_target="tpu_custom_call" | custom-call | flops 1000 | bytes 1000 | tf_op jit(solution)/shard_map/attn_grad/pallas_call | solution.py:418
  291.5 5.0 %row_sums.1 = f32[8,1024]{1,0:T(8,128)} custom-call(bf16[512,1024]{1,0:T(8,128)(2,1)} %convolution_convert_fusion.1.pa_ref.near, bf16[512,1024]{1,0:T(8,128)(2,1)} %copy-done.44, bf16[512,1024]{1,0:T(8,128)(2,1)} %pad_maximum_fusion.2.xa_ref, bf16[512,1024]{1,0:T(8,128)(2,1)} %collective-permute-done.4.xb_ref), custom_call_target="tpu_custom_call" | custom-call | flops 1000 | bytes 1000 | tf_op jit(solution)/shard_map/row_sums/pallas_call | solution.py:287
  301.2 16.1 %collective-permute-done.29 = bf16[4,128,1024]{2,1,0:T(8,128)(2,1)} collective-permute-done((bf16[4,128,1024]{2,1,0:T(8,128)(2,1)}, bf16[4,128,1024]{2,1,0:T(8,128)(2,1)}, u32[]{:S(2)}, u32[]{:S(2)}) %collective-permute-start.29) | collective-permute-done | bytes 1048608 | tf_op jit(solution)/shard_map/ppermute | solution.py:455
  333.8 7.6 %all-to-all-start.2 = ((bf16[8,2,9984]{2,1,0:T(2,128)(2,1)}), bf16[8,2,9984]{2,1,0:T(2,128)(2,1)S(1)}, u32[]{:S(2)}, u32[]{:S(2)}) async-start(bf16[8,2,9984]{2,1,0:T(2,128)(2,1)} %reshape.128), calls=%async_computation.2 | async-start | bytes 638976 | tf_op jit(solution)/shard_map/all_to_all | solution.py:463
  363.2 6.6 %collective-permute-done.33.chip = bf16[256,1024]{1,0:T(8,128)(2,1)} collective-permute-done((bf16[256,1024]{1,0:T(8,128)(2,1)}, bf16[256,1024]{1,0:T(8,128)(2,1)}, u32[]{:S(2)}, u32[]{:S(2)}) %collective-permute-start.33) | collective-permute-done | bytes 524320 | tf_op jit(solution)/shard_map/ppermute | solution.py:432
  375.0 5.7 %all-to-all-start.3 = ((f32[8,2,128]{2,1,0:T(2,128)}), f32[8,2,128]{2,1,0:T(2,128)S(1)}, u32[]{:S(2)}, u32[]{:S(2)}) async-start(f32[8,2,128]{2,1,0:T(2,128)} %bitcast.30), calls=%async_computation.4 | async-start | bytes 16384 | tf_op jit(solution)/shard_map/all_to_all | solution.py:463
  (320 shorter events, 156.3 us)
Async XLA Ops:
  7.2 58.5 %all-gather.3.cloned.1.call-start = ((), (), s32[]{:S(2)}) async-start(), calls=%async_computation.5 | async-start | bytes 2359296 | tf_op jit(solution)/shard_map/all_gather | solution.py:489
  29.3 24.9 %collective-permute-start.1 = (bf16[512,1024]{1,0:T(8,128)(2,1)}, bf16[512,1024]{1,0:T(8,128)(2,1)}, u32[]{:S(2)}, u32[]{:S(2)}) collective-permute-start(bf16[512,1024]{1,0:T(8,128)(2,1)} %pad_maximum_fusion.1.xa_ref), channel_id=1, source_target_pairs={{0,1},{1,0},{2,3},{3,2},{4,5},{5,4},{6,7},{7,6},{8,9},{9,8},{10,11... | collective-permute-start | bytes 3145736 | tf_op jit(solution)/shard_map/ppermute | solution.py:432
  30.3 23.9 %all-to-all-start.1 = ((f32[8,2,6,1024]{3,1,2,0:T(2,128)}), f32[8,2,6,1024]{3,1,2,0:T(2,128)S(1)}, u32[]{:S(2)}, u32[]{:S(2)}) async-start(f32[8,2,6,1024]{3,1,2,0:T(2,128)} %copy.83), calls=%async_computation.1 | async-start | bytes 786432 | tf_op jit(solution)/shard_map/all_to_all | solution.py:463
  36.0 111.3 %all-gather.5.cloned.1.call-start = ((), (), s32[]{:S(2)}) async-start(), calls=%async_computation.6 | async-start | bytes 4718592 | tf_op jit(solution)/shard_map/all_gather | solution.py:518
  55.8 300.0 %reduce-scatter.2.cloned.1.call-start = ((), (), s32[]{:S(2)}) async-start(), calls=%async_computation.7 | async-start | bytes 4718592 | tf_op jit(solution)/shard_map/reduce_scatter | solution.py:608
  59.4 22.2 %collective-permute-start.3 = (bf16[256,2,1024]{2,0,1:T(8,128)(2,1)}, bf16[256,2,1024]{2,0,1:T(8,128)(2,1)}, u32[]{:S(2)}, u32[]{:S(2)}) collective-permute-start(bf16[256,2,1024]{2,0,1:T(8,128)(2,1)} %copy.89), channel_id=1, source_target_pairs={{0,2},{1,3},{2,0},{3,1},{4,6},{5,7},{6,4},{7,5},{8,10},{9,11},{10,... | collective-permute-start | bytes 3145736 | tf_op jit(solution)/shard_map/ppermute | solution.py:432
  61.0 20.7 %collective-permute-start.4 = (bf16[512,1024]{1,0:T(8,128)(2,1)}, bf16[512,1024]{1,0:T(8,128)(2,1)}, u32[]{:S(2)}, u32[]{:S(2)}) collective-permute-start(bf16[512,1024]{1,0:T(8,128)(2,1)} %pad_maximum_fusion.2.xa_ref), channel_id=1, source_target_pairs={{0,1},{1,0},{2,3},{3,2},{4,5},{5,4},{6,7},{7,6},{8,9},{9,8},{10,11... | collective-permute-start | bytes 3145736 | tf_op jit(solution)/shard_map/ppermute | solution.py:432
  86.4 19.6 %collective-permute-start.7 = (bf16[512,1024]{1,0:T(8,128)(2,1)S(1)}, bf16[512,1024]{1,0:T(8,128)(2,1)}, u32[]{:S(2)}, u32[]{:S(2)}) collective-permute-start(bf16[512,1024]{1,0:T(8,128)(2,1)S(1)} %pad_maximum_fusion.3.ga_ref), channel_id=1, source_target_pairs={{0,1},{1,0},{2,3},{3,2},{4,5},{5,4},{6,7},{7,6},{8,9},{9,8},{10,11... | collective-permute-start | bytes 3145736 | tf_op jit(solution)/shard_map/ppermute | solution.py:432
  87.0 19.0 %collective-permute-start.8 = (bf16[512,1024]{1,0:T(8,128)(2,1)S(1)}, bf16[512,1024]{1,0:T(8,128)(2,1)}, u32[]{:S(2)}, u32[]{:S(2)}) collective-permute-start(bf16[512,1024]{1,0:T(8,128)(2,1)S(1)} %pad_maximum_fusion.4.ga_ref), channel_id=1, source_target_pairs={{0,1},{1,0},{2,3},{3,2},{4,5},{5,4},{6,7},{7,6},{8,9},{9,8},{10,11... | collective-permute-start | bytes 3145736 | tf_op jit(solution)/shard_map/ppermute | solution.py:432
  117.6 22.9 %collective-permute-start.10 = (bf16[256,1024]{1,0:T(8,128)(2,1)S(1)}, bf16[256,1024]{1,0:T(8,128)(2,1)S(1)}, u32[]{:S(2)}, u32[]{:S(2)}) collective-permute-start(bf16[256,1024]{1,0:T(8,128)(2,1)S(1)} %add_convert_fusion.8), channel_id=1, source_target_pairs={{0,2},{1,3},{2,0},{3,1},{4,6},{5,7},{6,4},{7,5},{8,10},{9,11},{10,... | collective-permute-start | bytes 1572872 | tf_op jit(solution)/shard_map/ppermute | solution.py:432
  145.2 19.7 %collective-permute-start.13 = (bf16[256,1024]{1,0:T(8,128)(2,1)}, bf16[256,1024]{1,0:T(8,128)(2,1)}, u32[]{:S(2)}, u32[]{:S(2)}) collective-permute-start(bf16[256,1024]{1,0:T(8,128)(2,1)} %get-tuple-element.176), channel_id=1, source_target_pairs={{0,2},{1,3},{2,0},{3,1},{4,6},{5,7},{6,4},{7,5},{8,10},{9,11},{10,... | collective-permute-start | bytes 1572872 | tf_op jit(solution)/shard_map/ppermute | solution.py:432
  168.0 19.6 %collective-permute-start.16 = (bf16[256,1024]{1,0:T(8,128)(2,1)S(1)}, bf16[256,1024]{1,0:T(8,128)(2,1)S(1)}, u32[]{:S(2)}, u32[]{:S(2)}) collective-permute-start(bf16[256,1024]{1,0:T(8,128)(2,1)S(1)} %add_convert_fusion.7), channel_id=1, source_target_pairs={{0,2},{1,3},{2,0},{3,1},{4,6},{5,7},{6,4},{7,5},{8,10},{9,11},{10,... | collective-permute-start | bytes 1572872 | tf_op jit(solution)/shard_map/ppermute | solution.py:432
  192.4 27.2 %collective-permute-start.20 = (bf16[512,1024]{1,0:T(8,128)(2,1)}, bf16[512,1024]{1,0:T(8,128)(2,1)S(1)}, u32[]{:S(2)}, u32[]{:S(2)}) collective-permute-start(bf16[512,1024]{1,0:T(8,128)(2,1)} %get-tuple-element.229), channel_id=1, source_target_pairs={{0,1},{1,0},{2,3},{3,2},{4,5},{5,4},{6,7},{7,6},{8,9},{9,8},{10,11... | collective-permute-start | bytes 3145736 | tf_op jit(solution)/shard_map/ppermute | solution.py:432
  192.7 26.9 %collective-permute-start.21 = (bf16[512,1024]{1,0:T(8,128)(2,1)}, bf16[512,1024]{1,0:T(8,128)(2,1)}, u32[]{:S(2)}, u32[]{:S(2)}) collective-permute-start(bf16[512,1024]{1,0:T(8,128)(2,1)} %get-tuple-element.231), channel_id=1, source_target_pairs={{0,1},{1,0},{2,3},{3,2},{4,5},{5,4},{6,7},{7,6},{8,9},{9,8},{10,11... | collective-permute-start | bytes 3145736 | tf_op jit(solution)/shard_map/ppermute | solution.py:432
  194.0 20.0 %collective-permute-start.19 = (bf16[256,1024]{1,0:T(8,128)(2,1)}, bf16[256,1024]{1,0:T(8,128)(2,1)S(1)}, u32[]{:S(2)}, u32[]{:S(2)}) collective-permute-start(bf16[256,1024]{1,0:T(8,128)(2,1)} %add_convert_fusion.6), channel_id=1, source_target_pairs={{0,2},{1,3},{2,0},{3,1},{4,6},{5,7},{6,4},{7,5},{8,10},{9,11},{10,... | collective-permute-start | bytes 1572872 | tf_op jit(solution)/shard_map/ppermute | solution.py:432
  195.0 24.6 %collective-permute-start.18 = (bf16[256,1024]{1,0:T(8,128)(2,1)}, bf16[256,1024]{1,0:T(8,128)(2,1)}, u32[]{:S(2)}, u32[]{:S(2)}) collective-permute-start(bf16[256,1024]{1,0:T(8,128)(2,1)} %get-tuple-element.217), channel_id=1, source_target_pairs={{0,2},{1,3},{2,0},{3,1},{4,6},{5,7},{6,4},{7,5},{8,10},{9,11},{10,... | collective-permute-start | bytes 1572872 | tf_op jit(solution)/shard_map/ppermute | solution.py:432
  225.9 20.3 %collective-permute-start.23 = (bf16[256,1024]{1,0:T(8,128)(2,1)}, bf16[256,1024]{1,0:T(8,128)(2,1)S(1)}, u32[]{:S(2)}, u32[]{:S(2)}) collective-permute-start(bf16[256,1024]{1,0:T(8,128)(2,1)} %get-tuple-element.238), channel_id=1, source_target_pairs={{0,2},{1,3},{2,0},{3,1},{4,6},{5,7},{6,4},{7,5},{8,10},{9,11},{10,... | collective-permute-start | bytes 1572872 | tf_op jit(solution)/shard_map/ppermute | solution.py:432
  285.4 31.9 %collective-permute-start.29 = (bf16[4,128,1024]{2,1,0:T(8,128)(2,1)}, bf16[4,128,1024]{2,1,0:T(8,128)(2,1)}, u32[]{:S(2)}, u32[]{:S(2)}) collective-permute-start(bf16[4,128,1024]{2,1,0:T(8,128)(2,1)} %get-tuple-element.360), channel_id=1, source_target_pairs={{0,4},{4,0},{8,12},{12,8},{16,20},{20,16},{24,28},{28,24},{1,5},{5... | collective-permute-start | bytes 3145736 | tf_op jit(solution)/shard_map/ppermute | solution.py:455
  323.6 32.2 %collective-permute-start.32 = (bf16[2,128,1024]{2,1,0:T(8,128)(2,1)}, bf16[2,128,1024]{2,1,0:T(8,128)(2,1)}, u32[]{:S(2)}, u32[]{:S(2)}) collective-permute-start(bf16[2,128,1024]{2,1,0:T(8,128)(2,1)} %get-tuple-element.362), channel_id=1, source_target_pairs={{0,8},{4,12},{8,0},{12,4},{16,24},{20,28},{24,16},{28,20},{1,9},{5... | collective-permute-start | bytes 1572872 | tf_op jit(solution)/shard_map/ppermute | solution.py:455
  326.8 20.9 %collective-permute-start.34 = (bf16[256,1024]{1,0:T(8,128)(2,1)}, bf16[256,1024]{1,0:T(8,128)(2,1)}, u32[]{:S(2)}, u32[]{:S(2)}) collective-permute-start(bf16[256,1024]{1,0:T(8,128)(2,1)} %add_convert_fusion.3), channel_id=1, source_target_pairs={{0,2},{1,3},{2,0},{3,1},{4,6},{5,7},{6,4},{7,5},{8,10},{9,11},{10,... | collective-permute-start | bytes 1572872 | tf_op jit(solution)/shard_map/ppermute | solution.py:432
  333.8 21.7 %all-to-all-start.2 = ((bf16[8,2,9984]{2,1,0:T(2,128)(2,1)}), bf16[8,2,9984]{2,1,0:T(2,128)(2,1)S(1)}, u32[]{:S(2)}, u32[]{:S(2)}) async-start(bf16[8,2,9984]{2,1,0:T(2,128)(2,1)} %reshape.128), calls=%async_computation.2 | async-start | bytes 638976 | tf_op jit(solution)/shard_map/all_to_all | solution.py:463
  345.7 24.1 %collective-permute-start.28 = (bf16[256,1024]{1,0:T(8,128)(2,1)}, bf16[256,1024]{1,0:T(8,128)(2,1)}, u32[]{:S(2)}, u32[]{:S(2)}) collective-permute-start(bf16[256,1024]{1,0:T(8,128)(2,1)} %add_convert_fusion.5), channel_id=1, source_target_pairs={{0,2},{1,3},{2,0},{3,1},{4,6},{5,7},{6,4},{7,5},{8,10},{9,11},{10,... | collective-permute-start | bytes 1572872 | tf_op jit(solution)/shard_map/ppermute | solution.py:432
  346.6 23.3 %collective-permute-start.33 = (bf16[256,1024]{1,0:T(8,128)(2,1)}, bf16[256,1024]{1,0:T(8,128)(2,1)}, u32[]{:S(2)}, u32[]{:S(2)}) collective-permute-start(bf16[256,1024]{1,0:T(8,128)(2,1)} %add_convert_fusion.1), channel_id=1, source_target_pairs={{0,2},{1,3},{2,0},{3,1},{4,6},{5,7},{6,4},{7,5},{8,10},{9,11},{10,... | collective-permute-start | bytes 1572872 | tf_op jit(solution)/shard_map/ppermute | solution.py:432
  358.8 30.0 %collective-permute-start.35 = (bf16[1,128,1024]{2,1,0:T(8,128)(2,1)}, bf16[1,128,1024]{2,1,0:T(8,128)(2,1)}, u32[]{:S(2)}, u32[]{:S(2)}) collective-permute-start(bf16[1,128,1024]{2,1,0:T(8,128)(2,1)} %get-tuple-element.372), channel_id=1, source_target_pairs={{0,16},{4,20},{8,24},{12,28},{16,0},{20,4},{24,8},{28,12},{1,17},{... | collective-permute-start | bytes 786440 | tf_op jit(solution)/shard_map/ppermute | solution.py:455
  (79 other events, 587.9 us)
Sparse Core Ops, SparseCore 0:
  10.7 54.9 all-gather.2
  67.8 72.4 all-gather.4
  222.0 97.2 reduce-scatter.1

commit v4 on v3

--- a/solution.py
+++ b/solution.py
@@ -659,9 +659,7 @@
         [jnp.concatenate([sums_a[i][:2], sums_m[i][2:3], sums_m[i][:2], gate_m[i]]) for i in both]
         + [sum(s[3:4] for s in sums_m), g_reduce_own]
     )
-    shared, received = joined(shared, received)
-    keep, received = halve(summed(keep, received).astype(BF16), 2)
-    shared = shared + swap(after(shared, keep), 1)
+    shared = shared + swap(shared, 1)
     chip1 = with_core(near1, core1)
     recv1 = swap(after(chip1, shared), 2)
     recv_b = [swap(after(with_core(ff[i][4], core_b[i]), chip1), 2) for i in both]
@@ -682,7 +680,7 @@
     everyone = exchange(jnp.broadcast_to(mine[None], (n_dp,) + mine.shape))
     everyone, received, g_ff_w = joined(everyone, received, g_ff_w)
     everyone = everyone.astype(F32)
-    keep, received = halve(summed(keep, received).astype(BF16), 4)
+    keep, received = halve(summed(keep, received).astype(BF16), 2)
     lat1 = last(1, (near1, core1, recv1))[0]
     grad_latent = [lat0, lat1]
     g_mod_all = everyone[:, :n_mod].reshape(n_dp * images, 6, model_width)
@@ -703,6 +701,8 @@
     act_rows = jnp.einsum("gke,dke->gd", g_mod_low, mod_weight, preferred_element_type=F32)
     act_rows, keep = joined(act_rows, keep)
     result = [finish(i, (ff[i][4], core_b[i], after(recv_b[i], act_rows))) for i in both]
+    act_rows, received, result = joined(act_rows, received, result)
+    keep, received = halve(summed(keep, received).astype(BF16), 4)
     grad_act = (
         exchange(act_rows.reshape(n_dp, images, mod_rows))
         .transpose(1, 0, 2)

time: 404 us -> 391 us (0.968)
  waiting for transfers between devices: 72.3 us -> 57.4 us
    ppermute x3, waiting for transfers between devices: 16.1 us -> 6.02 us  [halve(): return (keep, lax.ppermute(send, 'dp', [(i, i ^ bit) for i in range(n)]))]
    ppermute x33, waiting for transfers between devices: 52.4 us -> 46.9 us  [swap(): return lax.ppermute(value, 'tensor', [(i, i ^ bit) for i in range(n)])]
    unnamed x138 -> x144, local copies, waits for them, and re-layouts: 21 us -> 23.5 us
  transfers between devices with their start and end apart: 42 -> 42, of which waited for: 15 -> 16; matrix products, arithmetic and copies ran while one was open for 20% -> 22% of each run, Pallas kernels for 38% -> 39%
where the time goes in v4:
time: 391 us; the launch traced here: 386 us
  Pallas kernels  152 us (39%)
  waiting for transfers between devices  57.4 us (15%)
  starting transfers between devices  52.2 us (13%)
  local copies, waits for them, and re-layouts  47.5 us (12%)
  other arithmetic  35.2 us (9%)
  between operations  15.1 us (4%)
  matrix products  14.5 us (4%)
  blocking collectives  12.1 us (3%)
    ppermute x33, waiting for transfers between devices, swap(): return lax.ppermute(value, 'tensor', [(i, i ^ bit) for i in range(n)])  46.9 us
    pallas_call x2, Pallas kernels, mlp(): pl.pallas_call(mlp_kernel, grid=(2 * HALF_STEPS,), in_specs=two_parts(til...  35 us
    pallas_call x2, Pallas kernels, attend_back(): pl.pallas_call(functools.partial(attend_back_kernel, chunk), grid=(pairs,...  30.3 us
    pallas_call x8, Pallas kernels, by_rows(): pl.pallas_call(kernel, grid=(count // tile,), in_specs=[tiled] * len(tall...  26.2 us
    ppermute x33, starting transfers between devices, swap(): return lax.ppermute(value, 'tensor', [(i, i ^ bit) for i in range(n)])  24.9 us
    unnamed x144, local copies, waits for them, and re-layouts  23.5 us
    all_to_all x3, starting transfers between devices, exchange(): return lax.all_to_all(value, 'dp', 0, 0, tiled=True).reshape(value.shape)  19.8 us
    pallas_call x2, Pallas kernels, attend(): pl.pallas_call(functools.partial(attend_kernel, chunk), grid=(pairs,), in...  16.4 us
  transfers between devices with their start and end apart: 42, of which 16 were waited for; matrix products, arithmetic and copies ran while one was open for 22% of the time, Pallas kernels for 39%

profile of v4, /device:TPU:0, one launch (start us, length us, event | category | flops | bytes accessed | tf_op | source)
XLA Modules:
  0.0 386.0 jit_solution(14808261049439983471)
XLA Ops:
  15.8 12.1 %all_to_all.24 = bf16[8,2,128]{2,1,0:T(2,128)(2,1)S(1)} all-to-all(bf16[8,2,128]{2,1,0:T(2,128)(2,1)S(1)} %fusion.29), channel_id=1, replica_groups=mesh['dp'=8,'tensor'=4] {'dp'}, dimensions={0} | all-to-all | bytes 8192 | tf_op jit(solution)/shard_map/all_to_all | solution.py:463
  30.3 5.6 %all-to-all-start.1 = ((f32[8,2,6,1024]{3,1,2,0:T(2,128)}), f32[8,2,6,1024]{3,1,2,0:T(2,128)S(1)}, u32[]{:S(2)}, u32[]{:S(2)}) async-start(f32[8,2,6,1024]{3,1,2,0:T(2,128)} %copy.83), calls=%async_computation.1 | async-start | bytes 786432 | tf_op jit(solution)/shard_map/all_to_all | solution.py:463
  42.2 9.4 %collective-permute-done.2 = bf16[256,1024]{1,0:T(8,128)(2,1)} collective-permute-done((bf16[256,1024]{1,0:T(8,128)(2,1)S(1)}, bf16[256,1024]{1,0:T(8,128)(2,1)}, u32[]{:S(2)}, u32[]{:S(2)}) %collective-permute-start.2) | collective-permute-done | bytes 524320 | tf_op jit(solution)/shard_map/ppermute | solution.py:432
  65.7 6.3 %norm_project.2 = (bf16[1024,1024]{1,0:T(8,128)(2,1)}, bf16[1024,768]{1,0:T(8,128)(2,1)}) custom-call(bf16[512,1024]{1,0:T(8,128)(2,1)} %pad_maximum_fusion.1.xa_ref, bf16[512,1024]{1,0:T(8,128)(2,1)} %collective-permute-done.1.xb_ref, f32[6,1024]{1,0:T(8,128)} %get-tuple-element.377.mod_ref, bf16[1024,1024]{1,0:T(8,128)(2,1)} %all-gather.3.cloned.1.call-done.w_ref, ...), custom_call_target="tpu_custom_call" | custom-call | flops 1000 | bytes 1000 | tf_op jit(solution)/shard_map/norm_project/pallas_call | solution.py:266
  72.0 8.3 %attend.2 = (bf16[1024,256]{1,0:T(8,128)(2,1)}, f32[2,8,1024]{2,1,0:T(8,128)}) custom-call(bf16[1024,768]{1,0:T(8,128)(2,1)} %get-tuple-element.157.q_ref.k_ref.v_ref, bf16[1024,768]{1,0:T(8,128)(2,1)} %get-tuple-element.157.q_ref.k_ref.v_ref, bf16[1024,768]{1,0:T(8,128)(2,1)} %get-tuple-element.157.q_ref.k_ref.v_ref), custom_call_target="tpu_custom_call" | custom-call | flops 1000 | bytes 1000 | tf_op jit(solution)/shard_map/attend/pallas_call | solution.py:62
  87.9 6.7 %norm_project.3 = (bf16[1024,1024]{1,0:T(8,128)(2,1)}, bf16[1024,768]{1,0:T(8,128)(2,1)}) custom-call(bf16[512,1024]{1,0:T(8,128)(2,1)} %pad_maximum_fusion.2.xa_ref, bf16[512,1024]{1,0:T(8,128)(2,1)} %collective-permute-done.4.xb_ref, f32[6,1024]{1,0:T(8,128)} %get-tuple-element.376.mod_ref, bf16[1024,1024]{1,0:T(8,128)(2,1)} %all-gather.3.cloned.1.call-done.w_ref, ...), custom_call_target="tpu_custom_call" | custom-call | flops 1000 | bytes 1000 | tf_op jit(solution)/shard_map/norm_project/pallas_call | solution.py:266
  97.9 8.1 %attend.3 = (bf16[1024,256]{1,0:T(8,128)(2,1)}, f32[2,8,1024]{2,1,0:T(8,128)}) custom-call(bf16[1024,768]{1,0:T(8,128)(2,1)} %get-tuple-element.168.q_ref.k_ref.v_ref, bf16[1024,768]{1,0:T(8,128)(2,1)} %get-tuple-element.168.q_ref.k_ref.v_ref, bf16[1024,768]{1,0:T(8,128)(2,1)} %get-tuple-element.168.q_ref.k_ref.v_ref), custom_call_target="tpu_custom_call" | custom-call | flops 1000 | bytes 1000 | tf_op jit(solution)/shard_map/attend/pallas_call | solution.py:62
  106.0 4.3 %collective-permute-done.6.chip = bf16[256,1024]{1,0:T(8,128)(2,1)S(1)} collective-permute-done((bf16[256,1024]{1,0:T(8,128)(2,1)}, bf16[256,1024]{1,0:T(8,128)(2,1)S(1)}, u32[]{:S(2)}, u32[]{:S(2)}) %collective-permute-start.6) | collective-permute-done | bytes 524320 | tf_op jit(solution)/shard_map/ppermute | solution.py:432
  119.2 10.5 %collective-permute-done.11 = bf16[256,1024]{1,0:T(8,128)(2,1)S(1)} collective-permute-done((bf16[256,1024]{1,0:T(8,128)(2,1)}, bf16[256,1024]{1,0:T(8,128)(2,1)S(1)}, u32[]{:S(2)}, u32[]{:S(2)}) %collective-permute-start.11) | collective-permute-done | bytes 524320 | tf_op jit(solution)/shard_map/ppermute | solution.py:432
  129.7 10.8 %collective-permute-done.10.chip = bf16[256,1024]{1,0:T(8,128)(2,1)S(1)} collective-permute-done((bf16[256,1024]{1,0:T(8,128)(2,1)S(1)}, bf16[256,1024]{1,0:T(8,128)(2,1)S(1)}, u32[]{:S(2)}, u32[]{:S(2)}) %collective-permute-start.10) | collective-permute-done | bytes 524320 | tf_op jit(solution)/shard_map/ppermute | solution.py:432
  147.3 17.6 %feed_forward.2 = (bf16[1024,1024]{1,0:T(8,128)(2,1)}, bf16[1024,1024]{1,0:T(8,128)(2,1)}, bf16[1024,1024]{1,0:T(8,128)(2,1)}, bf16[1024,1024]{1,0:T(8,128)(2,1)...) custom-call(bf16[512,1024]{1,0:T(8,128)(2,1)} %copy-done.31, ...), custom_call_target="tpu_custom_call" | custom-call | flops 1000 | bytes 1000 | tf_op jit(solution)/shard_map/feed_forward/pallas_call | solution.py:375
  170.1 17.5 %feed_forward.3 = (bf16[1024,1024]{1,0:T(8,128)(2,1)}, bf16[1024,1024]{1,0:T(8,128)(2,1)}, bf16[1024,1024]{1,0:T(8,128)(2,1)}, bf16[1024,1024]{1,0:T(8,128)(2,1)...) custom-call(bf16[512,1024]{1,0:T(8,128)(2,1)} %copy-done.32, ...), custom_call_target="tpu_custom_call" | custom-call | flops 1000 | bytes 1000 | tf_op jit(solution)/shard_map/feed_forward/pallas_call | solution.py:375
  188.4 4.0 %middle_back.2 = (f32[256,1024]{1,0:T(8,128)}, bf16[256,1024]{1,0:T(8,128)(2,1)}, f32[8,1024]{1,0:T(8,128)}) custom-call(bf16[512,1024]{1,0:T(8,128)(2,1)} %get-tuple-element.192.near, bf16[512,1024]{1,0:T(8,128)(2,1)} %copy-done.30, bf16[256,1024]{1,0:T(8,128)(2,1)} %copy-done.50, f32[256,1024]{1,0:T(8,128)} %get-tuple-element.209.mid_ref, ...), custom_call_target="tpu_custom_call" | custom-call | flops 1000 | bytes 1000 | tf_op jit(solution)/shard_map/middle_back/pallas_call | solution.py:221
  196.0 16.1 %weight_grad.1 = bf16[1024,2048]{1,0:T(8,128)(2,1)} custom-call(bf16[1024,1024]{1,0:T(8,128)(2,1)} %get-tuple-element.220.refs_0_, bf16[1024,1024]{1,0:T(8,128)(2,1)} %get-tuple-element.221.refs_1_, bf16[1024,1024]{1,0:T(8,128)(2,1)} %get-tuple-element.222.refs_2_, bf16[1024,1024]{1,0:T(8,128)(2,1)} %get-tuple-element.223.refs_3_, ...), custom_call_target="tpu_custom_call" | custom-call | flops 1000 | bytes 1000 | tf_op jit(solution)/shard_map/weight_grad/pallas_call | solution.py:333
  212.2 7.4 %collective-permute-done.18 = bf16[256,1024]{1,0:T(8,128)(2,1)} collective-permute-done((bf16[256,1024]{1,0:T(8,128)(2,1)}, bf16[256,1024]{1,0:T(8,128)(2,1)}, u32[]{:S(2)}, u32[]{:S(2)}) %collective-permute-start.18) | collective-permute-done | bytes 524320 | tf_op jit(solution)/shard_map/ppermute | solution.py:432
  222.3 3.9 %middle_back.3 = (f32[256,1024]{1,0:T(8,128)}, bf16[256,1024]{1,0:T(8,128)(2,1)}, f32[8,1024]{1,0:T(8,128)}) custom-call(bf16[512,1024]{1,0:T(8,128)(2,1)} %get-tuple-element.218.near, bf16[512,1024]{1,0:T(8,128)(2,1)} %copy-done.28, bf16[256,1024]{1,0:T(8,128)(2,1)} %copy-done.49, f32[256,1024]{1,0:T(8,128)} %get-tuple-element.234.mid_ref, ...), custom_call_target="tpu_custom_call" | custom-call | flops 1000 | bytes 1000 | tf_op jit(solution)/shard_map/middle_back/pallas_call | solution.py:221
  229.3 15.2 %attend_back.2.qa = bf16[1024,768]{1,0:T(8,128)(2,1)} custom-call(bf16[1024,768]{1,0:T(8,128)(2,1)} %get-tuple-element.157.q_ref.k_ref.v_ref, bf16[1024,768]{1,0:T(8,128)(2,1)} %get-tuple-element.157.q_ref.k_ref.v_ref, bf16[1024,768]{1,0:T(8,128)(2,1)} %get-tuple-element.157.q_ref.k_ref.v_ref, bf16[1024,256]{1,0:T(8,128)(2,1)} %convolution_convert_fusion.9.g_ref, ...), custom_call_target="tpu_custom_call" | custom-call | flops 1000 | bytes 1000 | tf_op jit(solution)/shard_map/attend_back/pallas_call | solution.py:127
  254.2 15.1 %attend_back.3.qb = bf16[1024,768]{1,0:T(8,128)(2,1)} custom-call(bf16[1024,768]{1,0:T(8,128)(2,1)} %get-tuple-element.168.q_ref.k_ref.v_ref, bf16[1024,768]{1,0:T(8,128)(2,1)} %get-tuple-element.168.q_ref.k_ref.v_ref, bf16[1024,768]{1,0:T(8,128)(2,1)} %get-tuple-element.168.q_ref.k_ref.v_ref, bf16[1024,256]{1,0:T(8,128)(2,1)} %convolution_convert_fusion.8.g_ref, ...), custom_call_target="tpu_custom_call" | custom-call | flops 1000 | bytes 1000 | tf_op jit(solution)/shard_map/attend_back/pallas_call | solution.py:127
  269.3 9.9 %attn_grad.1 = bf16[1024,1024]{1,0:T(8,128)(2,1)} custom-call(bf16[1024,1024]{1,0:T(8,128)(2,1)} %get-tuple-element.253.xa, bf16[1024,1024]{1,0:T(8,128)(2,1)} %get-tuple-element.254.xb, bf16[1024,768]{1,0:T(8,128)(2,1)} %attend_back.2.qa, bf16[1024,768]{1,0:T(8,128)(2,1)} %attend_back.3.qb, bf16[1024,1024]{1,0:T(8,128)(2,1)} %copy-done.14, ...), custom_call_target="tpu_custom_call" | custom-call | flops 1000 | bytes 1000 | tf_op jit(solution)/shard_map/attn_grad/pallas_call | solution.py:418
  287.6 5.0 %row_sums.1 = f32[8,1024]{1,0:T(8,128)} custom-call(bf16[512,1024]{1,0:T(8,128)(2,1)} %convolution_convert_fusion.1.pa_ref.near, bf16[512,1024]{1,0:T(8,128)(2,1)} %copy-done.47, bf16[512,1024]{1,0:T(8,128)(2,1)} %pad_maximum_fusion.2.xa_ref, bf16[512,1024]{1,0:T(8,128)(2,1)} %collective-permute-done.4.xb_ref), custom_call_target="tpu_custom_call" | custom-call | flops 1000 | bytes 1000 | tf_op jit(solution)/shard_map/row_sums/pallas_call | solution.py:287
  292.7 3.7 last.2
  310.6 8.4 %all-to-all-start.2 = ((bf16[8,2,9984]{2,1,0:T(2,128)(2,1)}), bf16[8,2,9984]{2,1,0:T(2,128)(2,1)}, u32[]{:S(2)}, u32[]{:S(2)}) async-start(bf16[8,2,9984]{2,1,0:T(2,128)(2,1)} %reshape.130), calls=%async_computation.2 | async-start | bytes 638976 | tf_op jit(solution)/shard_map/all_to_all | solution.py:463
  357.0 5.7 %all-to-all-start.3 = ((f32[8,2,128]{2,1,0:T(2,128)}), f32[8,2,128]{2,1,0:T(2,128)S(1)}, u32[]{:S(2)}, u32[]{:S(2)}) async-start(f32[8,2,128]{2,1,0:T(2,128)} %bitcast.30), calls=%async_computation.4 | async-start | bytes 16384 | tf_op jit(solution)/shard_map/all_to_all | solution.py:463
  370.7 5.6 %collective-permute-done.35 = bf16[1,128,1024]{2,1,0:T(8,128)(2,1)S(1)} collective-permute-done((bf16[1,128,1024]{2,1,0:T(8,128)(2,1)S(1)}, bf16[1,128,1024]{2,1,0:T(8,128)(2,1)S(1)}, u32[]{:S(2)}, u32[]{:S(2)}) %collective-permute-start.35) | collective-permute-done | bytes 262176 | tf_op jit(solution)/shard_map/ppermute | solution.py:455
  (326 shorter events, 153.5 us)
Async XLA Ops:
  7.2 58.5 %all-gather.3.cloned.1.call-start = ((), (), s32[]{:S(2)}) async-start(), calls=%async_computation.5 | async-start | bytes 2359296 | tf_op jit(solution)/shard_map/all_gather | solution.py:489
  12.7 15.5 %collective-permute-start = (bf16[256,1024]{1,0:T(8,128)(2,1)S(1)}, bf16[256,1024]{1,0:T(8,128)(2,1)S(1)}, u32[]{:S(2)}, u32[]{:S(2)}) collective-permute-start(bf16[256,1024]{1,0:T(8,128)(2,1)S(1)} %bitcast.86), channel_id=1, source_target_pairs={{0,2},{1,3},{2,0},{3,1},{4,6},{5,7},{6,4},{7,5},{8,10},{9,11},{10,... | collective-permute-start | bytes 1572872 | tf_op jit(solution)/shard_map/ppermute | solution.py:432
  29.3 24.9 %collective-permute-start.1 = (bf16[512,1024]{1,0:T(8,128)(2,1)}, bf16[512,1024]{1,0:T(8,128)(2,1)}, u32[]{:S(2)}, u32[]{:S(2)}) collective-permute-start(bf16[512,1024]{1,0:T(8,128)(2,1)} %pad_maximum_fusion.1.xa_ref), channel_id=1, source_target_pairs={{0,1},{1,0},{2,3},{3,2},{4,5},{5,4},{6,7},{7,6},{8,9},{9,8},{10,11... | collective-permute-start | bytes 3145736 | tf_op jit(solution)/shard_map/ppermute | solution.py:432
  30.3 23.9 %all-to-all-start.1 = ((f32[8,2,6,1024]{3,1,2,0:T(2,128)}), f32[8,2,6,1024]{3,1,2,0:T(2,128)S(1)}, u32[]{:S(2)}, u32[]{:S(2)}) async-start(f32[8,2,6,1024]{3,1,2,0:T(2,128)} %copy.83), calls=%async_computation.1 | async-start | bytes 786432 | tf_op jit(solution)/shard_map/all_to_all | solution.py:463
  36.0 111.3 %all-gather.5.cloned.1.call-start = ((), (), s32[]{:S(2)}) async-start(), calls=%async_computation.6 | async-start | bytes 4718592 | tf_op jit(solution)/shard_map/all_gather | solution.py:518
  55.8 281.6 %reduce-scatter.2.cloned.1.call-start = ((), (), s32[]{:S(2)}) async-start(), calls=%async_computation.7 | async-start | bytes 4718592 | tf_op jit(solution)/shard_map/reduce_scatter | solution.py:608
  59.4 22.2 %collective-permute-start.3 = (bf16[256,2,1024]{2,0,1:T(8,128)(2,1)}, bf16[256,2,1024]{2,0,1:T(8,128)(2,1)}, u32[]{:S(2)}, u32[]{:S(2)}) collective-permute-start(bf16[256,2,1024]{2,0,1:T(8,128)(2,1)} %copy.89), channel_id=1, source_target_pairs={{0,2},{1,3},{2,0},{3,1},{4,6},{5,7},{6,4},{7,5},{8,10},{9,11},{10,... | collective-permute-start | bytes 3145736 | tf_op jit(solution)/shard_map/ppermute | solution.py:432
  60.9 20.7 %collective-permute-start.4 = (bf16[512,1024]{1,0:T(8,128)(2,1)}, bf16[512,1024]{1,0:T(8,128)(2,1)}, u32[]{:S(2)}, u32[]{:S(2)}) collective-permute-start(bf16[512,1024]{1,0:T(8,128)(2,1)} %pad_maximum_fusion.2.xa_ref), channel_id=1, source_target_pairs={{0,1},{1,0},{2,3},{3,2},{4,5},{5,4},{6,7},{7,6},{8,9},{9,8},{10,11... | collective-permute-start | bytes 3145736 | tf_op jit(solution)/shard_map/ppermute | solution.py:432
  86.4 19.6 %collective-permute-start.7 = (bf16[512,1024]{1,0:T(8,128)(2,1)S(1)}, bf16[512,1024]{1,0:T(8,128)(2,1)}, u32[]{:S(2)}, u32[]{:S(2)}) collective-permute-start(bf16[512,1024]{1,0:T(8,128)(2,1)S(1)} %pad_maximum_fusion.3.ga_ref), channel_id=1, source_target_pairs={{0,1},{1,0},{2,3},{3,2},{4,5},{5,4},{6,7},{7,6},{8,9},{9,8},{10,11... | collective-permute-start | bytes 3145736 | tf_op jit(solution)/shard_map/ppermute | solution.py:432
  87.0 19.0 %collective-permute-start.8 = (bf16[512,1024]{1,0:T(8,128)(2,1)S(1)}, bf16[512,1024]{1,0:T(8,128)(2,1)}, u32[]{:S(2)}, u32[]{:S(2)}) collective-permute-start(bf16[512,1024]{1,0:T(8,128)(2,1)S(1)} %pad_maximum_fusion.4.ga_ref), channel_id=1, source_target_pairs={{0,1},{1,0},{2,3},{3,2},{4,5},{5,4},{6,7},{7,6},{8,9},{9,8},{10,11... | collective-permute-start | bytes 3145736 | tf_op jit(solution)/shard_map/ppermute | solution.py:432
  117.6 22.9 %collective-permute-start.10 = (bf16[256,1024]{1,0:T(8,128)(2,1)S(1)}, bf16[256,1024]{1,0:T(8,128)(2,1)S(1)}, u32[]{:S(2)}, u32[]{:S(2)}) collective-permute-start(bf16[256,1024]{1,0:T(8,128)(2,1)S(1)} %add_convert_fusion.8), channel_id=1, source_target_pairs={{0,2},{1,3},{2,0},{3,1},{4,6},{5,7},{6,4},{7,5},{8,10},{9,11},{10,... | collective-permute-start | bytes 1572872 | tf_op jit(solution)/shard_map/ppermute | solution.py:432
  145.2 19.7 %collective-permute-start.13 = (bf16[256,1024]{1,0:T(8,128)(2,1)}, bf16[256,1024]{1,0:T(8,128)(2,1)}, u32[]{:S(2)}, u32[]{:S(2)}) collective-permute-start(bf16[256,1024]{1,0:T(8,128)(2,1)} %get-tuple-element.177), channel_id=1, source_target_pairs={{0,2},{1,3},{2,0},{3,1},{4,6},{5,7},{6,4},{7,5},{8,10},{9,11},{10,... | collective-permute-start | bytes 1572872 | tf_op jit(solution)/shard_map/ppermute | solution.py:432
  168.0 19.6 %collective-permute-start.16 = (bf16[256,1024]{1,0:T(8,128)(2,1)S(1)}, bf16[256,1024]{1,0:T(8,128)(2,1)S(1)}, u32[]{:S(2)}, u32[]{:S(2)}) collective-permute-start(bf16[256,1024]{1,0:T(8,128)(2,1)S(1)} %add_convert_fusion.7), channel_id=1, source_target_pairs={{0,2},{1,3},{2,0},{3,1},{4,6},{5,7},{6,4},{7,5},{8,10},{9,11},{10,... | collective-permute-start | bytes 1572872 | tf_op jit(solution)/shard_map/ppermute | solution.py:432
  192.5 27.2 %collective-permute-start.20 = (bf16[512,1024]{1,0:T(8,128)(2,1)}, bf16[512,1024]{1,0:T(8,128)(2,1)S(1)}, u32[]{:S(2)}, u32[]{:S(2)}) collective-permute-start(bf16[512,1024]{1,0:T(8,128)(2,1)} %get-tuple-element.229), channel_id=1, source_target_pairs={{0,1},{1,0},{2,3},{3,2},{4,5},{5,4},{6,7},{7,6},{8,9},{9,8},{10,11... | collective-permute-start | bytes 3145736 | tf_op jit(solution)/shard_map/ppermute | solution.py:432
  192.7 26.9 %collective-permute-start.21 = (bf16[512,1024]{1,0:T(8,128)(2,1)}, bf16[512,1024]{1,0:T(8,128)(2,1)}, u32[]{:S(2)}, u32[]{:S(2)}) collective-permute-start(bf16[512,1024]{1,0:T(8,128)(2,1)} %get-tuple-element.231), channel_id=1, source_target_pairs={{0,1},{1,0},{2,3},{3,2},{4,5},{5,4},{6,7},{7,6},{8,9},{9,8},{10,11... | collective-permute-start | bytes 3145736 | tf_op jit(solution)/shard_map/ppermute | solution.py:432
  194.0 18.1 %collective-permute-start.19 = (bf16[256,1024]{1,0:T(8,128)(2,1)}, bf16[256,1024]{1,0:T(8,128)(2,1)S(1)}, u32[]{:S(2)}, u32[]{:S(2)}) collective-permute-start(bf16[256,1024]{1,0:T(8,128)(2,1)} %add_convert_fusion.6), channel_id=1, source_target_pairs={{0,2},{1,3},{2,0},{3,1},{4,6},{5,7},{6,4},{7,5},{8,10},{9,11},{10,... | collective-permute-start | bytes 1572872 | tf_op jit(solution)/shard_map/ppermute | solution.py:432
  195.0 24.6 %collective-permute-start.18 = (bf16[256,1024]{1,0:T(8,128)(2,1)}, bf16[256,1024]{1,0:T(8,128)(2,1)}, u32[]{:S(2)}, u32[]{:S(2)}) collective-permute-start(bf16[256,1024]{1,0:T(8,128)(2,1)} %get-tuple-element.213), channel_id=1, source_target_pairs={{0,2},{1,3},{2,0},{3,1},{4,6},{5,7},{6,4},{7,5},{8,10},{9,11},{10,... | collective-permute-start | bytes 1572872 | tf_op jit(solution)/shard_map/ppermute | solution.py:432
  226.2 18.4 %collective-permute-start.23 = (bf16[256,1024]{1,0:T(8,128)(2,1)}, bf16[256,1024]{1,0:T(8,128)(2,1)S(1)}, u32[]{:S(2)}, u32[]{:S(2)}) collective-permute-start(bf16[256,1024]{1,0:T(8,128)(2,1)} %get-tuple-element.237), channel_id=1, source_target_pairs={{0,2},{1,3},{2,0},{3,1},{4,6},{5,7},{6,4},{7,5},{8,10},{9,11},{10,... | collective-permute-start | bytes 1572872 | tf_op jit(solution)/shard_map/ppermute | solution.py:432
  251.9 17.4 %collective-permute-start.26 = (bf16[256,1024]{1,0:T(8,128)(2,1)S(1)}, bf16[256,1024]{1,0:T(8,128)(2,1)S(1)}, u32[]{:S(2)}, u32[]{:S(2)}) collective-permute-start(bf16[256,1024]{1,0:T(8,128)(2,1)S(1)} %add_convert_fusion.5), channel_id=1, source_target_pairs={{0,2},{1,3},{2,0},{3,1},{4,6},{5,7},{6,4},{7,5},{8,10},{9,11},{10,... | collective-permute-start | bytes 1572872 | tf_op jit(solution)/shard_map/ppermute | solution.py:432
  298.0 39.4 %collective-permute-start.30 = (bf16[4,128,1024]{2,1,0:T(8,128)(2,1)}, bf16[4,128,1024]{2,1,0:T(8,128)(2,1)}, u32[]{:S(2)}, u32[]{:S(2)}) collective-permute-start(bf16[4,128,1024]{2,1,0:T(8,128)(2,1)} %get-tuple-element.362), channel_id=1, source_target_pairs={{0,4},{4,0},{8,12},{12,8},{16,20},{20,16},{24,28},{28,24},{1,5},{5... | collective-permute-start | bytes 3145736 | tf_op jit(solution)/shard_map/ppermute | solution.py:455
  303.5 21.9 %collective-permute-start.34 = (bf16[256,1024]{1,0:T(8,128)(2,1)}, bf16[256,1024]{1,0:T(8,128)(2,1)}, u32[]{:S(2)}, u32[]{:S(2)}) collective-permute-start(bf16[256,1024]{1,0:T(8,128)(2,1)} %add_convert_fusion.3), channel_id=1, source_target_pairs={{0,2},{1,3},{2,0},{3,1},{4,6},{5,7},{6,4},{7,5},{8,10},{9,11},{10,... | collective-permute-start | bytes 1572872 | tf_op jit(solution)/shard_map/ppermute | solution.py:432
  310.6 22.5 %all-to-all-start.2 = ((bf16[8,2,9984]{2,1,0:T(2,128)(2,1)}), bf16[8,2,9984]{2,1,0:T(2,128)(2,1)}, u32[]{:S(2)}, u32[]{:S(2)}) async-start(bf16[8,2,9984]{2,1,0:T(2,128)(2,1)} %reshape.130), calls=%async_computation.2 | async-start | bytes 638976 | tf_op jit(solution)/shard_map/all_to_all | solution.py:463
  323.3 27.6 %collective-permute-start.32 = (bf16[256,1024]{1,0:T(8,128)(2,1)}, bf16[256,1024]{1,0:T(8,128)(2,1)}, u32[]{:S(2)}, u32[]{:S(2)}) collective-permute-start(bf16[256,1024]{1,0:T(8,128)(2,1)} %add_convert_fusion.4), channel_id=1, source_target_pairs={{0,2},{1,3},{2,0},{3,1},{4,6},{5,7},{6,4},{7,5},{8,10},{9,11},{10,... | collective-permute-start | bytes 1572872 | tf_op jit(solution)/shard_map/ppermute | solution.py:432
  324.7 23.6 %collective-permute-start.33 = (bf16[256,1024]{1,0:T(8,128)(2,1)}, bf16[256,1024]{1,0:T(8,128)(2,1)}, u32[]{:S(2)}, u32[]{:S(2)}) collective-permute-start(bf16[256,1024]{1,0:T(8,128)(2,1)} %add_convert_fusion.2), channel_id=1, source_target_pairs={{0,2},{1,3},{2,0},{3,1},{4,6},{5,7},{6,4},{7,5},{8,10},{9,11},{10,... | collective-permute-start | bytes 1572872 | tf_op jit(solution)/shard_map/ppermute | solution.py:432
  (82 other events, 616.9 us)
Sparse Core Ops, SparseCore 0:
  10.7 54.9 all-gather.2
  67.8 72.4 all-gather.4
  219.8 92.2 reduce-scatter.1
